TPU v7x, 128 devices: a whole 4x4x4 slice. The times are simulated.
128 devices in a mesh: ctx: 16 (over z, x_lo, core), head: 8 (over x_hi, y).
Axes of the slice: x: 4 (x_hi: 2, x_lo: 2; x = x_hi * 2 + x_lo), y: 4, z: 4, core: 2. Of those that a mesh axis runs over, the one named last changes fastest.
Arguments:
- block_order: int32 [32], replicated, may hold values from 0 to 31, each once
- question_lengths: int32 [16, 2], P('ctx'), may hold values from 32 to 96, as said below
- document_query_matrix: bfloat16 [2048, 12288], P('ctx', 'head'), may hold values from -6 to 6
- document_key_matrix: bfloat16 [2048, 1024], P('ctx', 'head'), may hold values from -6 to 6
- document_value_matrix: bfloat16 [2048, 1024], P('ctx', 'head'), may hold values from -6 to 6
- document_output: bfloat16 [2048, 12288], P('ctx', 'head'), may hold values from -6 to 6
- document_outgrad: bfloat16 [2048, 12288], P('ctx', 'head'), may hold values from -6 to 6
- document_excess: float32 [2048, 96], P('ctx', 'head'), may hold values from 0.2 to 1
- question_query_matrix: bfloat16 [2048, 12288], P(('ctx', 'head')), may hold values from -6 to 6
- question_key_matrix: bfloat16 [2048, 1024], P(('ctx', 'head')), may hold values from -6 to 6
- question_value_matrix: bfloat16 [2048, 1024], P(('ctx', 'head')), may hold values from -6 to 6
- question_output: bfloat16 [2048, 12288], P(('ctx', 'head')), may hold values from -6 to 6
- question_outgrad: bfloat16 [2048, 12288], P(('ctx', 'head')), may hold values from -6 to 6
- question_excess: float32 [2048, 96], P(('ctx', 'head')), may hold values from 0.2 to 1
Outputs:
- document_query_grad: bfloat16 [2048, 12288], P('ctx', 'head')
- document_keys_grad: bfloat16 [2048, 1024], P('ctx', 'head')
- document_values_grad: bfloat16 [2048, 1024], P('ctx', 'head')
- question_query_grad: bfloat16 [2048, 12288], P(('ctx', 'head'))
- question_keys_grad: bfloat16 [2048, 1024], P(('ctx', 'head'))
- question_values_grad: bfloat16 [2048, 1024], P(('ctx', 'head'))
Inputs may be any that keep to these rules, and one draw needn't show every extreme that they name: `block_order`: a permutation: every block of 64 document positions is stored in exactly one slot; slots 2 c and 2 c + 1 lie on ctx index c. `question_lengths`: each row holds the lengths of the 2 questions of one group in packing order; they sum to 128; some group has a question of exactly 96 tokens.
All inputs are finite; a program needn't handle non-finite values.
Results may differ from a plain program's by a relative error of at most 0.007.
Values may be sent and summed in bfloat16 or wider, within the bound.
No kernel may reach another device: no remote copies, remote signals or barrier semaphores. Data moves between devices by JAX's collectives and lax.ppermute only.
A program may use at most 128 MiB of HBM per device.

v0:
```python
import jax
import jax.numpy as jnp
from jax import lax
from jax.sharding import PartitionSpec as P

HEAD_SIZE = 128


def shifted(block, axis, distance):
    devices = range(lax.axis_size(axis))
    route = [((i - distance) % len(devices), i) for i in devices]
    return lax.ppermute(block, axis, route)


def stored_positions(block_order, first_row, count, half):
    rows = first_row + jnp.arange(count, dtype=jnp.int32)
    blocks = jnp.arange(block_order.shape[0], dtype=jnp.int32)
    picked = (rows // half)[:, None] == blocks[None, :]
    owner = jnp.sum(jnp.where(picked, block_order[None, :], 0), axis=1)
    return owner * half + rows % half


def question_layout(lengths, count):
    ends = jnp.cumsum(lengths)
    starts = ends - lengths
    rows = jnp.arange(count, dtype=jnp.int32)
    segment = jnp.sum((rows[:, None] >= ends[None, :]).astype(jnp.int32), axis=1)
    member = segment[:, None] == jnp.arange(lengths.shape[0], dtype=jnp.int32)[None, :]
    within = rows - jnp.sum(jnp.where(member, starts[None, :], 0), axis=1)
    return (segment, within)


def delta_per_head(output, outgrad, heads):
    product = output.astype(jnp.float32) * outgrad.astype(jnp.float32)
    return jnp.sum(product.reshape(output.shape[0], heads, -1), axis=2)


def arrange_rows(values, kv_heads):
    return values.reshape(values.shape[0], kv_heads, -1).transpose(1, 2, 0)


def attend_block(query, outgrad, lse, delta, keys, values, mask):
    scale = query.shape[-1] ** (-0.5)
    scores = jnp.einsum("rkgd,nkd->kgrn", query, keys, preferred_element_type=jnp.float32) * scale
    prob = jnp.exp(scores - lse[..., None])
    if mask is not None:
        prob = jnp.where(mask[None, None], prob, 0.0)
    prob_b = prob.astype(jnp.bfloat16)
    value_grad = jnp.einsum("kgrn,rkgd->nkd", prob_b, outgrad, preferred_element_type=jnp.float32)
    dprob = jnp.einsum("rkgd,nkd->kgrn", outgrad, values, preferred_element_type=jnp.float32)
    dscore = (prob * (dprob - delta[..., None])).astype(jnp.bfloat16)
    query_grad = (
        jnp.einsum("kgrn,nkd->rkgd", dscore, keys, preferred_element_type=jnp.float32) * scale
    )
    key_grad = (
        jnp.einsum("kgrn,rkgd->nkd", dscore, query, preferred_element_type=jnp.float32) * scale
    )
    return (query_grad, key_grad, value_grad)


def local(
    block_order,
    question_lengths,
    document_query_matrix,
    document_key_matrix,
    document_value_matrix,
    document_output,
    document_outgrad,
    document_excess,
    question_query_matrix,
    question_key_matrix,
    question_value_matrix,
    question_output,
    question_outgrad,
    question_excess,
):
    ctx_size = lax.axis_size("ctx")
    place = lax.axis_index("ctx")
    doc_rows = document_query_matrix.shape[0]
    half = doc_rows // 2
    kv_local = document_key_matrix.shape[1] // HEAD_SIZE
    heads_local = document_excess.shape[1]
    total_doc = doc_rows * ctx_size
    asked_rows, asked_key_rows, asked_value_rows, asked_output, asked_gradient = (
        lax.all_to_all(question_query_matrix, "head", split_axis=1, concat_axis=0, tiled=True),
        lax.all_to_all(question_key_matrix, "head", split_axis=1, concat_axis=0, tiled=True),
        lax.all_to_all(question_value_matrix, "head", split_axis=1, concat_axis=0, tiled=True),
        lax.all_to_all(question_output, "head", split_axis=1, concat_axis=0, tiled=True),
        lax.all_to_all(question_outgrad, "head", split_axis=1, concat_axis=0, tiled=True),
    )
    asked_excess_rows = lax.all_to_all(
        question_excess, "head", split_axis=1, concat_axis=0, tiled=True
    )
    asked_delta = delta_per_head(asked_output, asked_gradient, heads_local)
    ques_rows = asked_rows.shape[0]
    segment, within = question_layout(question_lengths[0], ques_rows)
    question_counts = (within + 1 + total_doc).astype(jnp.float32)
    question_logsumexp = arrange_rows(
        asked_excess_rows + jnp.log(question_counts)[:, None], kv_local
    )
    question_delta = arrange_rows(asked_delta, kv_local)
    asked4 = asked_rows.reshape(ques_rows, kv_local, -1, HEAD_SIZE)
    gradient4 = asked_gradient.reshape(ques_rows, kv_local, -1, HEAD_SIZE)
    query_doc = document_query_matrix.reshape(doc_rows, kv_local, -1, HEAD_SIZE)
    grad_doc = document_outgrad.reshape(doc_rows, kv_local, -1, HEAD_SIZE)
    query_pos = stored_positions(block_order, place * doc_rows, doc_rows, half)
    counts_d = (query_pos + 1).astype(jnp.float32)
    lse_d = arrange_rows(document_excess + jnp.log(counts_d)[:, None], kv_local)
    delta_d = arrange_rows(delta_per_head(document_output, document_outgrad, heads_local), kv_local)

    def doc_part(keys3, values3, key_pos):
        mask = key_pos[None, :] <= query_pos[:, None]
        return attend_block(query_doc, grad_doc, lse_d, delta_d, keys3, values3, mask)

    def visit(document_query_gradient, dq_ques, key_piece, value_piece, key_start):
        count = key_piece.shape[0]
        keys3 = key_piece.reshape(count, kv_local, HEAD_SIZE)
        values3 = value_piece.reshape(count, kv_local, HEAD_SIZE)
        key_pos = stored_positions(block_order, key_start, count, half)
        add_q, dk_q, dv_q = attend_block(
            asked4, gradient4, question_logsumexp, question_delta, keys3, values3, None
        )
        add_d, dk_d, dv_d = doc_part(keys3, values3, key_pos)
        return (document_query_gradient + add_d, dq_ques + add_q, dk_q + dk_d, dv_q + dv_d)

    start_doc = jnp.zeros(query_doc.shape, jnp.float32)
    start_ques = jnp.zeros(asked4.shape, jnp.float32)

    def cycle_step(step, carry):
        document_query_gradient, dq_ques, key_piece, value_piece, key_grad, value_grad = carry
        owner = (place - step) % ctx_size
        document_query_gradient, dq_ques, dk_piece, dv_piece = visit(
            document_query_gradient, dq_ques, key_piece, value_piece, owner * doc_rows
        )
        key_piece, value_piece = shifted((key_piece, value_piece), "ctx", 1)
        key_grad, value_grad = shifted((key_grad + dk_piece, value_grad + dv_piece), "ctx", 1)
        return (document_query_gradient, dq_ques, key_piece, value_piece, key_grad, value_grad)

    empty_grad = jnp.zeros((doc_rows, kv_local, HEAD_SIZE), jnp.float32)
    result = lax.fori_loop(
        0,
        ctx_size,
        cycle_step,
        (start_doc, start_ques, document_key_matrix, document_value_matrix, empty_grad, empty_grad),
    )
    document_query_gradient = result[0]
    dq_ques = result[1]
    key_grad = result[4]
    value_grad = result[5]
    self_mask = (segment[:, None] == segment[None, :]) & (within[None, :] <= within[:, None])
    self_keys = asked_key_rows.reshape(ques_rows, kv_local, HEAD_SIZE)
    self_values = asked_value_rows.reshape(ques_rows, kv_local, HEAD_SIZE)
    add_self, key_self, value_self = attend_block(
        asked4, gradient4, question_logsumexp, question_delta, self_keys, self_values, self_mask
    )
    ques_query_grad = (dq_ques + add_self).astype(jnp.bfloat16).reshape(ques_rows, -1)
    ques_key_grad = key_self.astype(jnp.bfloat16).reshape(ques_rows, -1)
    ques_value_grad = value_self.astype(jnp.bfloat16).reshape(ques_rows, -1)
    back_query, back_keys, back_values = (
        lax.all_to_all(ques_query_grad, "head", split_axis=0, concat_axis=1, tiled=True),
        lax.all_to_all(ques_key_grad, "head", split_axis=0, concat_axis=1, tiled=True),
        lax.all_to_all(ques_value_grad, "head", split_axis=0, concat_axis=1, tiled=True),
    )
    return (
        document_query_gradient.astype(jnp.bfloat16).reshape(doc_rows, -1),
        key_grad.astype(jnp.bfloat16).reshape(doc_rows, -1),
        value_grad.astype(jnp.bfloat16).reshape(doc_rows, -1),
        back_query,
        back_keys,
        back_values,
    )


def solution(mesh):
    return jax.shard_map(
        local,
        mesh=mesh,
        in_specs=(
            P(),
            P("ctx", None),
            P("ctx", "head"),
            P("ctx", "head"),
            P("ctx", "head"),
            P("ctx", "head"),
            P("ctx", "head"),
            P("ctx", "head"),
            P(("ctx", "head"), None),
            P(("ctx", "head"), None),
            P(("ctx", "head"), None),
            P(("ctx", "head"), None),
            P(("ctx", "head"), None),
            P(("ctx", "head"), None),
        ),
        out_specs=(
            P("ctx", "head"),
            P("ctx", "head"),
            P("ctx", "head"),
            P(("ctx", "head"), None),
            P(("ctx", "head"), None),
            P(("ctx", "head"), None),
        ),
        check_vma=False,
    )
```

profile of v0, /device:TPU:0, one launch (start us, length us, event | category | flops | bytes accessed | tf_op | source)
XLA Modules:
  0.0 307.0 jit_solution(2090724213373455023)
XLA Ops:
  3.5 7.0 %all-to-all-start.1 = ((f32[8,1,192]{2,1,0:T(1,128)}), f32[8,1,192]{2,1,0:T(1,128)S(1)}, u32[]{:S(2)}, u32[]{:S(2)}) async-start(f32[8,1,192]{2,1,0:T(1,128)} %reshape.631), calls=%async_computation.1 | async-start | bytes 16384 | tf_op jit(solution)/shard_map/all_to_all | solution.py:91
  19.6 7.2 %all-to-all-start = ((bf16[16,8,1536]{2,0,1:T(8,128)(2,1)}), bf16[16,8,1536]{2,0,1:T(8,128)(2,1)S(1)}, u32[]{:S(2)}, u32[]{:S(2)}) async-start(bf16[16,8,1536]{2,0,1:T(8,128)(2,1)} %bitcast.305), calls=%async_computation | async-start | bytes 786432 | tf_op jit(solution)/shard_map/all_to_all | solution.py:85
  28.0 8.2 %all-to-all-done = bf16[16,8,1536]{2,0,1:T(8,128)(2,1)S(1)} async-done(((bf16[16,8,1536]{2,0,1:T(8,128)(2,1)}), bf16[16,8,1536]{2,0,1:T(8,128)(2,1)S(1)}, u32[]{:S(2)}, u32[]{:S(2)}) %all-to-all-start) | async-done | bytes 393248 | tf_op jit(solution)/shard_map/all_to_all | solution.py:85
  36.2 3.6 %all-to-all-start.3 = ((bf16[16,8,1536]{2,0,1:T(8,128)(2,1)}), bf16[16,8,1536]{2,0,1:T(8,128)(2,1)S(1)}, u32[]{:S(2)}, u32[]{:S(2)}) async-start(bf16[16,8,1536]{2,0,1:T(8,128)(2,1)} %bitcast.303), calls=%async_computation.3 | async-start | bytes 786432 | tf_op jit(solution)/shard_map/all_to_all | solution.py:88
  40.4 8.5 %all-to-all-done.3 = bf16[16,8,1536]{2,0,1:T(8,128)(2,1)S(1)} async-done(((bf16[16,8,1536]{2,0,1:T(8,128)(2,1)}), bf16[16,8,1536]{2,0,1:T(8,128)(2,1)S(1)}, u32[]{:S(2)}, u32[]{:S(2)}) %all-to-all-start.3) | async-done | bytes 393248 | tf_op jit(solution)/shard_map/all_to_all | solution.py:88
  49.7 3.5 %all-to-all-start.2 = ((bf16[16,8,1536]{2,0,1:T(8,128)(2,1)}), bf16[16,8,1536]{2,0,1:T(8,128)(2,1)S(1)}, u32[]{:S(2)}, u32[]{:S(2)}) async-start(bf16[16,8,1536]{2,0,1:T(8,128)(2,1)} %bitcast.304), calls=%async_computation.2 | async-start | bytes 786432 | tf_op jit(solution)/shard_map/all_to_all | solution.py:89
  55.2 7.2 %all-to-all-done.2 = bf16[16,8,1536]{2,0,1:T(8,128)(2,1)S(1)} async-done(((bf16[16,8,1536]{2,0,1:T(8,128)(2,1)}), bf16[16,8,1536]{2,0,1:T(8,128)(2,1)S(1)}, u32[]{:S(2)}, u32[]{:S(2)}) %all-to-all-start.2) | async-done | bytes 393248 | tf_op jit(solution)/shard_map/all_to_all | solution.py:89
  62.4 3.3 %all-to-all-start.4 = ((bf16[16,8,128]{2,0,1:T(8,128)(2,1)}), bf16[16,8,128]{2,0,1:T(8,128)(2,1)S(1)}, u32[]{:S(2)}, u32[]{:S(2)}) async-start(bf16[16,8,128]{2,0,1:T(8,128)(2,1)} %copy_bitcast_fusion.6), calls=%async_computation.4 | async-start | bytes 65536 | tf_op jit(solution)/shard_map/all_to_all | solution.py:86
  68.5 4.9 %all-to-all-done.4 = bf16[16,8,128]{2,0,1:T(8,128)(2,1)S(1)} async-done(((bf16[16,8,128]{2,0,1:T(8,128)(2,1)}), bf16[16,8,128]{2,0,1:T(8,128)(2,1)S(1)}, u32[]{:S(2)}, u32[]{:S(2)}) %all-to-all-start.4) | async-done | bytes 32800 | tf_op jit(solution)/shard_map/all_to_all | solution.py:86
  73.4 4.0 %all-to-all-start.5 = ((bf16[16,8,128]{2,0,1:T(8,128)(2,1)}), bf16[16,8,128]{2,0,1:T(8,128)(2,1)}, u32[]{:S(2)}, u32[]{:S(2)}) async-start(bf16[16,8,128]{2,0,1:T(8,128)(2,1)} %copy_bitcast_fusion.5), calls=%async_computation.5 | async-start | bytes 65536 | tf_op jit(solution)/shard_map/all_to_all | solution.py:87
  85.2 5.2 %all-to-all-start.8 = ((bf16[8,16,128]{2,1,0:T(8,128)(2,1)}), bf16[8,16,128]{2,1,0:T(8,128)(2,1)}, u32[]{:S(2)}, u32[]{:S(2)}) async-start(bf16[8,16,128]{2,1,0:T(8,128)(2,1)} %bitcast.51), calls=%async_computation.8 | async-start | bytes 65536 | tf_op jit(solution)/shard_map/all_to_all | solution.py:162
  93.3 182.7 %while.27 = (s32[]{:T(128)}, f32[128,1,12,128]{3,0,2,1:T(8,128)}, f32[128,1,12,128]{3,0,2,1:T(8,128)S(1)}, bf16[128,128]{1,0:T(8,128)(2,1)S(1)}, bf16[128,128]{1...) while((s32[]{:T(128)}, f32[128,1,12,128]{3,0,2,1:T(8,128)}, ...), condition=%wide.region_8.9_spmd.clone, body=%wide.region_6.8_spmd.clone.sunk | while | flops 507166336 | bytes 15071949 | solution.py:140
  98.7 2.9 collective-permute-start.3
  112.4 2.3 fusion.135
  124.4 2.3 fusion.135
  147.0 2.3 fusion.135
  203.4 2.3 fusion.135
  226.0 2.3 fusion.135
  237.3 2.3 fusion.135
  259.9 2.3 fusion.135
  278.4 7.4 %all-to-all-start.7 = ((bf16[8,16,128]{2,1,0:T(8,128)(2,1)}), bf16[8,16,128]{2,1,0:T(8,128)(2,1)S(1)}, u32[]{:S(2)}, u32[]{:S(2)}) async-start(bf16[8,16,128]{2,1,0:T(8,128)(2,1)} %bitcast.44), calls=%async_computation.7 | async-start | bytes 65536 | tf_op jit(solution)/shard_map/all_to_all | solution.py:161
  288.9 4.7 %all-to-all-done.7 = bf16[8,16,128]{2,1,0:T(8,128)(2,1)S(1)} async-done(((bf16[8,16,128]{2,1,0:T(8,128)(2,1)}), bf16[8,16,128]{2,1,0:T(8,128)(2,1)S(1)}, u32[]{:S(2)}, u32[]{:S(2)}) %all-to-all-start.7) | async-done | bytes 32800 | tf_op jit(solution)/shard_map/all_to_all | solution.py:161
  293.5 3.5 %all-to-all-start.6 = ((bf16[8,16,1536]{2,1,0:T(8,128)(2,1)}), bf16[8,16,1536]{2,1,0:T(8,128)(2,1)S(1)}, u32[]{:S(2)}, u32[]{:S(2)}) async-start(bf16[8,16,1536]{2,1,0:T(8,128)(2,1)} %all_to_all.135), calls=%async_computation.6 | async-start | bytes 786432 | tf_op jit(solution)/shard_map/all_to_all | solution.py:160
  299.0 7.2 %all-to-all-done.6 = bf16[8,16,1536]{2,1,0:T(8,128)(2,1)S(1)} async-done(((bf16[8,16,1536]{2,1,0:T(8,128)(2,1)}), bf16[8,16,1536]{2,1,0:T(8,128)(2,1)S(1)}, u32[]{:S(2)}, u32[]{:S(2)}) %all-to-all-start.6) | async-done | bytes 393248 | tf_op jit(solution)/shard_map/all_to_all | solution.py:160
  (553 shorter events, 199.4 us)
Async XLA Ops:
  3.5 16.1 %all-to-all-start.1 = ((f32[8,1,192]{2,1,0:T(1,128)}), f32[8,1,192]{2,1,0:T(1,128)S(1)}, u32[]{:S(2)}, u32[]{:S(2)}) async-start(f32[8,1,192]{2,1,0:T(1,128)} %reshape.631), calls=%async_computation.1 | async-start | bytes 16384 | tf_op jit(solution)/shard_map/all_to_all | solution.py:91
  19.6 16.6 %all-to-all-start = ((bf16[16,8,1536]{2,0,1:T(8,128)(2,1)}), bf16[16,8,1536]{2,0,1:T(8,128)(2,1)S(1)}, u32[]{:S(2)}, u32[]{:S(2)}) async-start(bf16[16,8,1536]{2,0,1:T(8,128)(2,1)} %bitcast.305), calls=%async_computation | async-start | bytes 786432 | tf_op jit(solution)/shard_map/all_to_all | solution.py:85
  36.2 12.8 %all-to-all-start.3 = ((bf16[16,8,1536]{2,0,1:T(8,128)(2,1)}), bf16[16,8,1536]{2,0,1:T(8,128)(2,1)S(1)}, u32[]{:S(2)}, u32[]{:S(2)}) async-start(bf16[16,8,1536]{2,0,1:T(8,128)(2,1)} %bitcast.303), calls=%async_computation.3 | async-start | bytes 786432 | tf_op jit(solution)/shard_map/all_to_all | solution.py:88
  49.7 12.6 %all-to-all-start.2 = ((bf16[16,8,1536]{2,0,1:T(8,128)(2,1)}), bf16[16,8,1536]{2,0,1:T(8,128)(2,1)S(1)}, u32[]{:S(2)}, u32[]{:S(2)}) async-start(bf16[16,8,1536]{2,0,1:T(8,128)(2,1)} %bitcast.304), calls=%async_computation.2 | async-start | bytes 786432 | tf_op jit(solution)/shard_map/all_to_all | solution.py:89
  62.4 11.0 %all-to-all-start.4 = ((bf16[16,8,128]{2,0,1:T(8,128)(2,1)}), bf16[16,8,128]{2,0,1:T(8,128)(2,1)S(1)}, u32[]{:S(2)}, u32[]{:S(2)}) async-start(bf16[16,8,128]{2,0,1:T(8,128)(2,1)} %copy_bitcast_fusion.6), calls=%async_computation.4 | async-start | bytes 65536 | tf_op jit(solution)/shard_map/all_to_all | solution.py:86
  73.4 11.7 %all-to-all-start.5 = ((bf16[16,8,128]{2,0,1:T(8,128)(2,1)}), bf16[16,8,128]{2,0,1:T(8,128)(2,1)}, u32[]{:S(2)}, u32[]{:S(2)}) async-start(bf16[16,8,128]{2,0,1:T(8,128)(2,1)} %copy_bitcast_fusion.5), calls=%async_computation.5 | async-start | bytes 65536 | tf_op jit(solution)/shard_map/all_to_all | solution.py:87
  85.2 193.2 %all-to-all-start.8 = ((bf16[8,16,128]{2,1,0:T(8,128)(2,1)}), bf16[8,16,128]{2,1,0:T(8,128)(2,1)}, u32[]{:S(2)}, u32[]{:S(2)}) async-start(bf16[8,16,128]{2,1,0:T(8,128)(2,1)} %bitcast.51), calls=%async_computation.8 | async-start | bytes 65536 | tf_op jit(solution)/shard_map/all_to_all | solution.py:162
  94.1 9.1 %collective-permute-start.1 = (bf16[128,128]{1,0:T(8,128)(2,1)S(1)}, bf16[128,128]{1,0:T(8,128)(2,1)}, u32[]{:S(2)}, u32[]{:S(2)}) collective-permute-start(bf16[128,128]{1,0:T(8,128)(2,1)S(1)} %copy.185), channel_id=1, source_target_pairs={{120,0},{0,8},{8,16},{16,24},{24,32},{32,40},{40,48},{48,56},{56,6... | collective-permute-start | bytes 98312 | tf_op jit(solution)/shard_map/while/body/eval_jaxpr/ppermute | solution.py:12
  94.1 9.1 %collective-permute-start = (bf16[128,128]{1,0:T(8,128)(2,1)S(1)}, bf16[128,128]{1,0:T(8,128)(2,1)S(1)}, u32[]{:S(2)}, u32[]{:S(2)}) collective-permute-start(bf16[128,128]{1,0:T(8,128)(2,1)S(1)} %copy.184), channel_id=1, source_target_pairs={{120,0},{0,8},{8,16},{16,24},{24,32},{32,40},{40,48},{48,56},{56,6... | collective-permute-start | bytes 98312 | tf_op jit(solution)/shard_map/while/body/eval_jaxpr/ppermute | solution.py:12
  106.1 9.0 %collective-permute-start.1 = (bf16[128,128]{1,0:T(8,128)(2,1)S(1)}, bf16[128,128]{1,0:T(8,128)(2,1)}, u32[]{:S(2)}, u32[]{:S(2)}) collective-permute-start(bf16[128,128]{1,0:T(8,128)(2,1)S(1)} %copy.185), channel_id=1, source_target_pairs={{120,0},{0,8},{8,16},{16,24},{24,32},{32,40},{40,48},{48,56},{56,6... | collective-permute-start | bytes 98312 | tf_op jit(solution)/shard_map/while/body/eval_jaxpr/ppermute | solution.py:12
  106.1 9.0 %collective-permute-start = (bf16[128,128]{1,0:T(8,128)(2,1)S(1)}, bf16[128,128]{1,0:T(8,128)(2,1)S(1)}, u32[]{:S(2)}, u32[]{:S(2)}) collective-permute-start(bf16[128,128]{1,0:T(8,128)(2,1)S(1)} %copy.184), channel_id=1, source_target_pairs={{120,0},{0,8},{8,16},{16,24},{24,32},{32,40},{40,48},{48,56},{56,6... | collective-permute-start | bytes 98312 | tf_op jit(solution)/shard_map/while/body/eval_jaxpr/ppermute | solution.py:12
  118.1 9.0 %collective-permute-start.1 = (bf16[128,128]{1,0:T(8,128)(2,1)S(1)}, bf16[128,128]{1,0:T(8,128)(2,1)}, u32[]{:S(2)}, u32[]{:S(2)}) collective-permute-start(bf16[128,128]{1,0:T(8,128)(2,1)S(1)} %copy.185), channel_id=1, source_target_pairs={{120,0},{0,8},{8,16},{16,24},{24,32},{32,40},{40,48},{48,56},{56,6... | collective-permute-start | bytes 98312 | tf_op jit(solution)/shard_map/while/body/eval_jaxpr/ppermute | solution.py:12
  118.1 9.0 %collective-permute-start = (bf16[128,128]{1,0:T(8,128)(2,1)S(1)}, bf16[128,128]{1,0:T(8,128)(2,1)S(1)}, u32[]{:S(2)}, u32[]{:S(2)}) collective-permute-start(bf16[128,128]{1,0:T(8,128)(2,1)S(1)} %copy.184), channel_id=1, source_target_pairs={{120,0},{0,8},{8,16},{16,24},{24,32},{32,40},{40,48},{48,56},{56,6... | collective-permute-start | bytes 98312 | tf_op jit(solution)/shard_map/while/body/eval_jaxpr/ppermute | solution.py:12
  129.8 8.7 %collective-permute-start.1 = (bf16[128,128]{1,0:T(8,128)(2,1)S(1)}, bf16[128,128]{1,0:T(8,128)(2,1)}, u32[]{:S(2)}, u32[]{:S(2)}) collective-permute-start(bf16[128,128]{1,0:T(8,128)(2,1)S(1)} %copy.185), channel_id=1, source_target_pairs={{120,0},{0,8},{8,16},{16,24},{24,32},{32,40},{40,48},{48,56},{56,6... | collective-permute-start | bytes 98312 | tf_op jit(solution)/shard_map/while/body/eval_jaxpr/ppermute | solution.py:12
  129.8 8.7 %collective-permute-start = (bf16[128,128]{1,0:T(8,128)(2,1)S(1)}, bf16[128,128]{1,0:T(8,128)(2,1)S(1)}, u32[]{:S(2)}, u32[]{:S(2)}) collective-permute-start(bf16[128,128]{1,0:T(8,128)(2,1)S(1)} %copy.184), channel_id=1, source_target_pairs={{120,0},{0,8},{8,16},{16,24},{24,32},{32,40},{40,48},{48,56},{56,6... | collective-permute-start | bytes 98312 | tf_op jit(solution)/shard_map/while/body/eval_jaxpr/ppermute | solution.py:12
  141.2 8.5 %collective-permute-start.1 = (bf16[128,128]{1,0:T(8,128)(2,1)S(1)}, bf16[128,128]{1,0:T(8,128)(2,1)}, u32[]{:S(2)}, u32[]{:S(2)}) collective-permute-start(bf16[128,128]{1,0:T(8,128)(2,1)S(1)} %copy.185), channel_id=1, source_target_pairs={{120,0},{0,8},{8,16},{16,24},{24,32},{32,40},{40,48},{48,56},{56,6... | collective-permute-start | bytes 98312 | tf_op jit(solution)/shard_map/while/body/eval_jaxpr/ppermute | solution.py:12
  141.2 8.5 %collective-permute-start = (bf16[128,128]{1,0:T(8,128)(2,1)S(1)}, bf16[128,128]{1,0:T(8,128)(2,1)S(1)}, u32[]{:S(2)}, u32[]{:S(2)}) collective-permute-start(bf16[128,128]{1,0:T(8,128)(2,1)S(1)} %copy.184), channel_id=1, source_target_pairs={{120,0},{0,8},{8,16},{16,24},{24,32},{32,40},{40,48},{48,56},{56,6... | collective-permute-start | bytes 98312 | tf_op jit(solution)/shard_map/while/body/eval_jaxpr/ppermute | solution.py:12
  175.1 8.4 %collective-permute-start = (bf16[128,128]{1,0:T(8,128)(2,1)S(1)}, bf16[128,128]{1,0:T(8,128)(2,1)S(1)}, u32[]{:S(2)}, u32[]{:S(2)}) collective-permute-start(bf16[128,128]{1,0:T(8,128)(2,1)S(1)} %copy.184), channel_id=1, source_target_pairs={{120,0},{0,8},{8,16},{16,24},{24,32},{32,40},{40,48},{48,56},{56,6... | collective-permute-start | bytes 98312 | tf_op jit(solution)/shard_map/while/body/eval_jaxpr/ppermute | solution.py:12
  186.4 8.4 %collective-permute-start = (bf16[128,128]{1,0:T(8,128)(2,1)S(1)}, bf16[128,128]{1,0:T(8,128)(2,1)S(1)}, u32[]{:S(2)}, u32[]{:S(2)}) collective-permute-start(bf16[128,128]{1,0:T(8,128)(2,1)S(1)} %copy.184), channel_id=1, source_target_pairs={{120,0},{0,8},{8,16},{16,24},{24,32},{32,40},{40,48},{48,56},{56,6... | collective-permute-start | bytes 98312 | tf_op jit(solution)/shard_map/while/body/eval_jaxpr/ppermute | solution.py:12
  197.7 8.4 %collective-permute-start = (bf16[128,128]{1,0:T(8,128)(2,1)S(1)}, bf16[128,128]{1,0:T(8,128)(2,1)S(1)}, u32[]{:S(2)}, u32[]{:S(2)}) collective-permute-start(bf16[128,128]{1,0:T(8,128)(2,1)S(1)} %copy.184), channel_id=1, source_target_pairs={{120,0},{0,8},{8,16},{16,24},{24,32},{32,40},{40,48},{48,56},{56,6... | collective-permute-start | bytes 98312 | tf_op jit(solution)/shard_map/while/body/eval_jaxpr/ppermute | solution.py:12
  209.0 8.4 %collective-permute-start = (bf16[128,128]{1,0:T(8,128)(2,1)S(1)}, bf16[128,128]{1,0:T(8,128)(2,1)S(1)}, u32[]{:S(2)}, u32[]{:S(2)}) collective-permute-start(bf16[128,128]{1,0:T(8,128)(2,1)S(1)} %copy.184), channel_id=1, source_target_pairs={{120,0},{0,8},{8,16},{16,24},{24,32},{32,40},{40,48},{48,56},{56,6... | collective-permute-start | bytes 98312 | tf_op jit(solution)/shard_map/while/body/eval_jaxpr/ppermute | solution.py:12
  220.3 8.4 %collective-permute-start = (bf16[128,128]{1,0:T(8,128)(2,1)S(1)}, bf16[128,128]{1,0:T(8,128)(2,1)S(1)}, u32[]{:S(2)}, u32[]{:S(2)}) collective-permute-start(bf16[128,128]{1,0:T(8,128)(2,1)S(1)} %copy.184), channel_id=1, source_target_pairs={{120,0},{0,8},{8,16},{16,24},{24,32},{32,40},{40,48},{48,56},{56,6... | collective-permute-start | bytes 98312 | tf_op jit(solution)/shard_map/while/body/eval_jaxpr/ppermute | solution.py:12
  278.4 15.2 %all-to-all-start.7 = ((bf16[8,16,128]{2,1,0:T(8,128)(2,1)}), bf16[8,16,128]{2,1,0:T(8,128)(2,1)S(1)}, u32[]{:S(2)}, u32[]{:S(2)}) async-start(bf16[8,16,128]{2,1,0:T(8,128)(2,1)} %bitcast.44), calls=%async_computation.7 | async-start | bytes 65536 | tf_op jit(solution)/shard_map/all_to_all | solution.py:161
  293.5 12.6 %all-to-all-start.6 = ((bf16[8,16,1536]{2,1,0:T(8,128)(2,1)}), bf16[8,16,1536]{2,1,0:T(8,128)(2,1)S(1)}, u32[]{:S(2)}, u32[]{:S(2)}) async-start(bf16[8,16,1536]{2,1,0:T(8,128)(2,1)} %all_to_all.135), calls=%async_computation.6 | async-start | bytes 786432 | tf_op jit(solution)/shard_map/all_to_all | solution.py:160
  (106 other events, 447.0 us)
where the time goes:
time: 312 us; the launch traced here: 307 us
  matrix products  104 us (33%)
  starting transfers between devices  78 us (25%)
  waiting for transfers between devices  65.9 us (21%)
  local copies, waits for them, and re-layouts  48 us (15%)
  other arithmetic  8.45 us (3%)
    dot_general x33, matrix products, attend_block(): jnp.einsum('kgrn,nkd->rkgd', dscore, keys, preferred_element_type=jnp.flo...  43.1 us
    ppermute x64, starting transfers between devices, shifted(): return lax.ppermute(block, axis, route)  33.3 us
    ppermute x64, waiting for transfers between devices, shifted(): return lax.ppermute(block, axis, route)  23.3 us
    while x96, local copies, waits for them, and re-layouts  22.9 us
    dot_general x33, matrix products, attend_block(): jnp.einsum('rkgd,nkd->kgrn', outgrad, values, preferred_element_type=jnp....  21.8 us
    dot_general x33, matrix products, attend_block(): jnp.einsum('rkgd,nkd->kgrn', query, keys, preferred_element_type=jnp.floa...  20.7 us
    unnamed x62, local copies, waits for them, and re-layouts  12.8 us
    dot_general x33, matrix products, attend_block(): jnp.einsum('kgrn,rkgd->nkd', dscore, query, preferred_element_type=jnp.fl...  9 us
  transfers between devices with their start and end apart: 73, of which 39 were waited for; matrix products, arithmetic and copies ran while one was open for 45% of the time, Pallas kernels for 0%

commit v1 on v0

v1 whole, which is shorter than its diff:
```python
import functools

import jax
import jax.numpy as jnp
from jax import lax
from jax.experimental import pallas as pl
from jax.experimental.pallas import tpu as pltpu
from jax.sharding import PartitionSpec as P

D = 128
SCALE = D**-0.5
LOG2E = 1.4426950408889634
HIDDEN = 1e30
BF = jnp.bfloat16
F32 = jnp.float32
VMEM = pltpu.CompilerParams(vmem_limit_bytes=40 * 2**20)


def dot(a, b, ca, cb):
    return lax.dot_general(a, b, (((ca,), (cb,)), ((), ())), preferred_element_type=F32)


def lanes(shape):
    return lax.broadcasted_iota(jnp.int32, shape, 1)


def sublanes(shape):
    return lax.broadcasted_iota(jnp.int32, shape, 0)


def smem():
    return pl.BlockSpec(memory_space=pltpu.SMEM)


def vmem():
    return pl.BlockSpec(memory_space=pltpu.VMEM)


def call(body, outs, n_smem, *args, **kw):
    return pl.pallas_call(
        body,
        out_shape=tuple(jax.ShapeDtypeStruct(s, t) for s, t in outs),
        in_specs=[smem()] * n_smem + [vmem()] * (len(args) - n_smem),
        out_specs=tuple(vmem() for _ in outs),
        compiler_params=VMEM,
        **kw,
    )(*args)


def pair_block(qs_ref, dos_ref, keys, values, lse, delta, mask):
    scores = dot(keys, qs_ref[...], 1, 1)
    dprob = dot(values, dos_ref[...], 1, 1)
    prob = jnp.exp2(scores * (SCALE * LOG2E) - lse)
    if mask is not None:
        prob = jnp.where(mask, prob, 0.0)
    dscore = (prob * (dprob - delta)).astype(BF)
    dv = dot(prob.astype(BF), dos_ref[...], 1, 0)
    dk = dot(dscore, qs_ref[...], 1, 0) * SCALE
    dq = dot(keys, dscore, 0, 0)
    return dq, dk, dv


def stack_heads(source, target, heads, first):
    for j in range(heads):
        at = first + j * D
        target[j * D : (j + 1) * D, :] = source[:, at : at + D]


def spread_rows(rows, target, heads):
    for j in range(heads):
        target[:, j * D : (j + 1) * D] = rows[j : j + 1, :]


def unstack_query_grad(dq, heads):
    return [(dq[:, j * D : (j + 1) * D].T * SCALE).astype(BF) for j in range(heads)]


def pack_kernel(heads, groups, total, len_ref, me_ref, q_ref, k_ref, v_ref, o_ref, do_ref, ex_ref, dk_ref, dv_ref, pay_ref, kv_ref, buf):
    rows = q_ref.shape[0]
    wide = heads * D
    kv_ref[:, :D] = dk_ref[...]
    kv_ref[:, D:] = dv_ref[...]
    row = me_ref[1] * rows + sublanes((rows, D))
    within = jnp.where(row < len_ref[0, 0], row, row - len_ref[0, 0])
    log_count = jnp.log((within + 1 + total).astype(F32))
    buf[:, : heads * groups] = ex_ref[...]
    lse = (buf[...] + log_count) * LOG2E
    lane = lanes((rows, D))
    for g in range(groups):
        delta = jnp.zeros((rows, D), F32)
        for j in range(heads):
            at = g * wide + j * D
            product = o_ref[:, at : at + D].astype(F32) * do_ref[:, at : at + D].astype(F32)
            delta = jnp.where(lane == j, jnp.sum(product, axis=1, keepdims=True), delta)
        mine = lse if g == 0 else pltpu.roll(lse, D - heads * g, 1)
        mine = jnp.where(lane < heads, mine, 0.0)
        stats = jnp.zeros((rows, D), F32)
        for n, value in enumerate((mine, delta)):
            for m in range(3):
                part = value.astype(BF).astype(F32)
                value = value - part
                at = (3 * n + m) * 16
                stats = stats + (pltpu.roll(part, at, 1) if at else part)
        pay_ref[g, :, :wide] = q_ref[:, g * wide : (g + 1) * wide]
        pay_ref[g, :, wide : 2 * wide] = do_ref[:, g * wide : (g + 1) * wide]
        pay_ref[g, :, 2 * wide : 2 * wide + D] = k_ref[:, g * D : (g + 1) * D]
        pay_ref[g, :, 2 * wide + D : 2 * wide + 2 * D] = v_ref[:, g * D : (g + 1) * D]
        pay_ref[g, :, 2 * wide + 2 * D :] = stats.astype(BF)


def doc_keys(order_ref, me, ctx_size, piece):
    core, z = piece
    place, low, step = me // 4, (me // 2) % 2, ctx_size // 4
    depth = lax.rem(place + step - z, step)
    return [(depth * 2 + (low ^ x if isinstance(low, int) else lax.bitwise_xor(low, x))) * 2 + lax.bitwise_xor(lax.rem(me, 2), core) for x in range(2)]


def doc_lse(order_ref, me, owner, lse, lane_half):
    parts = []
    for b in range(2):
        kb = order_ref[2 * owner + b]
        bias = [jnp.where(kb <= order_ref[2 * me + a], 0.0, HIDDEN).astype(F32) for a in range(2)]
        hide = jnp.where(lane_half, bias[1], bias[0])
        parts.append(jnp.broadcast_to(lse + hide, (D // 2, lse.shape[1])))
    return jnp.concatenate(parts, axis=0)


def doc_kernel(pieces, first, last, heads, ctx_size, order_ref, me_ref, *refs):
    n = len(pieces)
    refs = list(refs)
    kv_refs, refs = refs[:n], refs[n:]
    if first:
        q_ref, o_ref, do_ref, ex_ref = refs[:4]
        refs = refs[4:]
    else:
        qs_ref, dos_ref, lse_ref, delta_ref, dq_in = refs[:5]
        refs = refs[5:]
    if last:
        dq_out, refs = refs[0], refs[1:]
    out_refs, refs = refs[:n], refs[n:]
    if first and not last:
        dq_out, refs = refs[0], refs[1:]
    me = me_ref[0]
    rows = heads * D
    lane = lax.rem(lanes((1, rows)), D)
    half = D // 2
    lane_half = lane >= half
    if first:
        qs_ref, dos_ref, lse_ref, delta_ref = refs
        stack_heads(q_ref, qs_ref, heads, 0)
        stack_heads(do_ref, dos_ref, heads, 0)
        at = lanes((D, D))
        stats = jnp.zeros((D, D), F32)
        for j in range(heads):
            stats = jnp.where(at == j, ex_ref[:, j : j + 1], stats)
            cut = slice(j * D, (j + 1) * D)
            product = o_ref[:, cut].astype(F32) * do_ref[:, cut].astype(F32)
            stats = jnp.where(at == 16 + j, jnp.sum(product, axis=1, keepdims=True), stats)
        stats = stats.T
        one = lanes((1, D))
        pos = jnp.where(one < half, order_ref[2 * me] * half + one, order_ref[2 * me + 1] * half + one - half)
        spread_rows((stats[:16] + jnp.log((pos + 1).astype(F32))) * LOG2E, lse_ref, heads)
        spread_rows(stats[16:32], delta_ref, heads)
    lse = lse_ref[...]
    delta = delta_ref[...]
    total = None if first else dq_in[...]
    for n, piece in enumerate(pieces):
        owners = doc_keys(order_ref, me, ctx_size, piece)
        shift = jnp.concatenate([doc_lse(order_ref, me, o, lse, lane_half) for o in owners], axis=0)
        mask = None
        if piece == (0, 0):
            key = sublanes((2 * D, 1))
            own = key < D
            key_pos = jnp.where(key < half, order_ref[2 * me] * half + key, order_ref[2 * me + 1] * half + key - half)
            row_pos = jnp.where(lane_half, order_ref[2 * me + 1] * half + lane - half, order_ref[2 * me] * half + lane)
            mask = jnp.where(own, key_pos, -1) <= row_pos
        dq, dk, dv = pair_block(qs_ref, dos_ref, kv_refs[n][:, :D], kv_refs[n][:, D:], shift, delta, mask)
        out_refs[n][:, :D] = dk
        out_refs[n][:, D:] = dv
        total = dq if total is None else total + dq
    if last:
        for j, part in enumerate(unstack_query_grad(total, heads)):
            dq_out[:, j * D : (j + 1) * D] = part
    else:
        dq_out[...] = total


def far_kernel(heads, pay_ref, *refs):
    kv_refs, doc_refs = refs[:4], refs[4:8]
    send_ref, dq_ref, qs_ref, dos_ref, lse_ref, delta_ref = refs[8:]
    wide = heads * D
    stack_heads(pay_ref, qs_ref, heads, 0)
    stack_heads(pay_ref, dos_ref, heads, wide)
    stats = pay_ref[:, 2 * wide + 2 * D :].astype(F32).T
    spread_rows(stats[:16] + stats[16:32] + stats[32:48], lse_ref, heads)
    spread_rows(stats[48:64] + stats[64:80] + stats[80:96], delta_ref, heads)
    lse, delta = lse_ref[...], delta_ref[...]
    total = None
    for n in range(4):
        dq, dk, dv = pair_block(qs_ref, dos_ref, kv_refs[n][:, :D], kv_refs[n][:, D:], lse, delta, None)
        send_ref[n, :, :D] = (dk + doc_refs[n][:, :D]).astype(BF)
        send_ref[n, :, D:] = (dv + doc_refs[n][:, D:]).astype(BF)
        total = dq if total is None else total + dq
    dq_ref[...] = total


def near_kernel(heads, qs_ref, dos_ref, lse_ref, delta_ref, dq_in, *refs):
    kv_refs, doc_refs = refs[:4], refs[4:8]
    out_ref, dq_ref = refs[8:]
    lse, delta = lse_ref[...], delta_ref[...]
    total = dq_in[...]
    for pair in range(2):
        keys = jnp.concatenate([kv_refs[2 * pair + m][D:, :D] for m in range(2)], axis=0)
        values = jnp.concatenate([kv_refs[2 * pair + m][D:, D:] for m in range(2)], axis=0)
        dq, dk, dv = pair_block(qs_ref, dos_ref, keys, values, lse, delta, None)
        for m in range(2):
            n = 2 * pair + m
            out_ref[n, :, :D] = dk[m * D : (m + 1) * D] + doc_refs[n][D:, :D]
            out_ref[n, :, D:] = dv[m * D : (m + 1) * D] + doc_refs[n][D:, D:]
        total = total + dq
    dq_ref[...] = total


def own_kernel(heads, groups, len_ref, qs_ref, dos_ref, lse_ref, delta_ref, dq_in, pay_ref, *refs):
    kv_refs, doc_refs = refs[:4], refs[4:8]
    out_ref, back_ref = refs[8:]
    wide = heads * D
    lse, delta = lse_ref[...], delta_ref[...]
    rows = heads * D
    row = lax.rem(lanes((1, rows)), D)
    key = sublanes((D, 1))
    first = len_ref[0, 0]
    mask = (key <= row) & ((key >= first) | (row < first))
    keys = pay_ref[:, 2 * wide : 2 * wide + D]
    values = pay_ref[:, 2 * wide + D : 2 * wide + 2 * D]
    dq, dk, dv = pair_block(qs_ref, dos_ref, keys, values, lse, delta, mask)
    total = dq_in[...] + dq
    each = D // groups
    for g in range(groups):
        back_ref[g, :, wide : wide + D] = dk[g * each : (g + 1) * each].astype(BF)
        back_ref[g, :, wide + D :] = dv[g * each : (g + 1) * each].astype(BF)
    for pair in range(2):
        keys = jnp.concatenate([kv_refs[2 * pair + m][:D, :D] for m in range(2)], axis=0)
        values = jnp.concatenate([kv_refs[2 * pair + m][:D, D:] for m in range(2)], axis=0)
        dq, dk, dv = pair_block(qs_ref, dos_ref, keys, values, lse, delta, None)
        for m in range(2):
            n = 2 * pair + m
            out_ref[n, :, :D] = dk[m * D : (m + 1) * D] + doc_refs[n][:D, :D]
            out_ref[n, :, D:] = dv[m * D : (m + 1) * D] + doc_refs[n][:D, D:]
        total = total + dq
    for j, part in enumerate(unstack_query_grad(total, heads)):
        for g in range(groups):
            back_ref[g, :, j * D : (j + 1) * D] = part[g * each : (g + 1) * each]


def unpack_kernel(heads, groups, back_ref, q_ref, k_ref, v_ref):
    wide = heads * D
    for g in range(groups):
        q_ref[:, g * wide : (g + 1) * wide] = back_ref[g, :, :wide]
        k_ref[:, g * D : (g + 1) * D] = back_ref[g, :, wide : wide + D]
        v_ref[:, g * D : (g + 1) * D] = back_ref[g, :, wide + D :]


def local(
    block_order,
    question_lengths,
    document_query_matrix,
    document_key_matrix,
    document_value_matrix,
    document_output,
    document_outgrad,
    document_excess,
    question_query_matrix,
    question_key_matrix,
    question_value_matrix,
    question_output,
    question_outgrad,
    question_excess,
):
    ctx_size, groups = lax.axis_size("ctx"), lax.axis_size("head")
    heads = document_excess.shape[1]
    rows, each = document_query_matrix.shape[0], question_query_matrix.shape[0]
    total_doc = rows * ctx_size
    wide, stacked = heads * D, heads * rows
    me = jnp.stack([lax.axis_index("ctx"), lax.axis_index("head")]).astype(jnp.int32)
    depth = ctx_size // 4

    def other_core(x):
        return lax.ppermute(x, "ctx", [(i, i ^ 1) for i in range(ctx_size)])

    def other_chip(x):
        return lax.ppermute(x, "ctx", [(i, i ^ 2) for i in range(ctx_size)])

    def along_z(x, d):
        return lax.ppermute(x, "ctx", [(i, (i + 4 * d) % ctx_size) for i in range(ctx_size)])

    payload, kv = call(
        functools.partial(pack_kernel, heads, groups, total_doc),
        [((groups, each, 2 * wide + 3 * D), BF), ((rows, 2 * D), BF)],
        2,
        question_lengths, me, question_query_matrix, question_key_matrix, question_value_matrix, question_output,
        question_outgrad, question_excess, document_key_matrix, document_value_matrix,
        scratch_shapes=[pltpu.VMEM((each, D), F32)],
    )
    asked = lax.all_to_all(payload, "head", 0, 0, tiled=True).reshape(groups * each, -1)
    here = jnp.concatenate([kv, other_chip(kv)], axis=0)
    mine = [here] + [along_z(here, d) for d in range(1, depth)]
    theirs = [other_core(piece) for piece in mine]

    piece_grad = ((2 * rows, 2 * D), F32)
    row_state = [((stacked, D), BF), ((stacked, D), BF), ((1, stacked), F32), ((1, stacked), F32)]
    early = ((0, 0), (1, 0))
    late = tuple((0, d) for d in range(1, depth)) + tuple((1, d) for d in range(1, depth))
    first = call(
        functools.partial(doc_kernel, early, True, False, heads, ctx_size),
        [piece_grad] * 2 + [((D, stacked), F32)] + row_state,
        2,
        block_order, me, mine[0], theirs[0], document_query_matrix, document_output, document_outgrad, document_excess,
    )
    second = call(
        functools.partial(doc_kernel, late, False, True, heads, ctx_size),
        [((rows, wide), BF)] + [piece_grad] * 6,
        2,
        block_order, me, *mine[1:], *theirs[1:], *first[3:], first[2],
    )
    document_query_grad = second[0]
    doc_mine = (first[0],) + tuple(second[1 : depth])
    doc_theirs = (first[1],) + tuple(second[depth:])

    far = call(
        functools.partial(far_kernel, heads),
        [((4, 2 * rows, 2 * D), BF), ((D, stacked), F32)] + row_state,
        0,
        asked, *theirs, *doc_theirs,
    )
    core_sum = other_core(far[0])
    near, dq_near = call(
        functools.partial(near_kernel, heads),
        [((4, rows, 2 * D), F32), ((D, stacked), F32)],
        0,
        *far[2:], far[1], *mine, *doc_mine,
    )
    chip_sum = other_chip((near + core_sum[:, rows:].astype(F32)).astype(BF))
    own, back = call(
        functools.partial(own_kernel, heads, groups),
        [((4, rows, 2 * D), F32), ((groups, each, wide + 2 * D), BF)],
        1,
        question_lengths, *far[2:], dq_near, asked, *mine, *doc_mine,
    )
    back = lax.all_to_all(back, "head", 0, 0, tiled=True)
    held = own + core_sum[:, :rows].astype(F32) + chip_sum.astype(F32)
    grads = held[0]
    for d in range(1, depth):
        grads = grads + along_z(held[d].astype(BF), depth - d).astype(F32)
    grads = grads.astype(BF)
    question_query_grad, question_keys_grad, question_values_grad = call(
        functools.partial(unpack_kernel, heads, groups),
        [((each, wide * groups), BF), ((each, D * groups), BF), ((each, D * groups), BF)],
        0,
        back,
    )
    return (
        document_query_grad,
        grads[:, :D],
        grads[:, D:],
        question_query_grad,
        question_keys_grad,
        question_values_grad,
    )


def solution(mesh):
    return jax.shard_map(
        local,
        mesh=mesh,
        in_specs=(
            P(),
            P("ctx", None),
            P("ctx", "head"),
            P("ctx", "head"),
            P("ctx", "head"),
            P("ctx", "head"),
            P("ctx", "head"),
            P("ctx", "head"),
            P(("ctx", "head"), None),
            P(("ctx", "head"), None),
            P(("ctx", "head"), None),
            P(("ctx", "head"), None),
            P(("ctx", "head"), None),
            P(("ctx", "head"), None),
        ),
        out_specs=(
            P("ctx", "head"),
            P("ctx", "head"),
            P("ctx", "head"),
            P(("ctx", "head"), None),
            P(("ctx", "head"), None),
            P(("ctx", "head"), None),
        ),
        check_vma=False,
    )
```

time: 312 us -> 89.6 us (0.29); the launches traced: 307 us -> 88.8 us
  matrix products: 104 us -> 0 us
  starting transfers between devices: 78 us -> 24.6 us
  waiting for transfers between devices: 65.9 us -> 24.9 us
  local copies, waits for them, and re-layouts: 48 us -> 11.4 us
  Pallas kernels: 0 us -> 25.2 us
  other arithmetic: 8.45 us -> 1.9 us
    dot_general x165 -> x0, matrix products: 104 us -> none  [the longest x33 43.1 us: attend_block(): jnp.einsum('kgrn,nkd->rkgd', dscore, keys, preferred_element_type=jnp.flo...]
    all_to_all x9 -> x2, waiting for transfers between devices: 42.6 us -> 6.59 us  [the longest x1 6.59 us: local(): back = lax.all_to_all(back, 'head', 0, 0, tiled=True)]
    all_to_all x9 -> x2, starting transfers between devices: 44.7 us -> 13.8 us  [the longest x1 7.15 us: local(): lax.all_to_all(payload, 'head', 0, 0, tiled=True).reshape(groups * each, -1)]
    pallas_call x0 -> x7, Pallas kernels: none -> 25.2 us  [call(): pl.pallas_call(body, out_shape=tuple((jax.ShapeDtypeStruct(s, t) for s, t...]
    while x97 -> x0, local copies, waits for them, and re-layouts: 23.1 us -> none
    ppermute x64 -> x13, starting transfers between devices: 33.3 us -> 10.8 us  [the longest x6 8.17 us: along_z(): lax.ppermute(x, 'ctx', [(i, (i + 4 * d) % ctx_size) for i in range(ctx_si...]
    all_to_all x14 -> x0, local copies, waits for them, and re-layouts: 8.99 us -> none  [the longest x2 1.79 us: local(): lax.all_to_all(ques_query_grad, 'head', split_axis=0, concat_axis=1, tile...]
    ppermute x64 -> x13, waiting for transfers between devices: 23.3 us -> 18.3 us  [the longest x2 11.5 us: other_chip(): return lax.ppermute(x, 'ctx', [(i, i ^ 2) for i in range(ctx_size)])]
  transfers between devices with their start and end apart: 73 -> 15, of which waited for: 39 -> 5; matrix products, arithmetic and copies ran while one was open for 45% -> 1% of each run, Pallas kernels for 0% -> 21%
where the time goes in v1:
time: 89.6 us; the launch traced here: 88.8 us
  Pallas kernels  25.2 us (28%)
  waiting for transfers between devices  24.9 us (28%)
  starting transfers between devices  24.6 us (27%)
  local copies, waits for them, and re-layouts  11.4 us (13%)
  other arithmetic  1.9 us (2%)
    pallas_call x7, Pallas kernels, call(): pl.pallas_call(body, out_shape=tuple((jax.ShapeDtypeStruct(s, t) for s, t...  25.2 us
    ppermute x2, waiting for transfers between devices, other_chip(): return lax.ppermute(x, 'ctx', [(i, i ^ 2) for i in range(ctx_size)])  11.5 us
    unnamed x42, local copies, waits for them, and re-layouts  10.8 us
    ppermute x6, starting transfers between devices, along_z(): lax.ppermute(x, 'ctx', [(i, (i + 4 * d) % ctx_size) for i in range(ctx_si...  8.17 us
    all_to_all x1, starting transfers between devices, local(): lax.all_to_all(payload, 'head', 0, 0, tiled=True).reshape(groups * each, -1)  7.15 us
    ppermute x6, waiting for transfers between devices, along_z(): lax.ppermute(x, 'ctx', [(i, (i + 4 * d) % ctx_size) for i in range(ctx_si...  6.84 us
    all_to_all x1, starting transfers between devices, local(): back = lax.all_to_all(back, 'head', 0, 0, tiled=True)  6.61 us
    all_to_all x1, waiting for transfers between devices, local(): back = lax.all_to_all(back, 'head', 0, 0, tiled=True)  6.59 us
  transfers between devices with their start and end apart: 15, of which 5 were waited for; matrix products, arithmetic and copies ran while one was open for 1% of the time, Pallas kernels for 21%

profile of v1, /device:TPU:0, one launch (start us, length us, event | category | flops | bytes accessed | tf_op | source)
XLA Modules:
  0.0 88.8 jit_solution(12370340016852330508)
XLA Ops:
  1.3 1.0 %copy-done = bf16[16,12288]{1,0:T(8,128)(2,1)S(1)} copy-done((bf16[16,12288]{1,0:T(8,128)(2,1)S(1)}, bf16[16,12288]{1,0:T(8,128)(2,1)}, u32[]{:S(2)}) %copy-start) | copy-done | bytes 393240
  2.3 1.0 %copy-done.1 = bf16[16,12288]{1,0:T(8,128)(2,1)S(1)} copy-done((bf16[16,12288]{1,0:T(8,128)(2,1)S(1)}, bf16[16,12288]{1,0:T(8,128)(2,1)}, u32[]{:S(2)}) %copy-start.1) | copy-done | bytes 393240
  3.3 1.0 %copy-done.2 = bf16[16,12288]{1,0:T(8,128)(2,1)S(1)} copy-done((bf16[16,12288]{1,0:T(8,128)(2,1)S(1)}, bf16[16,12288]{1,0:T(8,128)(2,1)}, u32[]{:S(2)}) %copy-start.2) | copy-done | bytes 393240
  7.4 2.4 %shard_map.181 = (bf16[8,16,3456]{2,1,0:T(8,128)(2,1)}, bf16[128,256]{1,0:T(8,128)(2,1)S(1)}) custom-call(s32[1,2]{1,0:T(1,128)S(1)} %copy-done.18, s32[2]{0:T(128)S(1)} %pad_add_fusion.me_ref, bf16[16,12288]{1,0:T(8,128)(2,1)S(1)} %copy-done, bf16[16,1024]{1,0:T(8,128)(2,1)S(1)} %copy-done.12, bf16[16,1024]{1,0:T(8,128)(2,1)S(1)} %copy-done.13, ...), custom_call_target="tpu_custom_call" | custom-call | tf_op jit(solution)/shard_map/pallas_call | solution.py:40
  9.8 7.1 %all-to-all-start = ((bf16[8,16,3456]{2,1,0:T(8,128)(2,1)}), bf16[8,16,3456]{2,1,0:T(8,128)(2,1)S(1)}, u32[]{:S(2)}, u32[]{:S(2)}) async-start(bf16[8,16,3456]{2,1,0:T(8,128)(2,1)} %get-tuple-element.42), calls=%async_computation | async-start | bytes 1769472 | tf_op jit(solution)/shard_map/all_to_all | solution.py:305
  17.5 11.5 %collective-permute-done = bf16[128,256]{1,0:T(8,128)(2,1)S(1)} collective-permute-done((bf16[128,256]{1,0:T(8,128)(2,1)S(1)}, bf16[128,256]{1,0:T(8,128)(2,1)S(1)}, u32[]{:S(2)}, u32[]{:S(2)}) %collective-permute-start) | collective-permute-done | bytes 65568 | tf_op jit(solution)/shard_map/ppermute | solution.py:292
  29.0 4.1 %collective-permute-start.3 = (bf16[256,256]{1,0:T(8,128)(2,1)S(1)}, bf16[256,256]{1,0:T(8,128)(2,1)S(1)}, u32[]{:S(2)}, u32[]{:S(2)}) collective-permute-start(bf16[256,256]{1,0:T(8,128)(2,1)S(1)} %constant_dynamic-update-slice_fusion.refs_0_), channel_id=1, source_target_pairs={{0,96},{8,104},{16,112},{24,120},{32,0},{40,8},{48,16},{56,24},{64... | collective-permute-start | bytes 393224 | tf_op jit(solution)/shard_map/ppermute | solution.py:295
  33.1 1.3 %collective-permute-start.1 = (bf16[256,256]{1,0:T(8,128)(2,1)S(1)}, bf16[256,256]{1,0:T(8,128)(2,1)S(1)}, u32[]{:S(2)}, u32[]{:S(2)}) collective-permute-start(bf16[256,256]{1,0:T(8,128)(2,1)S(1)} %constant_dynamic-update-slice_fusion.refs_0_), channel_id=1, source_target_pairs={{0,32},{8,40},{16,48},{24,56},{32,64},{40,72},{48,80},{56,88},{64,... | collective-permute-start | bytes 393224 | tf_op jit(solution)/shard_map/ppermute | solution.py:295
  34.4 3.4 %collective-permute-done.3.refs_2_.refs_3_ = bf16[256,256]{1,0:T(8,128)(2,1)S(1)} collective-permute-done((bf16[256,256]{1,0:T(8,128)(2,1)S(1)}, bf16[256,256]{1,0:T(8,128)(2,1)S(1)}, u32[]{:S(2)}, u32[]{:S(2)}) %collective-permute-start.3) | collective-permute-done | bytes 131104 | tf_op jit(solution)/shard_map/ppermute | solution.py:295
  37.8 2.4 %collective-permute-done.2.refs_1_.refs_2_ = bf16[256,256]{1,0:T(8,128)(2,1)S(1)} collective-permute-done((bf16[256,256]{1,0:T(8,128)(2,1)S(1)}, bf16[256,256]{1,0:T(8,128)(2,1)S(1)}, u32[]{:S(2)}, u32[]{:S(2)}) %collective-permute-start.2) | collective-permute-done | bytes 131104 | tf_op jit(solution)/shard_map/ppermute | solution.py:295
  40.2 1.0 %collective-permute-done.1.refs_0_.refs_1_ = bf16[256,256]{1,0:T(8,128)(2,1)S(1)} collective-permute-done((bf16[256,256]{1,0:T(8,128)(2,1)S(1)}, bf16[256,256]{1,0:T(8,128)(2,1)S(1)}, u32[]{:S(2)}, u32[]{:S(2)}) %collective-permute-start.1) | collective-permute-done | bytes 131104 | tf_op jit(solution)/shard_map/ppermute | solution.py:295
  41.4 3.6 %shard_map.182 = (f32[256,256]{1,0:T(8,128)S(1)}, f32[256,256]{1,0:T(8,128)S(1)}, f32[128,1536]{1,0:T(8,128)S(1)}, bf16[1536,128]{1,0:T(8,128)(2,1)S(1)}, bf16[1...) custom-call(s32[32]{0:T(128)S(1)} %copy-done.17, s32[2]{0:T(128)S(1)} %pad_add_fusion.me_ref, ...), custom_call_target="tpu_custom_call" | custom-call | tf_op jit(solution)/shard_map/pallas_call | solution.py:40
  45.7 7.7 %shard_map.183 = (bf16[128,1536]{1,0:T(8,128)(2,1)}, f32[256,256]{1,0:T(8,128)S(1)}, f32[256,256]{1,0:T(8,128)S(1)}, f32[256,256]{1,0:T(8,128)S(1)}, f32[256,256...) custom-call(s32[32]{0:T(128)S(1)} %copy-done.17, s32[2]{0:T(128)S(1)} %pad_add_fusion.me_ref, ...), custom_call_target="tpu_custom_call" | custom-call | tf_op jit(solution)/shard_map/pallas_call | solution.py:40
  54.8 0.9 %copy-done.9 = f32[256,256]{1,0:T(8,128)S(1)} copy-done((f32[256,256]{1,0:T(8,128)S(1)}, f32[256,256]{1,0:T(8,128)}, u32[]{:S(2)}) %copy-start.9) | copy-done | bytes 262168
  55.7 0.9 %copy-done.11 = f32[256,256]{1,0:T(8,128)S(1)} copy-done((f32[256,256]{1,0:T(8,128)S(1)}, f32[256,256]{1,0:T(8,128)}, u32[]{:S(2)}) %copy-start.11) | copy-done | bytes 262168
  56.7 4.4 %shard_map.184 = (bf16[4,256,256]{2,1,0:T(8,128)(2,1)S(1)}, f32[128,1536]{1,0:T(8,128)S(1)}, bf16[1536,128]{1,0:T(8,128)(2,1)S(1)}, bf16[1536,128]{1,0:T(8,128)(...) custom-call(bf16[128,3456]{1,0:T(8,128)(2,1)S(1)} %bitcast.19, ...), custom_call_target="tpu_custom_call" | custom-call | tf_op jit(solution)/shard_map/pallas_call | solution.py:40
  61.6 2.1 %shard_map.185 = (f32[4,128,256]{2,1,0:T(8,128)S(1)}, f32[128,1536]{1,0:T(8,128)S(1)}) custom-call(bf16[1536,128]{1,0:T(8,128)(2,1)S(1)} %get-tuple-element.47.qs_ref, bf16[1536,128]{1,0:T(8,128)(2,1)S(1)} %get-tuple-element.48.dos_ref, f32[1,1536]{1,0:T(1,128)S(1)} %get-tuple-element.49.lse_ref, f32[1,1536]{1,0:T(1,128)S(1)} %get-tuple-element.50.delta_ref, ...), custom_call_target="tpu_custom_call" | custom-call | tf_op jit(solution)/shard_map/pallas_call | solution.py:40
  64.5 1.4 %collective-permute-start.9 = (bf16[4,128,256]{2,1,0:T(8,128)(2,1)}, bf16[4,128,256]{2,1,0:T(8,128)(2,1)}, u32[]{:S(2)}, u32[]{:S(2)}) collective-permute-start(bf16[4,128,256]{2,1,0:T(8,128)(2,1)} %add_convert_fusion), channel_id=1, source_target_pairs={{0,16},{8,24},{16,0},{24,8},{32,48},{40,56},{48,32},{56,40},{64,80... | collective-permute-start | bytes 786440 | tf_op jit(solution)/shard_map/ppermute | solution.py:292
  66.0 4.3 %shard_map.186 = (f32[4,128,256]{2,1,0:T(8,128)S(1)}, bf16[8,16,1792]{2,1,0:T(8,128)(2,1)}) custom-call(s32[1,2]{1,0:T(1,128)S(1)} %copy-done.18, bf16[1536,128]{1,0:T(8,128)(2,1)S(1)} %get-tuple-element.47.qs_ref, bf16[1536,128]{1,0:T(8,128)(2,1)S(1)} %get-tuple-element.48.dos_ref, f32[1,1536]{1,0:T(1,128)S(1)} %get-tuple-element.49.lse_ref, ...), custom_call_target="tpu_custom_call" | custom-call | tf_op jit(solution)/shard_map/pallas_call | solution.py:40
  70.3 6.6 %all-to-all-start.1 = ((bf16[8,16,1792]{2,1,0:T(8,128)(2,1)}), bf16[8,16,1792]{2,1,0:T(8,128)(2,1)S(1)}, u32[]{:S(2)}, u32[]{:S(2)}) async-start(bf16[8,16,1792]{2,1,0:T(8,128)(2,1)} %get-tuple-element.60), calls=%async_computation.1 | async-start | bytes 917504 | tf_op jit(solution)/shard_map/all_to_all | solution.py:350
  76.9 1.0 %fusion.4 = (bf16[4,128,256]{2,1,0:T(8,128)(2,1)S(1)}, f32[4,128,256]{2,1,0:T(8,128)S(1)}) fusion(bf16[4,128,256]{2,1,0:T(8,128)(2,1)} %collective-permute-done.9, f32[4,128,256]{2,1,0:T(8,128)S(1)} %get-tuple-element.57, bf16[4,256,256]{2,1,0:T(8,128)(2,1)S(1)} %collective-permute-done.8), kind=kLoop, calls=%fused_computation.13 | loop fusion | flops 655360 | bytes 1835008 | tf_op jit(solution)/shard_map/convert.2
  77.9 1.0 %collective-permute-start.10 = (bf16[128,256]{1,0:T(8,128)(2,1)S(1)}, bf16[128,256]{1,0:T(8,128)(2,1)S(1)}, u32[]{:S(2)}, u32[]{:S(2)}) collective-permute-start(bf16[128,256]{1,0:T(8,128)(2,1)S(1)} %get-tuple-element.66), channel_id=1, source_target_pairs={{0,96},{8,104},{16,112},{24,120},{32,0},{40,8},{48,16},{56,24},{64... | collective-permute-start | bytes 196616 | tf_op jit(solution)/shard_map/ppermute | solution.py:295
  78.9 1.1 %collective-permute-start.12 = (bf16[128,256]{1,0:T(8,128)(2,1)S(1)}, bf16[128,256]{1,0:T(8,128)(2,1)S(1)}, u32[]{:S(2)}, u32[]{:S(2)}) collective-permute-start(bf16[128,256]{1,0:T(8,128)(2,1)S(1)} %get-tuple-element.67), channel_id=1, source_target_pairs={{0,32},{8,40},{16,48},{24,56},{32,64},{40,72},{48,80},{56,88},{64,... | collective-permute-start | bytes 196616 | tf_op jit(solution)/shard_map/ppermute | solution.py:295
  80.7 6.6 %all-to-all-done.1.back_ref = bf16[8,16,1792]{2,1,0:T(8,128)(2,1)S(1)} async-done(((bf16[8,16,1792]{2,1,0:T(8,128)(2,1)}), bf16[8,16,1792]{2,1,0:T(8,128)(2,1)S(1)}, u32[]{:S(2)}, u32[]{:S(2)}) %all-to-all-start.1) | async-done | bytes 458784 | tf_op jit(solution)/shard_map/all_to_all | solution.py:350
  (62 shorter events, 10.1 us)
Async XLA Ops:
  1.3 1.0 %copy-start = (bf16[16,12288]{1,0:T(8,128)(2,1)S(1)}, bf16[16,12288]{1,0:T(8,128)(2,1)}, u32[]{:S(2)}) copy-start(bf16[16,12288]{1,0:T(8,128)(2,1)} %q_ref.1) | copy-start | bytes 1179652
  2.3 1.0 %copy-start.1 = (bf16[16,12288]{1,0:T(8,128)(2,1)S(1)}, bf16[16,12288]{1,0:T(8,128)(2,1)}, u32[]{:S(2)}) copy-start(bf16[16,12288]{1,0:T(8,128)(2,1)} %o_ref.1) | copy-start | bytes 1179652
  3.3 1.0 %copy-start.2 = (bf16[16,12288]{1,0:T(8,128)(2,1)S(1)}, bf16[16,12288]{1,0:T(8,128)(2,1)}, u32[]{:S(2)}) copy-start(bf16[16,12288]{1,0:T(8,128)(2,1)} %do_ref.1) | copy-start | bytes 1179652
  9.7 31.6 %copy-start.3 = (bf16[128,1536]{1,0:T(8,128)(2,1)S(1)}, bf16[128,1536]{1,0:T(8,128)(2,1)}, u32[]{:S(2)}) copy-start(bf16[128,1536]{1,0:T(8,128)(2,1)} %refs_2_.1) | copy-start | bytes 1179652
  9.7 31.6 %copy-start.4 = (bf16[128,1536]{1,0:T(8,128)(2,1)S(1)}, bf16[128,1536]{1,0:T(8,128)(2,1)}, u32[]{:S(2)}) copy-start(bf16[128,1536]{1,0:T(8,128)(2,1)} %refs_3_.1) | copy-start | bytes 1179652
  9.8 31.6 %copy-start.5 = (bf16[128,1536]{1,0:T(8,128)(2,1)S(1)}, bf16[128,1536]{1,0:T(8,128)(2,1)}, u32[]{:S(2)}) copy-start(bf16[128,1536]{1,0:T(8,128)(2,1)} %refs_4_.1) | copy-start | bytes 1179652
  9.8 45.0 %all-to-all-start = ((bf16[8,16,3456]{2,1,0:T(8,128)(2,1)}), bf16[8,16,3456]{2,1,0:T(8,128)(2,1)S(1)}, u32[]{:S(2)}, u32[]{:S(2)}) async-start(bf16[8,16,3456]{2,1,0:T(8,128)(2,1)} %get-tuple-element.42), calls=%async_computation | async-start | bytes 1769472 | tf_op jit(solution)/shard_map/all_to_all | solution.py:305
  16.9 12.1 %collective-permute-start = (bf16[128,256]{1,0:T(8,128)(2,1)S(1)}, bf16[128,256]{1,0:T(8,128)(2,1)S(1)}, u32[]{:S(2)}, u32[]{:S(2)}) collective-permute-start(bf16[128,256]{1,0:T(8,128)(2,1)S(1)} %get-tuple-element.35), channel_id=1, source_target_pairs={{0,16},{8,24},{16,0},{24,8},{32,48},{40,56},{48,32},{56,40},{64,80... | collective-permute-start | bytes 196616 | tf_op jit(solution)/shard_map/ppermute | solution.py:292
  17.5 23.7 %copy-start.19 = (f32[128,12]{0,1:T(8,128)S(1)}, f32[128,12]{0,1:T(8,128)}, u32[]{:S(2)}) copy-start(f32[128,12]{0,1:T(8,128)} %param.21) | copy-start | bytes 18436
  29.0 12.4 %copy-start.17 = (s32[32]{0:T(128)S(1)}, s32[32]{0:T(128)}, u32[]{:S(2)}) copy-start(s32[32]{0:T(128)} %order_ref.3) | copy-start | bytes 388
  29.0 8.8 %collective-permute-start.3 = (bf16[256,256]{1,0:T(8,128)(2,1)S(1)}, bf16[256,256]{1,0:T(8,128)(2,1)S(1)}, u32[]{:S(2)}, u32[]{:S(2)}) collective-permute-start(bf16[256,256]{1,0:T(8,128)(2,1)S(1)} %constant_dynamic-update-slice_fusion.refs_0_), channel_id=1, source_target_pairs={{0,96},{8,104},{16,112},{24,120},{32,0},{40,8},{48,16},{56,24},{64... | collective-permute-start | bytes 393224 | tf_op jit(solution)/shard_map/ppermute | solution.py:295
  33.1 7.1 %collective-permute-start.2 = (bf16[256,256]{1,0:T(8,128)(2,1)S(1)}, bf16[256,256]{1,0:T(8,128)(2,1)S(1)}, u32[]{:S(2)}, u32[]{:S(2)}) collective-permute-start(bf16[256,256]{1,0:T(8,128)(2,1)S(1)} %constant_dynamic-update-slice_fusion.refs_0_), channel_id=1, source_target_pairs={{0,64},{8,72},{16,80},{24,88},{32,96},{40,104},{48,112},{56,120},{... | collective-permute-start | bytes 393224 | tf_op jit(solution)/shard_map/ppermute | solution.py:295
  33.1 8.1 %collective-permute-start.1 = (bf16[256,256]{1,0:T(8,128)(2,1)S(1)}, bf16[256,256]{1,0:T(8,128)(2,1)S(1)}, u32[]{:S(2)}, u32[]{:S(2)}) collective-permute-start(bf16[256,256]{1,0:T(8,128)(2,1)S(1)} %constant_dynamic-update-slice_fusion.refs_0_), channel_id=1, source_target_pairs={{0,32},{8,40},{16,48},{24,56},{32,64},{40,72},{48,80},{56,88},{64,... | collective-permute-start | bytes 393224 | tf_op jit(solution)/shard_map/ppermute | solution.py:295
  34.4 7.0 %collective-permute-start.7 = (bf16[256,256]{1,0:T(8,128)(2,1)S(1)}, bf16[256,256]{1,0:T(8,128)(2,1)S(1)}, u32[]{:S(2)}, u32[]{:S(2)}) collective-permute-start(bf16[256,256]{1,0:T(8,128)(2,1)S(1)} %constant_dynamic-update-slice_fusion.refs_0_), channel_id=1, source_target_pairs={{0,8},{8,0},{16,24},{24,16},{32,40},{40,32},{48,56},{56,48},{64,72... | collective-permute-start | bytes 393224 | tf_op jit(solution)/shard_map/ppermute | solution.py:289
  37.8 7.8 %collective-permute-start.6 = (bf16[256,256]{1,0:T(8,128)(2,1)S(1)}, bf16[256,256]{1,0:T(8,128)(2,1)S(1)}, u32[]{:S(2)}, u32[]{:S(2)}) collective-permute-start(bf16[256,256]{1,0:T(8,128)(2,1)S(1)} %collective-permute-done.3.refs_2_.refs_3_), channel_id=1, source_target_pairs={{0,8},{8,0},{16,24},{24,16},{32,40},{40,32},{48,56},{56,48},{64,72... | collective-permute-start | bytes 393224 | tf_op jit(solution)/shard_map/ppermute | solution.py:289
  40.2 5.4 %collective-permute-start.5 = (bf16[256,256]{1,0:T(8,128)(2,1)S(1)}, bf16[256,256]{1,0:T(8,128)(2,1)S(1)}, u32[]{:S(2)}, u32[]{:S(2)}) collective-permute-start(bf16[256,256]{1,0:T(8,128)(2,1)S(1)} %collective-permute-done.2.refs_1_.refs_2_), channel_id=1, source_target_pairs={{0,8},{8,0},{16,24},{24,16},{32,40},{40,32},{48,56},{56,48},{64,72... | collective-permute-start | bytes 393224 | tf_op jit(solution)/shard_map/ppermute | solution.py:289
  41.2 4.4 %collective-permute-start.4 = (bf16[256,256]{1,0:T(8,128)(2,1)S(1)}, bf16[256,256]{1,0:T(8,128)(2,1)S(1)}, u32[]{:S(2)}, u32[]{:S(2)}) collective-permute-start(bf16[256,256]{1,0:T(8,128)(2,1)S(1)} %collective-permute-done.1.refs_0_.refs_1_), channel_id=1, source_target_pairs={{0,8},{8,0},{16,24},{24,16},{32,40},{40,32},{48,56},{56,48},{64,72... | collective-permute-start | bytes 393224 | tf_op jit(solution)/shard_map/ppermute | solution.py:289
  45.7 9.1 %copy-start.7 = (f32[256,256]{1,0:T(8,128)S(1)}, f32[256,256]{1,0:T(8,128)}, u32[]{:S(2)}) copy-start(f32[256,256]{1,0:T(8,128)} %copy-done.6) | copy-start | bytes 786436
  61.0 2.7 %collective-permute-start.8 = (bf16[4,256,256]{2,1,0:T(8,128)(2,1)S(1)}, bf16[4,256,256]{2,1,0:T(8,128)(2,1)S(1)}, u32[]{:S(2)}, u32[]{:S(2)}) collective-permute-start(bf16[4,256,256]{2,1,0:T(8,128)(2,1)S(1)} %get-tuple-element.58), channel_id=1, source_target_pairs={{0,8},{8,0},{16,24},{24,16},{32,40},{40,32},{48,56},{56,48},{64,72... | collective-permute-start | bytes 1572872 | tf_op jit(solution)/shard_map/ppermute | solution.py:289
  64.5 12.3 %collective-permute-start.9 = (bf16[4,128,256]{2,1,0:T(8,128)(2,1)}, bf16[4,128,256]{2,1,0:T(8,128)(2,1)}, u32[]{:S(2)}, u32[]{:S(2)}) collective-permute-start(bf16[4,128,256]{2,1,0:T(8,128)(2,1)} %add_convert_fusion), channel_id=1, source_target_pairs={{0,16},{8,24},{16,0},{24,8},{32,48},{40,56},{48,32},{56,40},{64,80... | collective-permute-start | bytes 786440 | tf_op jit(solution)/shard_map/ppermute | solution.py:292
  70.3 17.1 %all-to-all-start.1 = ((bf16[8,16,1792]{2,1,0:T(8,128)(2,1)}), bf16[8,16,1792]{2,1,0:T(8,128)(2,1)S(1)}, u32[]{:S(2)}, u32[]{:S(2)}) async-start(bf16[8,16,1792]{2,1,0:T(8,128)(2,1)} %get-tuple-element.60), calls=%async_computation.1 | async-start | bytes 917504 | tf_op jit(solution)/shard_map/all_to_all | solution.py:350
  77.9 10.2 %collective-permute-start.10 = (bf16[128,256]{1,0:T(8,128)(2,1)S(1)}, bf16[128,256]{1,0:T(8,128)(2,1)S(1)}, u32[]{:S(2)}, u32[]{:S(2)}) collective-permute-start(bf16[128,256]{1,0:T(8,128)(2,1)S(1)} %get-tuple-element.66), channel_id=1, source_target_pairs={{0,96},{8,104},{16,112},{24,120},{32,0},{40,8},{48,16},{56,24},{64... | collective-permute-start | bytes 196616 | tf_op jit(solution)/shard_map/ppermute | solution.py:295
  78.9 9.2 %collective-permute-start.12 = (bf16[128,256]{1,0:T(8,128)(2,1)S(1)}, bf16[128,256]{1,0:T(8,128)(2,1)S(1)}, u32[]{:S(2)}, u32[]{:S(2)}) collective-permute-start(bf16[128,256]{1,0:T(8,128)(2,1)S(1)} %get-tuple-element.67), channel_id=1, source_target_pairs={{0,32},{8,40},{16,48},{24,56},{32,64},{40,72},{48,80},{56,88},{64,... | collective-permute-start | bytes 196616 | tf_op jit(solution)/shard_map/ppermute | solution.py:295
  80.0 8.1 %collective-permute-start.11 = (bf16[128,256]{1,0:T(8,128)(2,1)S(1)}, bf16[128,256]{1,0:T(8,128)(2,1)S(1)}, u32[]{:S(2)}, u32[]{:S(2)}) collective-permute-start(bf16[128,256]{1,0:T(8,128)(2,1)S(1)} %get-tuple-element.68), channel_id=1, source_target_pairs={{0,64},{8,72},{16,80},{24,88},{32,96},{40,104},{48,112},{56,120},{... | collective-permute-start | bytes 196616 | tf_op jit(solution)/shard_map/ppermute | solution.py:295
  (11 other events, 8.4 us)

commit v2 on v1

v2 whole, which is shorter than its diff:
```python
import functools

import jax
import jax.numpy as jnp
from jax import lax
from jax.experimental import pallas as pl
from jax.experimental.pallas import tpu as pltpu
from jax.sharding import PartitionSpec as P

D = 128
SCALE = D**-0.5
LOG2E = 1.4426950408889634
HIDDEN = 1e30
BF = jnp.bfloat16
F32 = jnp.float32
SHARED = pltpu.CompilerParams(vmem_limit_bytes=20 * 2**20)
WHOLE = pltpu.CompilerParams(vmem_limit_bytes=60 * 2**20)


def dot(a, b, ca, cb):
    return lax.dot_general(a, b, (((ca,), (cb,)), ((), ())), preferred_element_type=F32)


def lanes(shape):
    return lax.broadcasted_iota(jnp.int32, shape, 1)


def sublanes(shape):
    return lax.broadcasted_iota(jnp.int32, shape, 0)


def smem():
    return pl.BlockSpec(memory_space=pltpu.SMEM)


def vmem():
    return pl.BlockSpec(memory_space=pltpu.VMEM)


def hbm():
    return pl.BlockSpec(memory_space=pltpu.HBM)


def cost(us):
    return pl.CostEstimate(flops=int(us * 1.1e9), bytes_accessed=0, transcendentals=0)


def call(us, body, outs, n_smem, *args, **kw):
    return pl.pallas_call(
        body,
        out_shape=tuple(jax.ShapeDtypeStruct(s, t) for s, t in outs),
        in_specs=[smem()] * n_smem + [vmem()] * (len(args) - n_smem),
        out_specs=tuple(vmem() for _ in outs),
        compiler_params=SHARED,
        cost_estimate=cost(us),
        **kw,
    )(*args)


def pair_block(qs_ref, dos_ref, keys, values, lse, delta, mask):
    scores = dot(keys, qs_ref[...], 1, 1)
    dprob = dot(values, dos_ref[...], 1, 1)
    prob = jnp.exp2(scores * (SCALE * LOG2E) - lse)
    if mask is not None:
        prob = jnp.where(mask, prob, 0.0)
    dscore = (prob * (dprob - delta)).astype(BF)
    dv = dot(prob.astype(BF), dos_ref[...], 1, 0)
    dk = dot(dscore, qs_ref[...], 1, 0) * SCALE
    dq = dot(keys, dscore, 0, 0)
    return dq, dk, dv


def both(ref):
    keys = jnp.concatenate([ref[:D], ref[2 * D : 3 * D]], axis=0)
    values = jnp.concatenate([ref[D : 2 * D], ref[3 * D :]], axis=0)
    return keys, values


def stack_heads(source, target, heads, first):
    for j in range(heads):
        at = first + j * D
        target[j * D : (j + 1) * D, :] = source[:, at : at + D]


def spread_rows(rows, target, heads):
    for j in range(heads):
        target[:, j * D : (j + 1) * D] = rows[j : j + 1, :]


def unstack_query_grad(dq, heads):
    return [(dq[:, j * D : (j + 1) * D].T * SCALE).astype(BF) for j in range(heads)]


def stats_kernel(heads, groups, total, len_ref, me_ref, o_ref, do_ref, ex_ref, packed, out, grad, buf, sems):
    rows = out.shape[0]
    wide = heads * D
    loads = [pltpu.make_async_copy(source, to, sems.at[n]) for n, (source, to) in enumerate(((o_ref, out), (do_ref, grad), (ex_ref, buf)))]
    for load in loads:
        load.start()
    row = me_ref[1] * rows + sublanes((rows, D))
    within = jnp.where(row < len_ref[0, 0], row, row - len_ref[0, 0])
    log_count = jnp.log((within + 1 + total).astype(F32))
    for load in loads:
        load.wait()
    lse = (buf[...] + log_count[:, : heads * groups]) * LOG2E
    lse = jnp.concatenate([lse, jnp.zeros((rows, D - heads * groups), F32)], axis=1)
    lane = lanes((rows, D))
    for g in range(groups):
        delta = jnp.zeros((rows, D), F32)
        for j in range(heads):
            cut = slice(g * wide + j * D, g * wide + (j + 1) * D)
            product = out[:, cut].astype(F32) * grad[:, cut].astype(F32)
            delta = jnp.where(lane == j, jnp.sum(product, axis=1, keepdims=True), delta)
        mine = lse if g == 0 else pltpu.roll(lse, D - heads * g, 1)
        mine = jnp.where(lane < heads, mine, 0.0)
        stats = jnp.zeros((rows, D), F32)
        for n, value in enumerate((mine, delta)):
            for m in range(3):
                part = value.astype(BF).astype(F32)
                value = value - part
                at = (3 * n + m) * 16
                stats = stats + (pltpu.roll(part, at, 1) if at else part)
        packed[g] = stats.astype(BF)


def pack_kernel(heads, groups, stats_ref, q_ref, do_ref, k_ref, v_ref, pay_ref, stats, query, grad, keys, values, sems):
    wide = heads * D
    pairs = ((q_ref, query), (do_ref, grad), (k_ref, keys), (v_ref, values), (stats_ref, stats))
    loads = [pltpu.make_async_copy(source, to, sems.at[n]) for n, (source, to) in enumerate(pairs)]
    for load in loads:
        load.start()
    sends = []
    for n, (source, to, size) in enumerate(((query, 0, wide), (grad, wide, wide), (keys, 2 * wide, D), (values, 2 * wide + D, D))):
        loads[n].wait()
        for g in range(groups):
            part = pay_ref.at[g, :, pl.ds(to, size)]
            sends.append(pltpu.make_async_copy(source.at[:, pl.ds(g * size, size)], part, sems.at[5 + n * groups + g]))
            sends[-1].start()
    loads[4].wait()
    sends.append(pltpu.make_async_copy(stats, pay_ref.at[:, :, pl.ds(2 * wide + 2 * D, D)], sems.at[5 + 4 * groups]))
    sends[-1].start()
    for copy in sends:
        copy.wait()


def doc_keys(order_ref, me, ctx_size, piece):
    core, z = piece
    place, low, step = me // 4, (me // 2) % 2, ctx_size // 4
    depth = lax.rem(place + step - z, step)
    return [(depth * 2 + (low ^ x if isinstance(low, int) else lax.bitwise_xor(low, x))) * 2 + lax.bitwise_xor(lax.rem(me, 2), core) for x in range(2)]


def doc_lse(order_ref, me, owner, lse, lane_half):
    parts = []
    for b in range(2):
        kb = order_ref[2 * owner + b]
        bias = [jnp.where(kb <= order_ref[2 * me + a], 0.0, HIDDEN).astype(F32) for a in range(2)]
        hide = jnp.where(lane_half, bias[1], bias[0])
        parts.append(jnp.broadcast_to(lse + hide, (D // 2, lse.shape[1])))
    return jnp.concatenate(parts, axis=0)


def doc_kernel(core, heads, ctx_size, order_ref, me_ref, *refs):
    kv_hbm, refs = refs[:4], refs[4:]
    kv_refs, sems = refs[-2:]
    if core == 0:
        ins, state_hbm, (dq_hbm, near_hbm, own_hbm) = refs[:4], refs[4:8], refs[8:11]
        bufs, state, (dq_ref, near_ref, own_ref) = refs[11:15], refs[15:19], refs[19:22]
        q_ref, o_ref, do_ref, ex_ref = bufs
    else:
        ins, (dq_hbm, far_hbm) = refs[:5], refs[5:7]
        bufs, (dq_ref, far_ref) = refs[7:12], refs[12:14]
        state = bufs[:4]
    qs_ref, dos_ref, lse_ref, delta_ref = state
    loads = [pltpu.make_async_copy(source, to, sems.at[n]) for n, (source, to) in enumerate(zip(ins, bufs))]
    pieces = [pltpu.make_async_copy(kv_hbm[n], kv_refs.at[n], sems.at[5 + n]) for n in range(4)]
    for load in loads[:4] + pieces + loads[4:]:
        load.start()
    stores = []

    def store(source, to):
        stores.append(pltpu.make_async_copy(source, to, sems.at[9 + len(stores)]))
        stores[-1].start()

    me = me_ref[0]
    rows = heads * D
    lane = lax.rem(lanes((1, rows)), D)
    half = D // 2
    lane_half = lane >= half
    if core == 0:
        loads[3].wait()
        one = lanes((1, D))
        pos = jnp.where(one < half, order_ref[2 * me] * half + one, order_ref[2 * me + 1] * half + one - half)
        spread_rows((ex_ref[...] + jnp.log((pos + 1).astype(F32))) * LOG2E, lse_ref, heads)
        loads[0].wait()
        stack_heads(q_ref, qs_ref, heads, 0)
        loads[2].wait()
        stack_heads(do_ref, dos_ref, heads, 0)
        loads[1].wait()
        at = lanes((D, D))
        stats = jnp.zeros((D, D), F32)
        for j in range(heads):
            cut = slice(j * D, (j + 1) * D)
            product = o_ref[:, cut].astype(F32) * do_ref[:, cut].astype(F32)
            stats = jnp.where(at == j, jnp.sum(product, axis=1, keepdims=True), stats)
        spread_rows(stats.T[:16], delta_ref, heads)
        for source, to in zip(state, state_hbm):
            store(source, to)
    else:
        for load in loads[:4]:
            load.wait()
    lse = lse_ref[...]
    delta = delta_ref[...]
    total = None
    for depth in range(4):
        owners = doc_keys(order_ref, me, ctx_size, (core, depth))
        shift = jnp.concatenate([doc_lse(order_ref, me, o, lse, lane_half) for o in owners], axis=0)
        mask = None
        if core == 0 and depth == 0:
            key = sublanes((2 * D, 1))
            key_pos = jnp.where(key < half, order_ref[2 * me] * half + key, order_ref[2 * me + 1] * half + key - half)
            row_pos = jnp.where(lane_half, order_ref[2 * me + 1] * half + lane - half, order_ref[2 * me] * half + lane)
            mask = jnp.where(key < D, key_pos, -1) <= row_pos
        pieces[depth].wait()
        dq, dk, dv = pair_block(qs_ref, dos_ref, *both(kv_refs.at[depth]), shift, delta, mask)
        for side, grad in enumerate((dk, dv)):
            cut = slice(side * D, (side + 1) * D)
            if core == 0:
                own_ref[depth, :, cut] = grad[:D]
                near_ref[depth, :, cut] = grad[D:]
            else:
                far_ref[depth, :, cut] = grad
        total = dq if total is None else total + dq
        if core == 0:
            store(own_ref.at[depth], own_hbm.at[depth])
            store(near_ref.at[depth], near_hbm.at[depth])
        else:
            store(far_ref.at[depth], far_hbm.at[depth])
    if core == 0:
        dq_ref[...] = total
    else:
        loads[4].wait()
        for j, part in enumerate(unstack_query_grad(total + bufs[4][...], heads)):
            dq_ref[:, j * D : (j + 1) * D] = part
    store(dq_ref, dq_hbm)
    for copy in stores:
        copy.wait()


def self_kernel(heads, len_ref, pay_ref, qs_ref, dos_ref, lse_ref, delta_ref, self_ref, dq_ref):
    wide = heads * D
    stack_heads(pay_ref, qs_ref, heads, 0)
    stack_heads(pay_ref, dos_ref, heads, wide)
    stats = pay_ref[:, 2 * wide + 2 * D :].astype(F32).T
    spread_rows(stats[:16] + stats[16:32] + stats[32:48], lse_ref, heads)
    spread_rows(stats[48:64] + stats[64:80] + stats[80:96], delta_ref, heads)
    row = lax.rem(lanes((1, wide)), D)
    key = sublanes((D, 1))
    first = len_ref[0, 0]
    mask = (key <= row) & ((key >= first) | (row < first))
    keys = pay_ref[:, 2 * wide : 2 * wide + D]
    values = pay_ref[:, 2 * wide + D : 2 * wide + 2 * D]
    dq, dk, dv = pair_block(qs_ref, dos_ref, keys, values, lse_ref[...], delta_ref[...], mask)
    self_ref[:, :D] = dk.astype(BF)
    self_ref[:, D:] = dv.astype(BF)
    dq_ref[...] = dq


def far_kernel(qs_ref, dos_ref, lse_ref, delta_ref, dq_in, *refs):
    kv_refs, doc_ref = refs[:4], refs[4]
    send_ref, dq_ref = refs[5:]
    lse, delta = lse_ref[...], delta_ref[...]
    total = dq_in[...]
    for n in range(4):
        dq, dk, dv = pair_block(qs_ref, dos_ref, *both(kv_refs[n]), lse, delta, None)
        send_ref[n, :, :D] = (dk + doc_ref[n, :, :D]).astype(BF)
        send_ref[n, :, D:] = (dv + doc_ref[n, :, D:]).astype(BF)
        total = total + dq
    dq_ref[...] = total


def column(x, qs_ref, dos_ref, lse, delta, kv_refs, total, store):
    for pair in range(len(kv_refs) // 2):
        refs = [kv_refs[2 * pair + m] for m in range(2)]
        keys = jnp.concatenate([ref[2 * x * D : 2 * x * D + D] for ref in refs], axis=0)
        values = jnp.concatenate([ref[2 * x * D + D : 2 * x * D + 2 * D] for ref in refs], axis=0)
        dq, dk, dv = pair_block(qs_ref, dos_ref, keys, values, lse, delta, None)
        for m in range(2):
            part = slice(m * D, (m + 1) * D)
            store(2 * pair + m, slice(0, D), dk[part])
            store(2 * pair + m, slice(D, 2 * D), dv[part])
        total = total + dq
    return total


def near_kernel(qs_ref, dos_ref, lse_ref, delta_ref, dq_in, core_ref, *refs):
    kv_refs, doc_ref = refs[:4], refs[4]
    send_ref, dq_ref = refs[5:]

    def store(n, cut, grad):
        send_ref[n, :, cut] = (grad + doc_ref[n, :, cut] + core_ref[n, D:, cut].astype(F32)).astype(BF)

    dq_ref[...] = column(1, qs_ref, dos_ref, lse_ref[...], delta_ref[...], kv_refs, dq_in[...], store)


def own_kernel(qs_ref, dos_ref, lse_ref, delta_ref, dq_in, *refs):
    kv_refs = refs[:2]
    out_ref, dq_ref = refs[2:]

    def store(n, cut, grad):
        out_ref[n, :, cut] = grad

    dq_ref[...] = column(0, qs_ref, dos_ref, lse_ref[...], delta_ref[...], kv_refs, dq_in[...], store)


def last_kernel(heads, groups, qs_ref, dos_ref, lse_ref, delta_ref, dq_in, self_ref, *refs):
    kv_refs = refs[:2]
    out_ref, back_ref = refs[2:]
    wide = heads * D

    def store(n, cut, grad):
        out_ref[n, :, cut] = grad

    total = column(0, qs_ref, dos_ref, lse_ref[...], delta_ref[...], kv_refs, dq_in[...], store)
    each = D // groups
    for g in range(groups):
        back_ref[g, :, wide:] = self_ref[g * each : (g + 1) * each]
    for j, part in enumerate(unstack_query_grad(total, heads)):
        for g in range(groups):
            back_ref[g, :, j * D : (j + 1) * D] = part[g * each : (g + 1) * each]


def held_kernel(low_ref, high_ref, doc_ref, core_ref, chip_ref, keep_ref, *send_refs):
    for n in range(4):
        own = low_ref[n] if n < 2 else high_ref[n - 2]
        held = own + doc_ref[n] + core_ref[n, :D].astype(F32) + chip_ref[n].astype(F32)
        if n == 0:
            keep_ref[...] = held
        else:
            send_refs[n - 1][...] = held.astype(BF)


def unpack_kernel(heads, groups, back_ref, keep_ref, *refs):
    q_ref, k_ref, v_ref, dk_ref, dv_ref = refs[3:]
    wide = heads * D
    total = keep_ref[...]
    for ref in refs[:3]:
        total = total + ref[...].astype(F32)
    dk_ref[...] = total[:, :D].astype(BF)
    dv_ref[...] = total[:, D:].astype(BF)
    for g in range(groups):
        q_ref[:, g * wide : (g + 1) * wide] = back_ref[g, :, :wide]
        k_ref[:, g * D : (g + 1) * D] = back_ref[g, :, wide : wide + D]
        v_ref[:, g * D : (g + 1) * D] = back_ref[g, :, wide + D :]


def local(
    block_order,
    question_lengths,
    document_query_matrix,
    document_key_matrix,
    document_value_matrix,
    document_output,
    document_outgrad,
    document_excess,
    question_query_matrix,
    question_key_matrix,
    question_value_matrix,
    question_output,
    question_outgrad,
    question_excess,
):
    ctx_size, groups = lax.axis_size("ctx"), lax.axis_size("head")
    heads = document_excess.shape[1]
    rows, each = document_query_matrix.shape[0], question_query_matrix.shape[0]
    total_doc = rows * ctx_size
    wide, stacked = heads * D, heads * rows
    me = jnp.stack([lax.axis_index("ctx"), lax.axis_index("head")]).astype(jnp.int32)
    depth = ctx_size // 4

    def other_core(x):
        return lax.ppermute(x, "ctx", [(i, i ^ 1) for i in range(ctx_size)])

    def other_chip(x):
        return lax.ppermute(x, "ctx", [(i, i ^ 2) for i in range(ctx_size)])

    def along_z(x, d):
        return lax.ppermute(x, "ctx", [(i, (i + 4 * d) % ctx_size) for i in range(ctx_size)])

    kv = jnp.concatenate([document_key_matrix, document_value_matrix], axis=0)
    here = jnp.concatenate([kv, other_chip(kv)], axis=0)
    mine = [here] + [along_z(here, d) for d in range(1, depth)]
    theirs = [other_core(piece) for piece in mine]
    def copying(us, body, outs, n_smem, scratch, *args):
        return pl.pallas_call(
            body,
            out_shape=tuple(jax.ShapeDtypeStruct(s, t) for s, t in outs),
            in_specs=[smem()] * n_smem + [hbm()] * (len(args) - n_smem),
            out_specs=(hbm(),) * len(outs),
            scratch_shapes=scratch,
            compiler_params=WHOLE,
            cost_estimate=cost(us),
        )(*args)

    asking = pltpu.VMEM((each, wide * groups), BF)
    parts = (groups, each, D)
    stats = pl.pallas_call(
        functools.partial(stats_kernel, heads, groups, total_doc),
        out_shape=jax.ShapeDtypeStruct(parts, BF),
        in_specs=[smem()] * 2 + [hbm()] * 3,
        out_specs=vmem(),
        scratch_shapes=[asking, asking, pltpu.VMEM((each, heads * groups), F32), pltpu.SemaphoreType.DMA((3,))],
        compiler_params=WHOLE,
        cost_estimate=cost(3),
    )(question_lengths, me, question_output, question_outgrad, question_excess)
    (payload,) = copying(
        4,
        functools.partial(pack_kernel, heads, groups),
        [((groups, each, 2 * wide + 3 * D), BF)],
        0,
        [pltpu.VMEM(parts, BF), asking, asking]
        + [pltpu.VMEM((each, D * groups), BF)] * 2
        + [pltpu.SemaphoreType.DMA((6 + 4 * groups,))],
        stats, question_query_matrix, question_outgrad, question_key_matrix, question_value_matrix,
    )
    asked = lax.all_to_all(payload, "head", 0, 0, tiled=True).reshape(groups * each, -1)

    quarter = ((depth, rows, 2 * D), F32)
    double = ((depth, 2 * rows, 2 * D), F32)
    row_state = [((stacked, D), BF), ((stacked, D), BF), ((1, stacked), F32), ((1, stacked), F32)]
    query_sum = ((D, stacked), F32)
    flat = ((rows, wide), BF)

    def held(*shapes):
        return [pltpu.VMEM(*shape) for shape in shapes] + [pltpu.VMEM((depth, 4 * rows, D), BF), pltpu.SemaphoreType.DMA((24,))]

    *doc_state, dq, near_doc, own_doc = copying(
        6,
        functools.partial(doc_kernel, 0, heads, ctx_size),
        row_state + [query_sum, quarter, quarter],
        2,
        held(flat, flat, flat, ((heads, rows), F32), *row_state, query_sum, quarter, quarter),
        block_order, me, *mine, document_query_matrix, document_output, document_outgrad, document_excess.T,
    )
    document_query_grad, far_doc = copying(
        6,
        functools.partial(doc_kernel, 1, heads, ctx_size),
        [flat, double],
        2,
        held(*row_state, query_sum, flat, double),
        block_order, me, *theirs, *doc_state, dq,
    )
    *state, own_self, dq = call(
        1.5,
        functools.partial(self_kernel, heads),
        row_state + [((rows, 2 * D), BF), query_sum],
        1,
        question_lengths, asked,
    )
    far, dq = call(4.4, far_kernel, [((depth, 2 * rows, 2 * D), BF), query_sum], 0, *state, dq, *theirs, far_doc)
    core_sum = other_core(far)
    low, dq = call(1.5, own_kernel, [((2, rows, 2 * D), F32), query_sum], 0, *state, dq, *mine[:2])
    near, dq = call(2.2, near_kernel, [((depth, rows, 2 * D), BF), query_sum], 0, *state, dq, core_sum, *mine, near_doc)
    chip_sum = other_chip(near)
    high, back = call(
        2,
        functools.partial(last_kernel, heads, groups),
        [((2, rows, 2 * D), F32), ((groups, each, wide + 2 * D), BF)],
        0,
        *state, dq, own_self, *mine[2:],
    )
    back = lax.all_to_all(back, "head", 0, 0, tiled=True)
    keep, *sends = call(
        25,
        held_kernel,
        [((rows, 2 * D), F32)] + [((rows, 2 * D), BF)] * (depth - 1),
        0,
        low, high, own_doc, core_sum, chip_sum,
    )
    arrived = [along_z(send, depth - 1 - n) for n, send in enumerate(sends)]
    question_query_grad, question_keys_grad, question_values_grad, document_keys_grad, document_values_grad = call(
        0.8,
        functools.partial(unpack_kernel, heads, groups),
        [((each, wide * groups), BF), ((each, D * groups), BF), ((each, D * groups), BF), ((rows, D), BF), ((rows, D), BF)],
        0,
        back, keep, *arrived,
    )
    return (
        document_query_grad,
        document_keys_grad,
        document_values_grad,
        question_query_grad,
        question_keys_grad,
        question_values_grad,
    )


def solution(mesh):
    return jax.shard_map(
        local,
        mesh=mesh,
        in_specs=(
            P(),
            P("ctx", None),
            P("ctx", "head"),
            P("ctx", "head"),
            P("ctx", "head"),
            P("ctx", "head"),
            P("ctx", "head"),
            P("ctx", "head"),
            P(("ctx", "head"), None),
            P(("ctx", "head"), None),
            P(("ctx", "head"), None),
            P(("ctx", "head"), None),
            P(("ctx", "head"), None),
            P(("ctx", "head"), None),
        ),
        out_specs=(
            P("ctx", "head"),
            P("ctx", "head"),
            P("ctx", "head"),
            P(("ctx", "head"), None),
            P(("ctx", "head"), None),
            P(("ctx", "head"), None),
        ),
        check_vma=False,
    )
```

time: 89.6 us -> 72.8 us (0.81)
  waiting for transfers between devices: 24.9 us -> 7.77 us
  local copies, waits for them, and re-layouts: 11.4 us -> 1.74 us
  Pallas kernels: 25.2 us -> 32.7 us
  starting transfers between devices: 24.6 us -> 27.7 us
    pallas_call x0 -> x4, Pallas kernels: none -> 20.9 us  [the longest x3 17.4 us: copying(): pl.pallas_call(body, out_shape=tuple((jax.ShapeDtypeStruct(s, t) for s, t...]
    pallas_call x7, Pallas kernels: 25.2 us -> 11.8 us  [call(): pl.pallas_call(body, out_shape=tuple((jax.ShapeDtypeStruct(s, t) for s, t...]
    ppermute x2, waiting for transfers between devices: 11.5 us -> 0.01 us  [other_chip(): return lax.ppermute(x, 'ctx', [(i, i ^ 2) for i in range(ctx_size)])]
    unnamed x42 -> x46, local copies, waits for them, and re-layouts: 10.8 us -> 1.73 us
    all_to_all x1, waiting for transfers between devices: 6.59 us -> 1.87 us  [local(): back = lax.all_to_all(back, 'head', 0, 0, tiled=True)]
    ppermute x6, starting transfers between devices: 8.17 us -> 9.72 us  [along_z(): lax.ppermute(x, 'ctx', [(i, (i + 4 * d) % ctx_size) for i in range(ctx_si...]
    ppermute x6, waiting for transfers between devices: 6.84 us -> 5.48 us  [along_z(): lax.ppermute(x, 'ctx', [(i, (i + 4 * d) % ctx_size) for i in range(ctx_si...]
    all_to_all x1, starting transfers between devices: 6.61 us -> 7.86 us  [local(): back = lax.all_to_all(back, 'head', 0, 0, tiled=True)]
  transfers between devices with their start and end apart: 15 -> 15, of which waited for: 5 -> 5; matrix products, arithmetic and copies ran while one was open for 1% -> 1% of each run, Pallas kernels for 21% -> 33%
where the time goes in v2:
time: 72.8 us; the launch traced here: 72.3 us
  Pallas kernels  32.7 us (45%)
  starting transfers between devices  27.7 us (38%)
  waiting for transfers between devices  7.77 us (11%)
  local copies, waits for them, and re-layouts  1.74 us (2%)
  other arithmetic  1.41 us (2%)
  between operations  0.96 us (1%)
    pallas_call x3, Pallas kernels, copying(): pl.pallas_call(body, out_shape=tuple((jax.ShapeDtypeStruct(s, t) for s, t...  17.4 us
    pallas_call x7, Pallas kernels, call(): pl.pallas_call(body, out_shape=tuple((jax.ShapeDtypeStruct(s, t) for s, t...  11.8 us
    ppermute x6, starting transfers between devices, along_z(): lax.ppermute(x, 'ctx', [(i, (i + 4 * d) % ctx_size) for i in range(ctx_si...  9.72 us
    all_to_all x1, starting transfers between devices, local(): back = lax.all_to_all(back, 'head', 0, 0, tiled=True)  7.86 us
    all_to_all x1, starting transfers between devices, local(): lax.all_to_all(payload, 'head', 0, 0, tiled=True).reshape(groups * each, -1)  6.65 us
    ppermute x6, waiting for transfers between devices, along_z(): lax.ppermute(x, 'ctx', [(i, (i + 4 * d) % ctx_size) for i in range(ctx_si...  5.48 us
    pallas_call x1, Pallas kernels, local(): pl.pallas_call(functools.partial(stats_kernel, heads, groups, total_doc),...  3.48 us
    ppermute x2, starting transfers between devices, other_chip(): return lax.ppermute(x, 'ctx', [(i, i ^ 2) for i in range(ctx_size)])  1.9 us
  transfers between devices with their start and end apart: 15, of which 5 were waited for; matrix products, arithmetic and copies ran while one was open for 1% of the time, Pallas kernels for 33%

profile of v2, /device:TPU:0, one launch (start us, length us, event | category | flops | bytes accessed | tf_op | source)
XLA Modules:
  0.0 72.3 jit_solution(256436064657983511)
XLA Ops:
  0.6 0.8 %pad_maximum_fusion = bf16[256,128]{1,0:T(8,128)(2,1)S(1)} fusion(bf16[128,128]{1,0:T(8,128)(2,1)} %param.18, bf16[128,128]{1,0:T(8,128)(2,1)} %param.17), kind=kLoop, calls=%fused_computation | loop fusion | flops 131072 | bytes 131072 | tf_op jit(solution)/shard_map/concatenate | solution.py:390
  1.5 1.6 %collective-permute-start = (bf16[256,128]{1,0:T(8,128)(2,1)S(1)}, bf16[256,128]{1,0:T(8,128)(2,1)S(1)}, u32[]{:S(2)}, u32[]{:S(2)}) collective-permute-start(bf16[256,128]{1,0:T(8,128)(2,1)S(1)} %pad_maximum_fusion), channel_id=1, source_target_pairs={{0,16},{8,24},{16,0},{24,8},{32,48},{40,56},{48,32},{56,40},{64,80... | collective-permute-start | bytes 196616 | tf_op jit(solution)/shard_map/ppermute | solution.py:385
  3.6 3.5 %shard_map.183.stats_ref = bf16[8,16,128]{2,1,0:T(8,128)(2,1)} custom-call(s32[1,2]{1,0:T(1,128)} %len_ref.3, s32[2]{0:T(128)} %pad_add_fusion.me_ref, bf16[16,12288]{1,0:T(8,128)(2,1)} %o_ref.1, bf16[16,12288]{1,0:T(8,128)(2,1)} %do_ref.3, f32[16,96]{1,0:T(8,128)} %ex_ref.1), custom_call_target="tpu_custom_call" | custom-call | flops 3300000000 | tf_op jit(solution)/shard_map/pallas_call | solution.py:407
  7.2 2.0 %collective-permute-start.2 = (bf16[512,128]{1,0:T(8,128)(2,1)S(1)}, bf16[512,128]{1,0:T(8,128)(2,1)S(1)}, u32[]{:S(2)}, u32[]{:S(2)}) collective-permute-start(bf16[512,128]{1,0:T(8,128)(2,1)S(1)} %constant_dynamic-update-slice_fusion.refs_0_), channel_id=1, source_target_pairs={{0,32},{8,40},{16,48},{24,56},{32,64},{40,72},{48,80},{56,88},{64,... | collective-permute-start | bytes 393224 | tf_op jit(solution)/shard_map/ppermute | solution.py:388
  9.2 3.6 %collective-permute-start.4 = (bf16[512,128]{1,0:T(8,128)(2,1)S(1)}, bf16[512,128]{1,0:T(8,128)(2,1)S(1)}, u32[]{:S(2)}, u32[]{:S(2)}) collective-permute-start(bf16[512,128]{1,0:T(8,128)(2,1)S(1)} %constant_dynamic-update-slice_fusion.refs_0_), channel_id=1, source_target_pairs={{0,64},{8,72},{16,80},{24,88},{32,96},{40,104},{48,112},{56,120},{... | collective-permute-start | bytes 393224 | tf_op jit(solution)/shard_map/ppermute | solution.py:388
  12.8 1.0 %collective-permute-start.6 = (bf16[512,128]{1,0:T(8,128)(2,1)S(1)}, bf16[512,128]{1,0:T(8,128)(2,1)S(1)}, u32[]{:S(2)}, u32[]{:S(2)}) collective-permute-start(bf16[512,128]{1,0:T(8,128)(2,1)S(1)} %constant_dynamic-update-slice_fusion.refs_0_), channel_id=1, source_target_pairs={{0,96},{8,104},{16,112},{24,120},{32,0},{40,8},{48,16},{56,24},{64... | collective-permute-start | bytes 393224 | tf_op jit(solution)/shard_map/ppermute | solution.py:388
  13.8 2.3 %shard_map.184 = bf16[8,16,3456]{2,1,0:T(8,128)(2,1)} custom-call(bf16[8,16,128]{2,1,0:T(8,128)(2,1)} %shard_map.183.stats_ref, bf16[16,12288]{1,0:T(8,128)(2,1)} %q_ref.1, bf16[16,12288]{1,0:T(8,128)(2,1)} %do_ref.3, bf16[16,1024]{1,0:T(8,128)(2,1)} %k_ref.1, bf16[16,1024]{1,0:T(8,128)(2,1)} %v_ref.1), custom_call_target="tpu_custom_call" | custom-call | flops 4400000000 | tf_op jit(solution)/shard_map/pallas_call | solution.py:395
  16.1 6.6 %all-to-all-start = ((bf16[8,16,3456]{2,1,0:T(8,128)(2,1)}), bf16[8,16,3456]{2,1,0:T(8,128)(2,1)S(1)}, u32[]{:S(2)}, u32[]{:S(2)}) async-start(bf16[8,16,3456]{2,1,0:T(8,128)(2,1)} %shard_map.184), calls=%async_computation | async-start | bytes 1769472 | tf_op jit(solution)/shard_map/all_to_all | solution.py:426
  24.1 7.8 %shard_map.181 = (bf16[1536,128]{1,0:T(8,128)(2,1)}, bf16[1536,128]{1,0:T(8,128)(2,1)}, f32[1,1536]{1,0:T(1,128)}, f32[1,1536]{1,0:T(1,128)}, f32[128,1536]{1,0:...) custom-call(s32[32]{0:T(128)} %order_ref.3, s32[2]{0:T(128)} %pad_add_fusion.me_ref, bf16[512,128]{1,0:T(8,128)(2,1)} %copy-done, ...), custom_call_target="tpu_custom_call" | custom-call | flops 6600000000 | tf_op jit(solution)/shard_map/pallas_call | solution.py:395
  32.0 0.6 copy-done.8
  32.8 7.3 %shard_map.182 = (bf16[128,1536]{1,0:T(8,128)(2,1)}, f32[4,256,256]{2,1,0:T(8,128)}) custom-call(s32[32]{0:T(128)} %order_ref.3, s32[2]{0:T(128)} %pad_add_fusion.me_ref, bf16[512,128]{1,0:T(8,128)(2,1)} %copy-done.8, bf16[512,128]{1,0:T(8,128)(2,1)} %copy-done.10, bf16[512,128]{1,0:T(8,128)(2,1)} %copy-done.12, bf16[512,128]{1,0:T(8,128)(2,1)} %copy-done.14, ...), custom_call_target="tpu_custom_call" | custom-call | flops 6600000000 | tf_op jit(solution)/shard_map/pallas_call | solution.py:395
  40.1 0.6 copy-done.16
  40.8 1.5 %shard_map.185 = (bf16[1536,128]{1,0:T(8,128)(2,1)S(1)}, bf16[1536,128]{1,0:T(8,128)(2,1)S(1)}, f32[1,1536]{1,0:T(1,128)S(1)}, f32[1,1536]{1,0:T(1,128)S(1)}, bf...) custom-call(s32[1,2]{1,0:T(1,128)S(1)} %copy-done.16, bf16[128,3456]{1,0:T(8,128)(2,1)S(1)} %bitcast.4), custom_call_target="tpu_custom_call" | custom-call | flops 1650000000 | tf_op jit(solution)/shard_map/pallas_call | solution.py:49
  42.3 4.2 %shard_map.186 = (bf16[4,256,256]{2,1,0:T(8,128)(2,1)S(1)}, f32[128,1536]{1,0:T(8,128)S(1)}) custom-call(bf16[1536,128]{1,0:T(8,128)(2,1)S(1)} %get-tuple-element.44.qs_ref, bf16[1536,128]{1,0:T(8,128)(2,1)S(1)} %get-tuple-element.45.dos_ref, f32[1,1536]{1,0:T(1,128)S(1)} %get-tuple-element.46.lse_ref, f32[1,1536]{1,0:T(1,128)S(1)} %get-tuple-element.47.delta_ref, ...), custom_call_target="tpu_custom_call" | custom-call | flops 4840000000 | tf_op jit(solution)/shard_map/pallas_call | solution.py:49
  47.0 1.1 %shard_map.187 = (f32[2,128,256]{2,1,0:T(8,128)S(1)}, f32[128,1536]{1,0:T(8,128)S(1)}) custom-call(bf16[1536,128]{1,0:T(8,128)(2,1)S(1)} %get-tuple-element.44.qs_ref, bf16[1536,128]{1,0:T(8,128)(2,1)S(1)} %get-tuple-element.45.dos_ref, f32[1,1536]{1,0:T(1,128)S(1)} %get-tuple-element.46.lse_ref, f32[1,1536]{1,0:T(1,128)S(1)} %get-tuple-element.47.delta_ref, ...), custom_call_target="tpu_custom_call" | custom-call | flops 1650000000 | tf_op jit(solution)/shard_map/pallas_call | solution.py:49
  48.5 2.1 %shard_map.188 = (bf16[4,128,256]{2,1,0:T(8,128)(2,1)S(1)}, f32[128,1536]{1,0:T(8,128)S(1)}) custom-call(bf16[1536,128]{1,0:T(8,128)(2,1)S(1)} %get-tuple-element.44.qs_ref, bf16[1536,128]{1,0:T(8,128)(2,1)S(1)} %get-tuple-element.45.dos_ref, f32[1,1536]{1,0:T(1,128)S(1)} %get-tuple-element.46.lse_ref, f32[1,1536]{1,0:T(1,128)S(1)} %get-tuple-element.47.delta_ref, ...), custom_call_target="tpu_custom_call" | custom-call | flops 2420000000 | tf_op jit(solution)/shard_map/pallas_call | solution.py:49
  50.9 2.0 %shard_map.189 = (f32[2,128,256]{2,1,0:T(8,128)S(1)}, bf16[8,16,1792]{2,1,0:T(8,128)(2,1)}) custom-call(bf16[1536,128]{1,0:T(8,128)(2,1)S(1)} %get-tuple-element.44.qs_ref, bf16[1536,128]{1,0:T(8,128)(2,1)S(1)} %get-tuple-element.45.dos_ref, f32[1,1536]{1,0:T(1,128)S(1)} %get-tuple-element.46.lse_ref, f32[1,1536]{1,0:T(1,128)S(1)} %get-tuple-element.47.delta_ref, ...), custom_call_target="tpu_custom_call" | custom-call | flops 2200000000 | tf_op jit(solution)/shard_map/pallas_call | solution.py:49
  52.9 7.9 %all-to-all-start.1 = ((bf16[8,16,1792]{2,1,0:T(8,128)(2,1)}), bf16[8,16,1792]{2,1,0:T(8,128)(2,1)S(1)}, u32[]{:S(2)}, u32[]{:S(2)}) async-start(bf16[8,16,1792]{2,1,0:T(8,128)(2,1)} %get-tuple-element.56), calls=%async_computation.1 | async-start | bytes 917504 | tf_op jit(solution)/shard_map/all_to_all | solution.py:472
  61.0 3.1 %collective-permute-start.11 = (bf16[128,256]{1,0:T(8,128)(2,1)S(1)}, bf16[128,256]{1,0:T(8,128)(2,1)S(1)}, u32[]{:S(2)}, u32[]{:S(2)}) collective-permute-start(bf16[128,256]{1,0:T(8,128)(2,1)S(1)} %get-tuple-element.63), channel_id=1, source_target_pairs={{0,64},{8,72},{16,80},{24,88},{32,96},{40,104},{48,112},{56,120},{... | collective-permute-start | bytes 196616 | tf_op jit(solution)/shard_map/ppermute | solution.py:388
  64.1 1.4 %collective-permute-done.10.refs_0_ = bf16[128,256]{1,0:T(8,128)(2,1)S(1)} collective-permute-done((bf16[128,256]{1,0:T(8,128)(2,1)S(1)}, bf16[128,256]{1,0:T(8,128)(2,1)S(1)}, u32[]{:S(2)}, u32[]{:S(2)}) %collective-permute-start.10) | collective-permute-done | bytes 65568 | tf_op jit(solution)/shard_map/ppermute | solution.py:388
  65.5 1.4 %collective-permute-done.11.refs_1_ = bf16[128,256]{1,0:T(8,128)(2,1)S(1)} collective-permute-done((bf16[128,256]{1,0:T(8,128)(2,1)S(1)}, bf16[128,256]{1,0:T(8,128)(2,1)S(1)}, u32[]{:S(2)}, u32[]{:S(2)}) %collective-permute-start.11) | collective-permute-done | bytes 65568 | tf_op jit(solution)/shard_map/ppermute | solution.py:388
  66.9 2.7 %collective-permute-done.12.refs_2_ = bf16[128,256]{1,0:T(8,128)(2,1)S(1)} collective-permute-done((bf16[128,256]{1,0:T(8,128)(2,1)S(1)}, bf16[128,256]{1,0:T(8,128)(2,1)S(1)}, u32[]{:S(2)}, u32[]{:S(2)}) %collective-permute-start.12) | collective-permute-done | bytes 65568 | tf_op jit(solution)/shard_map/ppermute | solution.py:388
  69.6 1.9 %all-to-all-done.1.back_ref = bf16[8,16,1792]{2,1,0:T(8,128)(2,1)S(1)} async-done(((bf16[8,16,1792]{2,1,0:T(8,128)(2,1)}), bf16[8,16,1792]{2,1,0:T(8,128)(2,1)S(1)}, u32[]{:S(2)}, u32[]{:S(2)}) %all-to-all-start.1) | async-done | bytes 458784 | tf_op jit(solution)/shard_map/all_to_all | solution.py:472
  71.4 0.8 %shard_map.191 = (bf16[16,12288]{1,0:T(8,128)(2,1)}, bf16[16,1024]{1,0:T(8,128)(2,1)}, bf16[16,1024]{1,0:T(8,128)(2,1)}, bf16[128,128]{1,0:T(8,128)(2,1)}, bf16[128,128]{1,0:T(8,128)(2,1)}) custom-call(bf16[8,16,1792]{2,1,0:T(8,128)(2,1)S(1)} %all-to-all-done.1.back_ref, f32[128,256]{1,0:T(8,128)S(1)} %get-tuple-element.61.keep_ref, ...), custom_call_target="tpu_custom_call" | custom-call | flops 880000000 | tf_op jit(solution)/shard_map/pallas_call | solution.py:49
  (66 shorter events, 3.6 us)
Async XLA Ops:
  0.6 2.4 %copy-start.20 = (bf16[128,128]{1,0:T(8,128)(2,1)S(1)}, bf16[128,128]{1,0:T(8,128)(2,1)}, u32[]{:S(2)}) copy-start(bf16[128,128]{1,0:T(8,128)(2,1)} %param.17) | copy-start | bytes 98308
  1.5 5.7 %collective-permute-start = (bf16[256,128]{1,0:T(8,128)(2,1)S(1)}, bf16[256,128]{1,0:T(8,128)(2,1)S(1)}, u32[]{:S(2)}, u32[]{:S(2)}) collective-permute-start(bf16[256,128]{1,0:T(8,128)(2,1)S(1)} %pad_maximum_fusion), channel_id=1, source_target_pairs={{0,16},{8,24},{16,0},{24,8},{32,48},{40,56},{48,32},{56,40},{64,80... | collective-permute-start | bytes 196616 | tf_op jit(solution)/shard_map/ppermute | solution.py:385
  3.6 3.5 %copy-start.21 = (bf16[128,128]{1,0:T(8,128)(2,1)S(1)}, bf16[128,128]{1,0:T(8,128)(2,1)}, u32[]{:S(2)}) copy-start(bf16[128,128]{1,0:T(8,128)(2,1)} %param.18) | copy-start | bytes 98308
  7.2 15.5 %copy-start = (bf16[512,128]{1,0:T(8,128)(2,1)}, bf16[512,128]{1,0:T(8,128)(2,1)S(1)}, u32[]{:S(2)}) copy-start(bf16[512,128]{1,0:T(8,128)(2,1)S(1)} %constant_dynamic-update-slice_fusion.refs_0_) | copy-start | bytes 393220
  7.2 15.6 %collective-permute-start.2 = (bf16[512,128]{1,0:T(8,128)(2,1)S(1)}, bf16[512,128]{1,0:T(8,128)(2,1)S(1)}, u32[]{:S(2)}, u32[]{:S(2)}) collective-permute-start(bf16[512,128]{1,0:T(8,128)(2,1)S(1)} %constant_dynamic-update-slice_fusion.refs_0_), channel_id=1, source_target_pairs={{0,32},{8,40},{16,48},{24,56},{32,64},{40,72},{48,80},{56,88},{64,... | collective-permute-start | bytes 393224 | tf_op jit(solution)/shard_map/ppermute | solution.py:388
  9.2 14.1 %collective-permute-start.4 = (bf16[512,128]{1,0:T(8,128)(2,1)S(1)}, bf16[512,128]{1,0:T(8,128)(2,1)S(1)}, u32[]{:S(2)}, u32[]{:S(2)}) collective-permute-start(bf16[512,128]{1,0:T(8,128)(2,1)S(1)} %constant_dynamic-update-slice_fusion.refs_0_), channel_id=1, source_target_pairs={{0,64},{8,72},{16,80},{24,88},{32,96},{40,104},{48,112},{56,120},{... | collective-permute-start | bytes 393224 | tf_op jit(solution)/shard_map/ppermute | solution.py:388
  12.8 10.7 %collective-permute-start.6 = (bf16[512,128]{1,0:T(8,128)(2,1)S(1)}, bf16[512,128]{1,0:T(8,128)(2,1)S(1)}, u32[]{:S(2)}, u32[]{:S(2)}) collective-permute-start(bf16[512,128]{1,0:T(8,128)(2,1)S(1)} %constant_dynamic-update-slice_fusion.refs_0_), channel_id=1, source_target_pairs={{0,96},{8,104},{16,112},{24,120},{32,0},{40,8},{48,16},{56,24},{64... | collective-permute-start | bytes 393224 | tf_op jit(solution)/shard_map/ppermute | solution.py:388
  16.1 24.0 %all-to-all-start = ((bf16[8,16,3456]{2,1,0:T(8,128)(2,1)}), bf16[8,16,3456]{2,1,0:T(8,128)(2,1)S(1)}, u32[]{:S(2)}, u32[]{:S(2)}) async-start(bf16[8,16,3456]{2,1,0:T(8,128)(2,1)} %shard_map.184), calls=%async_computation | async-start | bytes 1769472 | tf_op jit(solution)/shard_map/all_to_all | solution.py:426
  22.7 9.2 %collective-permute-start.1 = (bf16[512,128]{1,0:T(8,128)(2,1)S(1)}, bf16[512,128]{1,0:T(8,128)(2,1)S(1)}, u32[]{:S(2)}, u32[]{:S(2)}) collective-permute-start(bf16[512,128]{1,0:T(8,128)(2,1)S(1)} %constant_dynamic-update-slice_fusion.refs_0_), channel_id=1, source_target_pairs={{0,8},{8,0},{16,24},{24,16},{32,40},{40,32},{48,56},{56,48},{64,72... | collective-permute-start | bytes 393224 | tf_op jit(solution)/shard_map/ppermute | solution.py:382
  22.8 9.1 %collective-permute-start.3 = (bf16[512,128]{1,0:T(8,128)(2,1)S(1)}, bf16[512,128]{1,0:T(8,128)(2,1)S(1)}, u32[]{:S(2)}, u32[]{:S(2)}) collective-permute-start(bf16[512,128]{1,0:T(8,128)(2,1)S(1)} %collective-permute-done.2.refs_1_), channel_id=1, source_target_pairs={{0,8},{8,0},{16,24},{24,16},{32,40},{40,32},{48,56},{56,48},{64,72... | collective-permute-start | bytes 393224 | tf_op jit(solution)/shard_map/ppermute | solution.py:382
  23.3 8.7 %collective-permute-start.5 = (bf16[512,128]{1,0:T(8,128)(2,1)S(1)}, bf16[512,128]{1,0:T(8,128)(2,1)S(1)}, u32[]{:S(2)}, u32[]{:S(2)}) collective-permute-start(bf16[512,128]{1,0:T(8,128)(2,1)S(1)} %collective-permute-done.4.refs_2_.refs_0_), channel_id=1, source_target_pairs={{0,8},{8,0},{16,24},{24,16},{32,40},{40,32},{48,56},{56,48},{64,72... | collective-permute-start | bytes 393224 | tf_op jit(solution)/shard_map/ppermute | solution.py:382
  23.4 8.6 %collective-permute-start.7 = (bf16[512,128]{1,0:T(8,128)(2,1)S(1)}, bf16[512,128]{1,0:T(8,128)(2,1)S(1)}, u32[]{:S(2)}, u32[]{:S(2)}) collective-permute-start(bf16[512,128]{1,0:T(8,128)(2,1)S(1)} %collective-permute-done.6.refs_3_.refs_1_), channel_id=1, source_target_pairs={{0,8},{8,0},{16,24},{24,16},{32,40},{40,32},{48,56},{56,48},{64,72... | collective-permute-start | bytes 393224 | tf_op jit(solution)/shard_map/ppermute | solution.py:382
  42.3 4.7 %copy-start.1 = (bf16[512,128]{1,0:T(8,128)(2,1)S(1)}, bf16[512,128]{1,0:T(8,128)(2,1)}, u32[]{:S(2)}) copy-start(bf16[512,128]{1,0:T(8,128)(2,1)} %copy-done) | copy-start | bytes 393220
  42.3 4.7 %copy-start.7 = (bf16[512,128]{1,0:T(8,128)(2,1)S(1)}, bf16[512,128]{1,0:T(8,128)(2,1)}, u32[]{:S(2)}) copy-start(bf16[512,128]{1,0:T(8,128)(2,1)} %copy-done.6) | copy-start | bytes 393220
  46.5 2.0 %collective-permute-start.8 = (bf16[4,256,256]{2,1,0:T(8,128)(2,1)S(1)}, bf16[4,256,256]{2,1,0:T(8,128)(2,1)S(1)}, u32[]{:S(2)}, u32[]{:S(2)}) collective-permute-start(bf16[4,256,256]{2,1,0:T(8,128)(2,1)S(1)} %get-tuple-element.52), channel_id=1, source_target_pairs={{0,8},{8,0},{16,24},{24,16},{32,40},{40,32},{48,56},{56,48},{64,72... | collective-permute-start | bytes 1572872 | tf_op jit(solution)/shard_map/ppermute | solution.py:382
  47.0 1.5 %copy-start.3 = (bf16[512,128]{1,0:T(8,128)(2,1)S(1)}, bf16[512,128]{1,0:T(8,128)(2,1)}, u32[]{:S(2)}) copy-start(bf16[512,128]{1,0:T(8,128)(2,1)} %copy-done.2) | copy-start | bytes 393220
  47.0 1.5 %copy-start.5 = (bf16[512,128]{1,0:T(8,128)(2,1)S(1)}, bf16[512,128]{1,0:T(8,128)(2,1)}, u32[]{:S(2)}) copy-start(bf16[512,128]{1,0:T(8,128)(2,1)} %copy-done.4) | copy-start | bytes 393220
  47.0 1.5 %copy-start.17 = (f32[4,128,256]{2,1,0:T(8,128)S(1)}, f32[4,128,256]{2,1,0:T(8,128)}, u32[]{:S(2)}) copy-start(f32[4,128,256]{2,1,0:T(8,128)} %get-tuple-element.53.refs_4_) | copy-start | bytes 1572868
  50.6 10.2 %collective-permute-start.9 = (bf16[4,128,256]{2,1,0:T(8,128)(2,1)S(1)}, bf16[4,128,256]{2,1,0:T(8,128)(2,1)S(1)}, u32[]{:S(2)}, u32[]{:S(2)}) collective-permute-start(bf16[4,128,256]{2,1,0:T(8,128)(2,1)S(1)} %get-tuple-element.60), channel_id=1, source_target_pairs={{0,16},{8,24},{16,0},{24,8},{32,48},{40,56},{48,32},{56,40},{64,80... | collective-permute-start | bytes 786440 | tf_op jit(solution)/shard_map/ppermute | solution.py:385
  52.9 7.9 %copy-start.19 = (f32[4,128,256]{2,1,0:T(8,128)S(1)}, f32[4,128,256]{2,1,0:T(8,128)}, u32[]{:S(2)}) copy-start(f32[4,128,256]{2,1,0:T(8,128)} %get-tuple-element.59.doc_ref) | copy-start | bytes 1572868
  52.9 18.5 %all-to-all-start.1 = ((bf16[8,16,1792]{2,1,0:T(8,128)(2,1)}), bf16[8,16,1792]{2,1,0:T(8,128)(2,1)S(1)}, u32[]{:S(2)}, u32[]{:S(2)}) async-start(bf16[8,16,1792]{2,1,0:T(8,128)(2,1)} %get-tuple-element.56), calls=%async_computation.1 | async-start | bytes 917504 | tf_op jit(solution)/shard_map/all_to_all | solution.py:472
  60.9 4.6 %collective-permute-start.10 = (bf16[128,256]{1,0:T(8,128)(2,1)S(1)}, bf16[128,256]{1,0:T(8,128)(2,1)S(1)}, u32[]{:S(2)}, u32[]{:S(2)}) collective-permute-start(bf16[128,256]{1,0:T(8,128)(2,1)S(1)} %get-tuple-element.62), channel_id=1, source_target_pairs={{0,96},{8,104},{16,112},{24,120},{32,0},{40,8},{48,16},{56,24},{64... | collective-permute-start | bytes 196616 | tf_op jit(solution)/shard_map/ppermute | solution.py:388
  61.0 5.8 %collective-permute-start.11 = (bf16[128,256]{1,0:T(8,128)(2,1)S(1)}, bf16[128,256]{1,0:T(8,128)(2,1)S(1)}, u32[]{:S(2)}, u32[]{:S(2)}) collective-permute-start(bf16[128,256]{1,0:T(8,128)(2,1)S(1)} %get-tuple-element.63), channel_id=1, source_target_pairs={{0,64},{8,72},{16,80},{24,88},{32,96},{40,104},{48,112},{56,120},{... | collective-permute-start | bytes 196616 | tf_op jit(solution)/shard_map/ppermute | solution.py:388
  64.1 5.5 %collective-permute-start.12 = (bf16[128,256]{1,0:T(8,128)(2,1)S(1)}, bf16[128,256]{1,0:T(8,128)(2,1)S(1)}, u32[]{:S(2)}, u32[]{:S(2)}) collective-permute-start(bf16[128,256]{1,0:T(8,128)(2,1)S(1)} %get-tuple-element.64), channel_id=1, source_target_pairs={{0,32},{8,40},{16,48},{24,56},{32,64},{40,72},{48,80},{56,88},{64,... | collective-permute-start | bytes 196616 | tf_op jit(solution)/shard_map/ppermute | solution.py:388
  (13 other events, 13.4 us)

commit v3 on v2

--- a/solution.py
+++ b/solution.py
@@ -60,7 +60,12 @@
 def pair_block(qs_ref, dos_ref, keys, values, lse, delta, mask):
     scores = dot(keys, qs_ref[...], 1, 1)
     dprob = dot(values, dos_ref[...], 1, 1)
-    prob = jnp.exp2(scores * (SCALE * LOG2E) - lse)
+    scores = scores * (SCALE * LOG2E)
+    if isinstance(lse, list):
+        step = scores.shape[0] // len(lse)
+        prob = jnp.concatenate([jnp.exp2(scores[n * step : (n + 1) * step] - row) for n, row in enumerate(lse)], axis=0)
+    else:
+        prob = jnp.exp2(scores - lse)
     if mask is not None:
         prob = jnp.where(mask, prob, 0.0)
     dscore = (prob * (dprob - delta)).astype(BF)
@@ -76,6 +81,17 @@
     return keys, values
 
 
+def head_parts(out, grad):
+    product = out.astype(F32) * grad.astype(F32)
+    high = product.astype(BF)
+    return high, (product - high.astype(F32)).astype(BF)
+
+
+def head_ones(shape, axis):
+    position = lax.broadcasted_iota(jnp.int32, shape, 1 - axis) // D
+    return jnp.where(position == lax.broadcasted_iota(jnp.int32, shape, axis), 1.0, 0.0).astype(BF)
+
+
 def stack_heads(source, target, heads, first):
     for j in range(heads):
         at = first + j * D
@@ -88,58 +104,64 @@
 
 
 def unstack_query_grad(dq, heads):
-    return [(dq[:, j * D : (j + 1) * D].T * SCALE).astype(BF) for j in range(heads)]
-
-
-def stats_kernel(heads, groups, total, len_ref, me_ref, o_ref, do_ref, ex_ref, packed, out, grad, buf, sems):
+    dq = (dq * SCALE).astype(BF)
+    return [dq[:, j * D : (j + 1) * D].T for j in range(heads)]
+
+
+def pack_kernel(heads, groups, total, len_ref, do_ref, o_ref, q_ref, k_ref, v_ref, ex_ref, dk_ref, dv_ref, pay_ref, kv_ref, *refs):
+    grad, out, query, keys, values, buf, packed, high, low, sems = refs
     rows = out.shape[0]
     wide = heads * D
-    loads = [pltpu.make_async_copy(source, to, sems.at[n]) for n, (source, to) in enumerate(((o_ref, out), (do_ref, grad), (ex_ref, buf)))]
+    pairs = (
+        (do_ref, grad), (o_ref, out), (q_ref, query), (k_ref, keys), (v_ref, values), (ex_ref, buf),
+        (dk_ref, kv_ref.at[pl.ds(0, D)]), (dv_ref, kv_ref.at[pl.ds(D, D)]),
+    )
+    loads = [pltpu.make_async_copy(source, to, sems.at[n]) for n, (source, to) in enumerate(pairs)]
     for load in loads:
         load.start()
-    row = me_ref[1] * rows + sublanes((rows, D))
+    sends = []
+
+    def send(source, to, size):
+        for g in range(groups):
+            part = pay_ref.at[g, :, pl.ds(to, size)]
+            sends.append(pltpu.make_async_copy(source.at[:, pl.ds(g * size, size)], part, sems.at[len(pairs) + len(sends)]))
+            sends[-1].start()
+
+    row = lax.axis_index("head") * rows + sublanes((rows, D))
     within = jnp.where(row < len_ref[0, 0], row, row - len_ref[0, 0])
     log_count = jnp.log((within + 1 + total).astype(F32))
-    for load in loads:
-        load.wait()
+    loads[0].wait()
+    send(grad, wide, wide)
+    loads[2].wait()
+    send(query, 0, wide)
+    loads[3].wait()
+    send(keys, 2 * wide, D)
+    loads[4].wait()
+    send(values, 2 * wide + D, D)
+    loads[1].wait()
+    for g in range(groups):
+        cut, at = slice(g * wide, (g + 1) * wide), slice(g * rows, (g + 1) * rows)
+        high[at, :], low[at, :] = head_parts(out[:, cut], grad[:, cut])
+    ones = head_ones((wide, D), 1)
+    deltas = dot(high[...], ones, 1, 0) + dot(low[...], ones, 1, 0)
+    loads[5].wait()
     lse = (buf[...] + log_count[:, : heads * groups]) * LOG2E
     lse = jnp.concatenate([lse, jnp.zeros((rows, D - heads * groups), F32)], axis=1)
     lane = lanes((rows, D))
     for g in range(groups):
-        delta = jnp.zeros((rows, D), F32)
-        for j in range(heads):
-            cut = slice(g * wide + j * D, g * wide + (j + 1) * D)
-            product = out[:, cut].astype(F32) * grad[:, cut].astype(F32)
-            delta = jnp.where(lane == j, jnp.sum(product, axis=1, keepdims=True), delta)
         mine = lse if g == 0 else pltpu.roll(lse, D - heads * g, 1)
         mine = jnp.where(lane < heads, mine, 0.0)
         stats = jnp.zeros((rows, D), F32)
-        for n, value in enumerate((mine, delta)):
+        for n, value in enumerate((mine, deltas[g * rows : (g + 1) * rows])):
             for m in range(3):
                 part = value.astype(BF).astype(F32)
                 value = value - part
                 at = (3 * n + m) * 16
                 stats = stats + (pltpu.roll(part, at, 1) if at else part)
-        packed[g] = stats.astype(BF)
-
-
-def pack_kernel(heads, groups, stats_ref, q_ref, do_ref, k_ref, v_ref, pay_ref, stats, query, grad, keys, values, sems):
-    wide = heads * D
-    pairs = ((q_ref, query), (do_ref, grad), (k_ref, keys), (v_ref, values), (stats_ref, stats))
-    loads = [pltpu.make_async_copy(source, to, sems.at[n]) for n, (source, to) in enumerate(pairs)]
-    for load in loads:
-        load.start()
-    sends = []
-    for n, (source, to, size) in enumerate(((query, 0, wide), (grad, wide, wide), (keys, 2 * wide, D), (values, 2 * wide + D, D))):
-        loads[n].wait()
-        for g in range(groups):
-            part = pay_ref.at[g, :, pl.ds(to, size)]
-            sends.append(pltpu.make_async_copy(source.at[:, pl.ds(g * size, size)], part, sems.at[5 + n * groups + g]))
-            sends[-1].start()
-    loads[4].wait()
-    sends.append(pltpu.make_async_copy(stats, pay_ref.at[:, :, pl.ds(2 * wide + 2 * D, D)], sems.at[5 + 4 * groups]))
+        packed[g] = jnp.where(lane == 96, (row - within).astype(F32), stats).astype(BF)
+    sends.append(pltpu.make_async_copy(packed, pay_ref.at[:, :, pl.ds(2 * wide + 2 * D, D)], sems.at[len(pairs) + len(sends)]))
     sends[-1].start()
-    for copy in sends:
+    for copy in loads[6:] + sends:
         copy.wait()
 
 
@@ -155,74 +177,50 @@
     for b in range(2):
         kb = order_ref[2 * owner + b]
         bias = [jnp.where(kb <= order_ref[2 * me + a], 0.0, HIDDEN).astype(F32) for a in range(2)]
-        hide = jnp.where(lane_half, bias[1], bias[0])
-        parts.append(jnp.broadcast_to(lse + hide, (D // 2, lse.shape[1])))
-    return jnp.concatenate(parts, axis=0)
-
-
-def doc_kernel(core, heads, ctx_size, order_ref, me_ref, *refs):
-    kv_hbm, refs = refs[:4], refs[4:]
-    kv_refs, sems = refs[-2:]
+        parts.append(lse + jnp.where(lane_half, bias[1], bias[0]))
+    return parts
+
+
+def doc_kernel(core, heads, ctx_size, order_ref, *refs):
+    kv_refs, refs = refs[:4], refs[4:]
     if core == 0:
-        ins, state_hbm, (dq_hbm, near_hbm, own_hbm) = refs[:4], refs[4:8], refs[8:11]
-        bufs, state, (dq_ref, near_ref, own_ref) = refs[11:15], refs[15:19], refs[19:22]
-        q_ref, o_ref, do_ref, ex_ref = bufs
+        q_ref, o_ref, do_ref, ex_ref, *state, dq_ref, near_hbm, own_hbm, near_ref, own_ref, sems = refs
     else:
-        ins, (dq_hbm, far_hbm) = refs[:5], refs[5:7]
-        bufs, (dq_ref, far_ref) = refs[7:12], refs[12:14]
-        state = bufs[:4]
+        *state, dq_in, far_hbm, dq_hbm, far_ref, dq_ref, sems = refs
     qs_ref, dos_ref, lse_ref, delta_ref = state
-    loads = [pltpu.make_async_copy(source, to, sems.at[n]) for n, (source, to) in enumerate(zip(ins, bufs))]
-    pieces = [pltpu.make_async_copy(kv_hbm[n], kv_refs.at[n], sems.at[5 + n]) for n in range(4)]
-    for load in loads[:4] + pieces + loads[4:]:
-        load.start()
     stores = []
 
     def store(source, to):
-        stores.append(pltpu.make_async_copy(source, to, sems.at[9 + len(stores)]))
+        stores.append(pltpu.make_async_copy(source, to, sems.at[len(stores)]))
         stores[-1].start()
 
-    me = me_ref[0]
+    me = lax.axis_index("ctx")
     rows = heads * D
     lane = lax.rem(lanes((1, rows)), D)
     half = D // 2
     lane_half = lane >= half
     if core == 0:
-        loads[3].wait()
         one = lanes((1, D))
         pos = jnp.where(one < half, order_ref[2 * me] * half + one, order_ref[2 * me + 1] * half + one - half)
         spread_rows((ex_ref[...] + jnp.log((pos + 1).astype(F32))) * LOG2E, lse_ref, heads)
-        loads[0].wait()
         stack_heads(q_ref, qs_ref, heads, 0)
-        loads[2].wait()
         stack_heads(do_ref, dos_ref, heads, 0)
-        loads[1].wait()
-        at = lanes((D, D))
-        stats = jnp.zeros((D, D), F32)
-        for j in range(heads):
-            cut = slice(j * D, (j + 1) * D)
-            product = o_ref[:, cut].astype(F32) * do_ref[:, cut].astype(F32)
-            stats = jnp.where(at == j, jnp.sum(product, axis=1, keepdims=True), stats)
-        spread_rows(stats.T[:16], delta_ref, heads)
-        for source, to in zip(state, state_hbm):
-            store(source, to)
-    else:
-        for load in loads[:4]:
-            load.wait()
+        ones = head_ones((16, rows), 0)
+        high, low = head_parts(o_ref[...], do_ref[...])
+        spread_rows(dot(ones, high, 1, 1) + dot(ones, low, 1, 1), delta_ref, heads)
     lse = lse_ref[...]
     delta = delta_ref[...]
     total = None
     for depth in range(4):
         owners = doc_keys(order_ref, me, ctx_size, (core, depth))
-        shift = jnp.concatenate([doc_lse(order_ref, me, o, lse, lane_half) for o in owners], axis=0)
+        shift = [row for o in owners for row in doc_lse(order_ref, me, o, lse, lane_half)]
         mask = None
         if core == 0 and depth == 0:
             key = sublanes((2 * D, 1))
             key_pos = jnp.where(key < half, order_ref[2 * me] * half + key, order_ref[2 * me + 1] * half + key - half)
             row_pos = jnp.where(lane_half, order_ref[2 * me + 1] * half + lane - half, order_ref[2 * me] * half + lane)
             mask = jnp.where(key < D, key_pos, -1) <= row_pos
-        pieces[depth].wait()
-        dq, dk, dv = pair_block(qs_ref, dos_ref, *both(kv_refs.at[depth]), shift, delta, mask)
+        dq, dk, dv = pair_block(qs_ref, dos_ref, *both(kv_refs[depth]), shift, delta, mask)
         for side, grad in enumerate((dk, dv)):
             cut = slice(side * D, (side + 1) * D)
             if core == 0:
@@ -239,25 +237,28 @@
     if core == 0:
         dq_ref[...] = total
     else:
-        loads[4].wait()
-        for j, part in enumerate(unstack_query_grad(total + bufs[4][...], heads)):
-            dq_ref[:, j * D : (j + 1) * D] = part
-    store(dq_ref, dq_hbm)
+        dq_ref[...] = ((total + dq_in[...]) * SCALE).astype(BF)
+        store(dq_ref, dq_hbm)
     for copy in stores:
         copy.wait()
 
 
-def self_kernel(heads, len_ref, pay_ref, qs_ref, dos_ref, lse_ref, delta_ref, self_ref, dq_ref):
+def turn_kernel(heads, turned_ref, out_ref):
+    for j in range(heads):
+        out_ref[:, j * D : (j + 1) * D] = turned_ref[:, j * D : (j + 1) * D].T
+
+
+def self_kernel(heads, pay_ref, qs_ref, dos_ref, lse_ref, delta_ref, self_ref, dq_ref):
     wide = heads * D
     stack_heads(pay_ref, qs_ref, heads, 0)
     stack_heads(pay_ref, dos_ref, heads, wide)
     stats = pay_ref[:, 2 * wide + 2 * D :].astype(F32).T
     spread_rows(stats[:16] + stats[16:32] + stats[32:48], lse_ref, heads)
     spread_rows(stats[48:64] + stats[64:80] + stats[80:96], delta_ref, heads)
-    row = lax.rem(lanes((1, wide)), D)
+    row = lanes((1, D))
     key = sublanes((D, 1))
-    first = len_ref[0, 0]
-    mask = (key <= row) & ((key >= first) | (row < first))
+    seen = (key <= row) & (key >= stats[96:97].astype(jnp.int32))
+    mask = jnp.concatenate([seen] * heads, axis=1)
     keys = pay_ref[:, 2 * wide : 2 * wide + D]
     values = pay_ref[:, 2 * wide + D : 2 * wide + 2 * D]
     dq, dk, dv = pair_block(qs_ref, dos_ref, keys, values, lse_ref[...], delta_ref[...], mask)
@@ -375,7 +376,6 @@
     rows, each = document_query_matrix.shape[0], question_query_matrix.shape[0]
     total_doc = rows * ctx_size
     wide, stacked = heads * D, heads * rows
-    me = jnp.stack([lax.axis_index("ctx"), lax.axis_index("head")]).astype(jnp.int32)
     depth = ctx_size // 4
 
     def other_core(x):
@@ -387,42 +387,37 @@
     def along_z(x, d):
         return lax.ppermute(x, "ctx", [(i, (i + 4 * d) % ctx_size) for i in range(ctx_size)])
 
-    kv = jnp.concatenate([document_key_matrix, document_value_matrix], axis=0)
-    here = jnp.concatenate([kv, other_chip(kv)], axis=0)
+    chip = [other_chip(document_key_matrix), other_chip(document_value_matrix)]
+    asking = pltpu.VMEM((each, wide * groups), BF)
+    narrow = pltpu.VMEM((each, D * groups), BF)
+    both_parts = pltpu.VMEM((groups * each, wide), BF)
+    payload, kv = pl.pallas_call(
+        functools.partial(pack_kernel, heads, groups, total_doc),
+        out_shape=(
+            pltpu.HBM((groups, each, 2 * wide + 3 * D), BF),
+            jax.ShapeDtypeStruct((4 * rows, D), BF),
+        ),
+        in_specs=[smem()] + [hbm()] * 8,
+        out_specs=(hbm(), vmem()),
+        scratch_shapes=[asking, asking, asking, narrow, narrow, pltpu.VMEM((each, heads * groups), F32)]
+        + [pltpu.VMEM((groups, each, D), BF), both_parts, both_parts, pltpu.SemaphoreType.DMA((9 + 4 * groups,))],
+        compiler_params=SHARED,
+        cost_estimate=cost(5),
+    )(
+        question_lengths,
+        *[
+            pltpu.with_memory_space_constraint(x, pltpu.HBM)
+            for x in (
+                question_outgrad, question_output, question_query_matrix, question_key_matrix, question_value_matrix,
+                question_excess, document_key_matrix, document_value_matrix,
+            )
+        ],
+    )
+    here = kv
+    for n, part in enumerate(chip):
+        here = lax.dynamic_update_slice(here, part, ((2 + n) * rows, 0))
     mine = [here] + [along_z(here, d) for d in range(1, depth)]
     theirs = [other_core(piece) for piece in mine]
-    def copying(us, body, outs, n_smem, scratch, *args):
-        return pl.pallas_call(
-            body,
-            out_shape=tuple(jax.ShapeDtypeStruct(s, t) for s, t in outs),
-            in_specs=[smem()] * n_smem + [hbm()] * (len(args) - n_smem),
-            out_specs=(hbm(),) * len(outs),
-            scratch_shapes=scratch,
-            compiler_params=WHOLE,
-            cost_estimate=cost(us),
-        )(*args)
-
-    asking = pltpu.VMEM((each, wide * groups), BF)
-    parts = (groups, each, D)
-    stats = pl.pallas_call(
-        functools.partial(stats_kernel, heads, groups, total_doc),
-        out_shape=jax.ShapeDtypeStruct(parts, BF),
-        in_specs=[smem()] * 2 + [hbm()] * 3,
-        out_specs=vmem(),
-        scratch_shapes=[asking, asking, pltpu.VMEM((each, heads * groups), F32), pltpu.SemaphoreType.DMA((3,))],
-        compiler_params=WHOLE,
-        cost_estimate=cost(3),
-    )(question_lengths, me, question_output, question_outgrad, question_excess)
-    (payload,) = copying(
-        4,
-        functools.partial(pack_kernel, heads, groups),
-        [((groups, each, 2 * wide + 3 * D), BF)],
-        0,
-        [pltpu.VMEM(parts, BF), asking, asking]
-        + [pltpu.VMEM((each, D * groups), BF)] * 2
-        + [pltpu.SemaphoreType.DMA((6 + 4 * groups,))],
-        stats, question_query_matrix, question_outgrad, question_key_matrix, question_value_matrix,
-    )
     asked = lax.all_to_all(payload, "head", 0, 0, tiled=True).reshape(groups * each, -1)
 
     quarter = ((depth, rows, 2 * D), F32)
@@ -431,31 +426,30 @@
     query_sum = ((D, stacked), F32)
     flat = ((rows, wide), BF)
 
-    def held(*shapes):
-        return [pltpu.VMEM(*shape) for shape in shapes] + [pltpu.VMEM((depth, 4 * rows, D), BF), pltpu.SemaphoreType.DMA((24,))]
-
-    *doc_state, dq, near_doc, own_doc = copying(
-        6,
-        functools.partial(doc_kernel, 0, heads, ctx_size),
-        row_state + [query_sum, quarter, quarter],
-        2,
-        held(flat, flat, flat, ((heads, rows), F32), *row_state, query_sum, quarter, quarter),
-        block_order, me, *mine, document_query_matrix, document_output, document_outgrad, document_excess.T,
-    )
-    document_query_grad, far_doc = copying(
-        6,
-        functools.partial(doc_kernel, 1, heads, ctx_size),
-        [flat, double],
-        2,
-        held(*row_state, query_sum, flat, double),
-        block_order, me, *theirs, *doc_state, dq,
-    )
+    def document(core, outs, partial, *args):
+        return pl.pallas_call(
+            functools.partial(doc_kernel, core, heads, ctx_size),
+            out_shape=tuple(jax.ShapeDtypeStruct(*out) for out in outs) + tuple(pltpu.HBM(*out) for out in partial),
+            in_specs=[smem()] + [vmem()] * (len(args) - 1),
+            out_specs=(vmem(),) * len(outs) + (hbm(),) * len(partial),
+            scratch_shapes=[pltpu.VMEM(*out) for out in partial] + [pltpu.SemaphoreType.DMA((8,))],
+            compiler_params=SHARED,
+            cost_estimate=cost(6),
+        )(*args)
+
+    *doc_state, dq, near_doc, own_doc = document(
+        0,
+        row_state + [query_sum],
+        [quarter, quarter],
+        block_order, *mine, document_query_matrix, document_output, document_outgrad, document_excess.T,
+    )
+    far_doc, doc_turned = document(1, [], [double, ((D, stacked), BF)], block_order, *theirs, *doc_state, dq)
     *state, own_self, dq = call(
         1.5,
         functools.partial(self_kernel, heads),
         row_state + [((rows, 2 * D), BF), query_sum],
-        1,
-        question_lengths, asked,
+        0,
+        asked,
     )
     far, dq = call(4.4, far_kernel, [((depth, 2 * rows, 2 * D), BF), query_sum], 0, *state, dq, *theirs, far_doc)
     core_sum = other_core(far)
@@ -477,6 +471,7 @@
         0,
         low, high, own_doc, core_sum, chip_sum,
     )
+    (document_query_grad,) = call(2, functools.partial(turn_kernel, heads), [flat], 0, doc_turned)
     arrived = [along_z(send, depth - 1 - n) for n, send in enumerate(sends)]
     question_query_grad, question_keys_grad, question_values_grad, document_keys_grad, document_values_grad = call(
         0.8,

time: 72.8 us -> 64.8 us (0.89)
  Pallas kernels: 32.7 us -> 26.5 us
  other arithmetic: 1.41 us -> 0 us
    pallas_call x4 -> x3, Pallas kernels: 20.9 us -> 14.6 us  [the longest x2 11.1 us: document(): pl.pallas_call(functools.partial(doc_kernel, core, heads, ctx_size), out_...]
    ppermute x2 -> x3, starting transfers between devices: 1.9 us -> 3 us  [other_chip(): return lax.ppermute(x, 'ctx', [(i, i ^ 2) for i in range(ctx_size)])]
    all_to_all x1, starting transfers between devices: 7.86 us -> 6.86 us  [local(): back = lax.all_to_all(back, 'head', 0, 0, tiled=True)]
    ppermute x6, waiting for transfers between devices: 5.48 us -> 4.58 us  [along_z(): lax.ppermute(x, 'ctx', [(i, (i + 4 * d) % ctx_size) for i in range(ctx_si...]
    concatenate x1 -> x0, other arithmetic: 0.83 us -> none  [local(): kv = jnp.concatenate([document_key_matrix, document_value_matrix], axis=0)]
    all_to_all x1, waiting for transfers between devices: 0.01 us -> 0.81 us  [local(): lax.all_to_all(payload, 'head', 0, 0, tiled=True).reshape(groups * each, -1)]
    unnamed x46 -> x20, local copies, waits for them, and re-layouts: 1.73 us -> 1.12 us
    pallas_call x7 -> x8, Pallas kernels: 11.8 us -> 11.9 us  [call(): pl.pallas_call(body, out_shape=tuple((jax.ShapeDtypeStruct(s, t) for s, t...]
  transfers between devices with their start and end apart: 15 -> 16, of which waited for: 5 -> 6; matrix products, arithmetic and copies ran while one was open for 1% -> 0% of each run, Pallas kernels for 33% -> 29%
where the time goes in v3:
time: 64.8 us; the launch traced here: 64.4 us
  starting transfers between devices  27.9 us (43%)
  Pallas kernels  26.5 us (41%)
  waiting for transfers between devices  7.99 us (12%)
  local copies, waits for them, and re-layouts  1.15 us (2%)
  between operations  0.84 us (1%)
    pallas_call x8, Pallas kernels, call(): pl.pallas_call(body, out_shape=tuple((jax.ShapeDtypeStruct(s, t) for s, t...  11.9 us
    pallas_call x2, Pallas kernels, document(): pl.pallas_call(functools.partial(doc_kernel, core, heads, ctx_size), out_...  11.1 us
    ppermute x6, starting transfers between devices, along_z(): lax.ppermute(x, 'ctx', [(i, (i + 4 * d) % ctx_size) for i in range(ctx_si...  9.84 us
    all_to_all x1, starting transfers between devices, local(): lax.all_to_all(payload, 'head', 0, 0, tiled=True).reshape(groups * each, -1)  7.07 us
    all_to_all x1, starting transfers between devices, local(): back = lax.all_to_all(back, 'head', 0, 0, tiled=True)  6.86 us
    ppermute x6, waiting for transfers between devices, along_z(): lax.ppermute(x, 'ctx', [(i, (i + 4 * d) % ctx_size) for i in range(ctx_si...  4.58 us
    pallas_call x1, Pallas kernels, local(): pl.pallas_call(functools.partial(pack_kernel, heads, groups, total_doc),...  3.43 us
    ppermute x3, starting transfers between devices, other_chip(): return lax.ppermute(x, 'ctx', [(i, i ^ 2) for i in range(ctx_size)])  3 us
  transfers between devices with their start and end apart: 16, of which 6 were waited for; matrix products, arithmetic and copies ran while one was open for 0% of the time, Pallas kernels for 29%

profile of v3, /device:TPU:0, one launch (start us, length us, event | category | flops | bytes accessed | tf_op | source)
XLA Modules:
  0.0 64.4 jit_solution(13726748747314657200)
XLA Ops:
  0.6 1.7 %collective-permute-start = (bf16[128,128]{1,0:T(8,128)(2,1)}, bf16[128,128]{1,0:T(8,128)(2,1)S(1)}, u32[]{:S(2)}, u32[]{:S(2)}) collective-permute-start(bf16[128,128]{1,0:T(8,128)(2,1)} %dk_ref.1), channel_id=1, source_target_pairs={{0,16},{8,24},{16,0},{24,8},{32,48},{40,56},{48,32},{56,40},{64,80... | collective-permute-start | bytes 98312 | tf_op jit(solution)/shard_map/ppermute | solution.py:385
  2.7 0.7 %copy-done.4 = s32[1,2]{1,0:T(1,128)S(1)} copy-done((s32[1,2]{1,0:T(1,128)S(1)}, s32[1,2]{1,0:T(1,128)}, u32[]{:S(2)}) %copy-start.4) | copy-done | bytes 32
  3.4 3.4 %shard_map.181 = (bf16[8,16,3456]{2,1,0:T(8,128)(2,1)}, bf16[512,128]{1,0:T(8,128)(2,1)S(1)}) custom-call(s32[1,2]{1,0:T(1,128)S(1)} %copy-done.4, bf16[16,12288]{1,0:T(8,128)(2,1)} %do_ref.1, bf16[16,12288]{1,0:T(8,128)(2,1)} %o_ref.1, bf16[16,12288]{1,0:T(8,128)(2,1)} %q_ref.1, bf16[16,1024]{1,0:T(8,128)(2,1)} %k_ref.1, bf16[16,1024]{1,0:T(8,128)(2,1)} %v_ref.1, ...), custom_call_target="tpu_custom_call" | custom-call | flops 5500000256 | tf_op jit(solution)/shard_map/pallas_call | solution.py:394
  6.9 2.1 %collective-permute-start.3 = (bf16[512,128]{1,0:T(8,128)(2,1)S(1)}, bf16[512,128]{1,0:T(8,128)(2,1)S(1)}, u32[]{:S(2)}, u32[]{:S(2)}) collective-permute-start(bf16[512,128]{1,0:T(8,128)(2,1)S(1)} %constant_dynamic-update-slice_fusion.refs_0_), channel_id=1, source_target_pairs={{0,32},{8,40},{16,48},{24,56},{32,64},{40,72},{48,80},{56,88},{64,... | collective-permute-start | bytes 393224 | tf_op jit(solution)/shard_map/ppermute | solution.py:388
  9.0 3.6 %collective-permute-start.5 = (bf16[512,128]{1,0:T(8,128)(2,1)S(1)}, bf16[512,128]{1,0:T(8,128)(2,1)S(1)}, u32[]{:S(2)}, u32[]{:S(2)}) collective-permute-start(bf16[512,128]{1,0:T(8,128)(2,1)S(1)} %constant_dynamic-update-slice_fusion.refs_0_), channel_id=1, source_target_pairs={{0,64},{8,72},{16,80},{24,88},{32,96},{40,104},{48,112},{56,120},{... | collective-permute-start | bytes 393224 | tf_op jit(solution)/shard_map/ppermute | solution.py:388
  12.5 1.0 %collective-permute-start.7 = (bf16[512,128]{1,0:T(8,128)(2,1)S(1)}, bf16[512,128]{1,0:T(8,128)(2,1)S(1)}, u32[]{:S(2)}, u32[]{:S(2)}) collective-permute-start(bf16[512,128]{1,0:T(8,128)(2,1)S(1)} %constant_dynamic-update-slice_fusion.refs_0_), channel_id=1, source_target_pairs={{0,96},{8,104},{16,112},{24,120},{32,0},{40,8},{48,16},{56,24},{64... | collective-permute-start | bytes 393224 | tf_op jit(solution)/shard_map/ppermute | solution.py:388
  13.6 7.1 %all-to-all-start = ((bf16[8,16,3456]{2,1,0:T(8,128)(2,1)}), bf16[8,16,3456]{2,1,0:T(8,128)(2,1)S(1)}, u32[]{:S(2)}, u32[]{:S(2)}) async-start(bf16[8,16,3456]{2,1,0:T(8,128)(2,1)} %get-tuple-element.47), calls=%async_computation | async-start | bytes 1769472 | tf_op jit(solution)/shard_map/all_to_all | solution.py:421
  21.8 5.6 %shard_map.182 = (bf16[1536,128]{1,0:T(8,128)(2,1)S(1)}, bf16[1536,128]{1,0:T(8,128)(2,1)S(1)}, f32[1,1536]{1,0:T(1,128)S(1)}, f32[1,1536]{1,0:T(1,128)S(1)}, f3...) custom-call(s32[32]{0:T(128)S(1)} %copy-done.5, ...), custom_call_target="tpu_custom_call" | custom-call | flops 6600000000 | tf_op jit(solution)/shard_map/pallas_call | solution.py:430
  27.4 5.5 %shard_map.183 = (f32[4,256,256]{2,1,0:T(8,128)}, bf16[128,1536]{1,0:T(8,128)(2,1)}) custom-call(s32[32]{0:T(128)S(1)} %copy-done.5, bf16[512,128]{1,0:T(8,128)(2,1)S(1)} %collective-permute-done.2.refs_0_, bf16[512,128]{1,0:T(8,128)(2,1)S(1)} %collective-permute-done.4.refs_1_, bf16[512,128]{1,0:T(8,128)(2,1)S(1)} %collective-permute-done.6.refs_2_, ...), custom_call_target="tpu_custom_call" | custom-call | flops 6600000000 | tf_op jit(solution)/shard_map/pallas_call | solution.py:430
  33.0 0.8 %all-to-all-done = bf16[8,16,3456]{2,1,0:T(8,128)(2,1)S(1)} async-done(((bf16[8,16,3456]{2,1,0:T(8,128)(2,1)}), bf16[8,16,3456]{2,1,0:T(8,128)(2,1)S(1)}, u32[]{:S(2)}, u32[]{:S(2)}) %all-to-all-start) | async-done | bytes 884768 | tf_op jit(solution)/shard_map/all_to_all | solution.py:421
  33.8 0.8 %shard_map.185 = (bf16[1536,128]{1,0:T(8,128)(2,1)S(1)}, bf16[1536,128]{1,0:T(8,128)(2,1)S(1)}, f32[1,1536]{1,0:T(1,128)S(1)}, f32[1,1536]{1,0:T(1,128)S(1)}, bf...) custom-call(bf16[128,3456]{1,0:T(8,128)(2,1)S(1)} %bitcast.2), custom_call_target="tpu_custom_call" | custom-call | flops 1650000000 | tf_op jit(solution)/shard_map/pallas_call | solution.py:49
  35.0 4.2 %shard_map.186 = (bf16[4,256,256]{2,1,0:T(8,128)(2,1)S(1)}, f32[128,1536]{1,0:T(8,128)S(1)}) custom-call(bf16[1536,128]{1,0:T(8,128)(2,1)S(1)} %get-tuple-element.48.qs_ref, bf16[1536,128]{1,0:T(8,128)(2,1)S(1)} %get-tuple-element.49.dos_ref, f32[1,1536]{1,0:T(1,128)S(1)} %get-tuple-element.50.lse_ref, f32[1,1536]{1,0:T(1,128)S(1)} %get-tuple-element.51.delta_ref, ...), custom_call_target="tpu_custom_call" | custom-call | flops 4840000000 | tf_op jit(solution)/shard_map/pallas_call | solution.py:49
  39.3 1.1 %shard_map.187 = (f32[2,128,256]{2,1,0:T(8,128)S(1)}, f32[128,1536]{1,0:T(8,128)S(1)}) custom-call(bf16[1536,128]{1,0:T(8,128)(2,1)S(1)} %get-tuple-element.48.qs_ref, bf16[1536,128]{1,0:T(8,128)(2,1)S(1)} %get-tuple-element.49.dos_ref, f32[1,1536]{1,0:T(1,128)S(1)} %get-tuple-element.50.lse_ref, f32[1,1536]{1,0:T(1,128)S(1)} %get-tuple-element.51.delta_ref, ...), custom_call_target="tpu_custom_call" | custom-call | flops 1650000000 | tf_op jit(solution)/shard_map/pallas_call | solution.py:49
  40.4 0.8 %collective-permute-done.9.core_ref = bf16[4,256,256]{2,1,0:T(8,128)(2,1)S(1)} collective-permute-done((bf16[4,256,256]{2,1,0:T(8,128)(2,1)S(1)}, bf16[4,256,256]{2,1,0:T(8,128)(2,1)S(1)}, u32[]{:S(2)}, u32[]{:S(2)}) %collective-permute-start.9) | collective-permute-done | bytes 524320 | tf_op jit(solution)/shard_map/ppermute | solution.py:382
  41.2 2.1 %shard_map.188 = (bf16[4,128,256]{2,1,0:T(8,128)(2,1)S(1)}, f32[128,1536]{1,0:T(8,128)S(1)}) custom-call(bf16[1536,128]{1,0:T(8,128)(2,1)S(1)} %get-tuple-element.48.qs_ref, bf16[1536,128]{1,0:T(8,128)(2,1)S(1)} %get-tuple-element.49.dos_ref, f32[1,1536]{1,0:T(1,128)S(1)} %get-tuple-element.50.lse_ref, f32[1,1536]{1,0:T(1,128)S(1)} %get-tuple-element.51.delta_ref, ...), custom_call_target="tpu_custom_call" | custom-call | flops 2420000000 | tf_op jit(solution)/shard_map/pallas_call | solution.py:49
  43.3 0.9 %collective-permute-start.10 = (bf16[4,128,256]{2,1,0:T(8,128)(2,1)S(1)}, bf16[4,128,256]{2,1,0:T(8,128)(2,1)S(1)}, u32[]{:S(2)}, u32[]{:S(2)}) collective-permute-start(bf16[4,128,256]{2,1,0:T(8,128)(2,1)S(1)} %get-tuple-element.64), channel_id=1, source_target_pairs={{0,16},{8,24},{16,0},{24,8},{32,48},{40,56},{48,32},{56,40},{64,80... | collective-permute-start | bytes 786440 | tf_op jit(solution)/shard_map/ppermute | solution.py:385
  44.2 2.0 %shard_map.189 = (f32[2,128,256]{2,1,0:T(8,128)S(1)}, bf16[8,16,1792]{2,1,0:T(8,128)(2,1)}) custom-call(bf16[1536,128]{1,0:T(8,128)(2,1)S(1)} %get-tuple-element.48.qs_ref, bf16[1536,128]{1,0:T(8,128)(2,1)S(1)} %get-tuple-element.49.dos_ref, f32[1,1536]{1,0:T(1,128)S(1)} %get-tuple-element.50.lse_ref, f32[1,1536]{1,0:T(1,128)S(1)} %get-tuple-element.51.delta_ref, ...), custom_call_target="tpu_custom_call" | custom-call | flops 2200000000 | tf_op jit(solution)/shard_map/pallas_call | solution.py:49
  46.1 6.9 %all-to-all-start.1 = ((bf16[8,16,1792]{2,1,0:T(8,128)(2,1)}), bf16[8,16,1792]{2,1,0:T(8,128)(2,1)S(1)}, u32[]{:S(2)}, u32[]{:S(2)}) async-start(bf16[8,16,1792]{2,1,0:T(8,128)(2,1)} %get-tuple-element.60), calls=%async_computation.1 | async-start | bytes 917504 | tf_op jit(solution)/shard_map/all_to_all | solution.py:466
  53.2 3.1 %collective-permute-start.12 = (bf16[128,256]{1,0:T(8,128)(2,1)S(1)}, bf16[128,256]{1,0:T(8,128)(2,1)S(1)}, u32[]{:S(2)}, u32[]{:S(2)}) collective-permute-start(bf16[128,256]{1,0:T(8,128)(2,1)S(1)} %get-tuple-element.67), channel_id=1, source_target_pairs={{0,64},{8,72},{16,80},{24,88},{32,96},{40,104},{48,112},{56,120},{... | collective-permute-start | bytes 196616 | tf_op jit(solution)/shard_map/ppermute | solution.py:388
  56.3 0.9 %shard_map.184 = bf16[128,1536]{1,0:T(8,128)(2,1)} custom-call(bf16[128,1536]{1,0:T(8,128)(2,1)S(1)} %copy-done.7), custom_call_target="tpu_custom_call" | custom-call | flops 2200000000 | tf_op jit(solution)/shard_map/pallas_call | solution.py:49
  57.6 1.4 %collective-permute-done.12.refs_1_ = bf16[128,256]{1,0:T(8,128)(2,1)S(1)} collective-permute-done((bf16[128,256]{1,0:T(8,128)(2,1)S(1)}, bf16[128,256]{1,0:T(8,128)(2,1)S(1)}, u32[]{:S(2)}, u32[]{:S(2)}) %collective-permute-start.12) | collective-permute-done | bytes 65568 | tf_op jit(solution)/shard_map/ppermute | solution.py:388
  59.0 2.7 %collective-permute-done.13.refs_2_ = bf16[128,256]{1,0:T(8,128)(2,1)S(1)} collective-permute-done((bf16[128,256]{1,0:T(8,128)(2,1)S(1)}, bf16[128,256]{1,0:T(8,128)(2,1)S(1)}, u32[]{:S(2)}, u32[]{:S(2)}) %collective-permute-start.13) | collective-permute-done | bytes 65568 | tf_op jit(solution)/shard_map/ppermute | solution.py:388
  61.8 1.8 %all-to-all-done.1.back_ref = bf16[8,16,1792]{2,1,0:T(8,128)(2,1)S(1)} async-done(((bf16[8,16,1792]{2,1,0:T(8,128)(2,1)}), bf16[8,16,1792]{2,1,0:T(8,128)(2,1)S(1)}, u32[]{:S(2)}, u32[]{:S(2)}) %all-to-all-start.1) | async-done | bytes 458784 | tf_op jit(solution)/shard_map/all_to_all | solution.py:466
  63.6 0.8 %shard_map.191 = (bf16[16,12288]{1,0:T(8,128)(2,1)}, bf16[16,1024]{1,0:T(8,128)(2,1)}, bf16[16,1024]{1,0:T(8,128)(2,1)}, bf16[128,128]{1,0:T(8,128)(2,1)}, bf16[128,128]{1,0:T(8,128)(2,1)}) custom-call(bf16[8,16,1792]{2,1,0:T(8,128)(2,1)S(1)} %all-to-all-done.1.back_ref, f32[128,256]{1,0:T(8,128)S(1)} %get-tuple-element.65.keep_ref, ...), custom_call_target="tpu_custom_call" | custom-call | flops 880000000 | tf_op jit(solution)/shard_map/pallas_call | solution.py:49
  (41 shorter events, 2.7 us)
Async XLA Ops:
  0.6 6.2 %collective-permute-start = (bf16[128,128]{1,0:T(8,128)(2,1)}, bf16[128,128]{1,0:T(8,128)(2,1)S(1)}, u32[]{:S(2)}, u32[]{:S(2)}) collective-permute-start(bf16[128,128]{1,0:T(8,128)(2,1)} %dk_ref.1), channel_id=1, source_target_pairs={{0,16},{8,24},{16,0},{24,8},{32,48},{40,56},{48,32},{56,40},{64,80... | collective-permute-start | bytes 98312 | tf_op jit(solution)/shard_map/ppermute | solution.py:385
  2.3 4.6 %collective-permute-start.1 = (bf16[128,128]{1,0:T(8,128)(2,1)}, bf16[128,128]{1,0:T(8,128)(2,1)S(1)}, u32[]{:S(2)}, u32[]{:S(2)}) collective-permute-start(bf16[128,128]{1,0:T(8,128)(2,1)} %dv_ref.1), channel_id=1, source_target_pairs={{0,16},{8,24},{16,0},{24,8},{32,48},{40,56},{48,32},{56,40},{64,80... | collective-permute-start | bytes 98312 | tf_op jit(solution)/shard_map/ppermute | solution.py:385
  6.9 13.8 %collective-permute-start.3 = (bf16[512,128]{1,0:T(8,128)(2,1)S(1)}, bf16[512,128]{1,0:T(8,128)(2,1)S(1)}, u32[]{:S(2)}, u32[]{:S(2)}) collective-permute-start(bf16[512,128]{1,0:T(8,128)(2,1)S(1)} %constant_dynamic-update-slice_fusion.refs_0_), channel_id=1, source_target_pairs={{0,32},{8,40},{16,48},{24,56},{32,64},{40,72},{48,80},{56,88},{64,... | collective-permute-start | bytes 393224 | tf_op jit(solution)/shard_map/ppermute | solution.py:388
  9.0 12.3 %collective-permute-start.5 = (bf16[512,128]{1,0:T(8,128)(2,1)S(1)}, bf16[512,128]{1,0:T(8,128)(2,1)S(1)}, u32[]{:S(2)}, u32[]{:S(2)}) collective-permute-start(bf16[512,128]{1,0:T(8,128)(2,1)S(1)} %constant_dynamic-update-slice_fusion.refs_0_), channel_id=1, source_target_pairs={{0,64},{8,72},{16,80},{24,88},{32,96},{40,104},{48,112},{56,120},{... | collective-permute-start | bytes 393224 | tf_op jit(solution)/shard_map/ppermute | solution.py:388
  12.5 8.8 %collective-permute-start.7 = (bf16[512,128]{1,0:T(8,128)(2,1)S(1)}, bf16[512,128]{1,0:T(8,128)(2,1)S(1)}, u32[]{:S(2)}, u32[]{:S(2)}) collective-permute-start(bf16[512,128]{1,0:T(8,128)(2,1)S(1)} %constant_dynamic-update-slice_fusion.refs_0_), channel_id=1, source_target_pairs={{0,96},{8,104},{16,112},{24,120},{32,0},{40,8},{48,16},{56,24},{64... | collective-permute-start | bytes 393224 | tf_op jit(solution)/shard_map/ppermute | solution.py:388
  13.6 8.2 %copy-start = (bf16[128,1536]{1,0:T(8,128)(2,1)S(1)}, bf16[128,1536]{1,0:T(8,128)(2,1)}, u32[]{:S(2)}) copy-start(bf16[128,1536]{1,0:T(8,128)(2,1)} %refs_4_.1) | copy-start | bytes 1179652
  13.6 8.2 %copy-start.1 = (bf16[128,1536]{1,0:T(8,128)(2,1)S(1)}, bf16[128,1536]{1,0:T(8,128)(2,1)}, u32[]{:S(2)}) copy-start(bf16[128,1536]{1,0:T(8,128)(2,1)} %refs_5_.1) | copy-start | bytes 1179652
  13.6 8.2 %copy-start.2 = (bf16[128,1536]{1,0:T(8,128)(2,1)S(1)}, bf16[128,1536]{1,0:T(8,128)(2,1)}, u32[]{:S(2)}) copy-start(bf16[128,1536]{1,0:T(8,128)(2,1)} %refs_6_.1) | copy-start | bytes 1179652
  13.6 8.2 %copy-start.3 = (f32[128,12]{0,1:T(8,128)S(1)}, f32[128,12]{0,1:T(8,128)}, u32[]{:S(2)}) copy-start(f32[128,12]{0,1:T(8,128)} %param.21) | copy-start | bytes 18436
  13.6 20.2 %all-to-all-start = ((bf16[8,16,3456]{2,1,0:T(8,128)(2,1)}), bf16[8,16,3456]{2,1,0:T(8,128)(2,1)S(1)}, u32[]{:S(2)}, u32[]{:S(2)}) async-start(bf16[8,16,3456]{2,1,0:T(8,128)(2,1)} %get-tuple-element.47), calls=%async_computation | async-start | bytes 1769472 | tf_op jit(solution)/shard_map/all_to_all | solution.py:421
  20.6 6.8 %collective-permute-start.2 = (bf16[512,128]{1,0:T(8,128)(2,1)S(1)}, bf16[512,128]{1,0:T(8,128)(2,1)S(1)}, u32[]{:S(2)}, u32[]{:S(2)}) collective-permute-start(bf16[512,128]{1,0:T(8,128)(2,1)S(1)} %constant_dynamic-update-slice_fusion.refs_0_), channel_id=1, source_target_pairs={{0,8},{8,0},{16,24},{24,16},{32,40},{40,32},{48,56},{56,48},{64,72... | collective-permute-start | bytes 393224 | tf_op jit(solution)/shard_map/ppermute | solution.py:382
  20.7 6.7 %collective-permute-start.4 = (bf16[512,128]{1,0:T(8,128)(2,1)S(1)}, bf16[512,128]{1,0:T(8,128)(2,1)S(1)}, u32[]{:S(2)}, u32[]{:S(2)}) collective-permute-start(bf16[512,128]{1,0:T(8,128)(2,1)S(1)} %collective-permute-done.3.refs_1_), channel_id=1, source_target_pairs={{0,8},{8,0},{16,24},{24,16},{32,40},{40,32},{48,56},{56,48},{64,72... | collective-permute-start | bytes 393224 | tf_op jit(solution)/shard_map/ppermute | solution.py:382
  21.2 6.2 %collective-permute-start.6 = (bf16[512,128]{1,0:T(8,128)(2,1)S(1)}, bf16[512,128]{1,0:T(8,128)(2,1)S(1)}, u32[]{:S(2)}, u32[]{:S(2)}) collective-permute-start(bf16[512,128]{1,0:T(8,128)(2,1)S(1)} %collective-permute-done.5.refs_2_.refs_0_), channel_id=1, source_target_pairs={{0,8},{8,0},{16,24},{24,16},{32,40},{40,32},{48,56},{56,48},{64,72... | collective-permute-start | bytes 393224 | tf_op jit(solution)/shard_map/ppermute | solution.py:382
  21.3 6.1 %collective-permute-start.8 = (bf16[512,128]{1,0:T(8,128)(2,1)S(1)}, bf16[512,128]{1,0:T(8,128)(2,1)S(1)}, u32[]{:S(2)}, u32[]{:S(2)}) collective-permute-start(bf16[512,128]{1,0:T(8,128)(2,1)S(1)} %collective-permute-done.7.refs_3_.refs_1_), channel_id=1, source_target_pairs={{0,8},{8,0},{16,24},{24,16},{32,40},{40,32},{48,56},{56,48},{64,72... | collective-permute-start | bytes 393224 | tf_op jit(solution)/shard_map/ppermute | solution.py:382
  33.8 1.2 %copy-start.8 = (f32[4,256,256]{2,1,0:T(8,128)S(1)}, f32[4,256,256]{2,1,0:T(8,128)}, u32[]{:S(2)}) copy-start(f32[4,256,256]{2,1,0:T(8,128)} %get-tuple-element.53.refs_4_) | copy-start | bytes 3145732
  39.2 2.0 %collective-permute-start.9 = (bf16[4,256,256]{2,1,0:T(8,128)(2,1)S(1)}, bf16[4,256,256]{2,1,0:T(8,128)(2,1)S(1)}, u32[]{:S(2)}, u32[]{:S(2)}) collective-permute-start(bf16[4,256,256]{2,1,0:T(8,128)(2,1)S(1)} %get-tuple-element.56), channel_id=1, source_target_pairs={{0,8},{8,0},{16,24},{24,16},{32,40},{40,32},{48,56},{56,48},{64,72... | collective-permute-start | bytes 1572872 | tf_op jit(solution)/shard_map/ppermute | solution.py:382
  39.3 1.9 %copy-start.6 = (f32[4,128,256]{2,1,0:T(8,128)S(1)}, f32[4,128,256]{2,1,0:T(8,128)}, u32[]{:S(2)}) copy-start(f32[4,128,256]{2,1,0:T(8,128)} %get-tuple-element.57.refs_4_) | copy-start | bytes 1572868
  43.3 9.7 %collective-permute-start.10 = (bf16[4,128,256]{2,1,0:T(8,128)(2,1)S(1)}, bf16[4,128,256]{2,1,0:T(8,128)(2,1)S(1)}, u32[]{:S(2)}, u32[]{:S(2)}) collective-permute-start(bf16[4,128,256]{2,1,0:T(8,128)(2,1)S(1)} %get-tuple-element.64), channel_id=1, source_target_pairs={{0,16},{8,24},{16,0},{24,8},{32,48},{40,56},{48,32},{56,40},{64,80... | collective-permute-start | bytes 786440 | tf_op jit(solution)/shard_map/ppermute | solution.py:385
  46.1 6.9 %copy-start.9 = (f32[4,128,256]{2,1,0:T(8,128)S(1)}, f32[4,128,256]{2,1,0:T(8,128)}, u32[]{:S(2)}) copy-start(f32[4,128,256]{2,1,0:T(8,128)} %get-tuple-element.63.doc_ref) | copy-start | bytes 1572868
  46.1 17.5 %all-to-all-start.1 = ((bf16[8,16,1792]{2,1,0:T(8,128)(2,1)}), bf16[8,16,1792]{2,1,0:T(8,128)(2,1)S(1)}, u32[]{:S(2)}, u32[]{:S(2)}) async-start(bf16[8,16,1792]{2,1,0:T(8,128)(2,1)} %get-tuple-element.60), calls=%async_computation.1 | async-start | bytes 917504 | tf_op jit(solution)/shard_map/all_to_all | solution.py:466
  53.0 3.3 %copy-start.7 = (bf16[128,1536]{1,0:T(8,128)(2,1)S(1)}, bf16[128,1536]{1,0:T(8,128)(2,1)}, u32[]{:S(2)}) copy-start(bf16[128,1536]{1,0:T(8,128)(2,1)} %get-tuple-element.46.turned_ref) | copy-start | bytes 1179652
  53.1 4.5 %collective-permute-start.11 = (bf16[128,256]{1,0:T(8,128)(2,1)S(1)}, bf16[128,256]{1,0:T(8,128)(2,1)S(1)}, u32[]{:S(2)}, u32[]{:S(2)}) collective-permute-start(bf16[128,256]{1,0:T(8,128)(2,1)S(1)} %get-tuple-element.66), channel_id=1, source_target_pairs={{0,96},{8,104},{16,112},{24,120},{32,0},{40,8},{48,16},{56,24},{64... | collective-permute-start | bytes 196616 | tf_op jit(solution)/shard_map/ppermute | solution.py:388
  53.2 5.8 %collective-permute-start.12 = (bf16[128,256]{1,0:T(8,128)(2,1)S(1)}, bf16[128,256]{1,0:T(8,128)(2,1)S(1)}, u32[]{:S(2)}, u32[]{:S(2)}) collective-permute-start(bf16[128,256]{1,0:T(8,128)(2,1)S(1)} %get-tuple-element.67), channel_id=1, source_target_pairs={{0,64},{8,72},{16,80},{24,88},{32,96},{40,104},{48,112},{56,120},{... | collective-permute-start | bytes 196616 | tf_op jit(solution)/shard_map/ppermute | solution.py:388
  56.3 5.5 %collective-permute-start.13 = (bf16[128,256]{1,0:T(8,128)(2,1)S(1)}, bf16[128,256]{1,0:T(8,128)(2,1)S(1)}, u32[]{:S(2)}, u32[]{:S(2)}) collective-permute-start(bf16[128,256]{1,0:T(8,128)(2,1)S(1)} %get-tuple-element.68), channel_id=1, source_target_pairs={{0,32},{8,40},{16,48},{24,56},{32,64},{40,72},{48,80},{56,88},{64,... | collective-permute-start | bytes 196616 | tf_op jit(solution)/shard_map/ppermute | solution.py:388
  (2 other events, 1.8 us)

commit v4 on v3

--- a/solution.py
+++ b/solution.py
@@ -108,12 +108,12 @@
     return [dq[:, j * D : (j + 1) * D].T for j in range(heads)]
 
 
-def pack_kernel(heads, groups, total, len_ref, do_ref, o_ref, q_ref, k_ref, v_ref, ex_ref, dk_ref, dv_ref, pay_ref, kv_ref, *refs):
-    grad, out, query, keys, values, buf, packed, high, low, sems = refs
+def pack_kernel(heads, groups, total, len_hbm, do_ref, o_ref, q_ref, k_ref, v_ref, ex_ref, dk_ref, dv_ref, pay_ref, kv_ref, *refs):
+    grad, out, query, keys, values, buf, len_ref, packed, high, low, sems = refs
     rows = out.shape[0]
     wide = heads * D
     pairs = (
-        (do_ref, grad), (o_ref, out), (q_ref, query), (k_ref, keys), (v_ref, values), (ex_ref, buf),
+        (do_ref, grad), (o_ref, out), (q_ref, query), (k_ref, keys), (v_ref, values), (ex_ref, buf), (len_hbm, len_ref),
         (dk_ref, kv_ref.at[pl.ds(0, D)]), (dv_ref, kv_ref.at[pl.ds(D, D)]),
     )
     loads = [pltpu.make_async_copy(source, to, sems.at[n]) for n, (source, to) in enumerate(pairs)]
@@ -127,9 +127,6 @@
             sends.append(pltpu.make_async_copy(source.at[:, pl.ds(g * size, size)], part, sems.at[len(pairs) + len(sends)]))
             sends[-1].start()
 
-    row = lax.axis_index("head") * rows + sublanes((rows, D))
-    within = jnp.where(row < len_ref[0, 0], row, row - len_ref[0, 0])
-    log_count = jnp.log((within + 1 + total).astype(F32))
     loads[0].wait()
     send(grad, wide, wide)
     loads[2].wait()
@@ -145,6 +142,10 @@
     ones = head_ones((wide, D), 1)
     deltas = dot(high[...], ones, 1, 0) + dot(low[...], ones, 1, 0)
     loads[5].wait()
+    loads[6].wait()
+    row = lax.axis_index("head") * rows + sublanes((rows, D))
+    within = jnp.where(row < len_ref[0, 0], row, row - len_ref[0, 0])
+    log_count = jnp.log((within + 1 + total).astype(F32))
     lse = (buf[...] + log_count[:, : heads * groups]) * LOG2E
     lse = jnp.concatenate([lse, jnp.zeros((rows, D - heads * groups), F32)], axis=1)
     lane = lanes((rows, D))
@@ -161,7 +162,7 @@
         packed[g] = jnp.where(lane == 96, (row - within).astype(F32), stats).astype(BF)
     sends.append(pltpu.make_async_copy(packed, pay_ref.at[:, :, pl.ds(2 * wide + 2 * D, D)], sems.at[len(pairs) + len(sends)]))
     sends[-1].start()
-    for copy in loads[6:] + sends:
+    for copy in loads[7:] + sends:
         copy.wait()
 
 
@@ -229,11 +230,13 @@
             else:
                 far_ref[depth, :, cut] = grad
         total = dq if total is None else total + dq
-        if core == 0:
-            store(own_ref.at[depth], own_hbm.at[depth])
-            store(near_ref.at[depth], near_hbm.at[depth])
-        else:
-            store(far_ref.at[depth], far_hbm.at[depth])
+        if depth % 2 == 1:
+            done = pl.ds(depth - 1, 2)
+            if core == 0:
+                store(own_ref.at[done], own_hbm.at[done])
+                store(near_ref.at[done], near_hbm.at[done])
+            else:
+                store(far_ref.at[done], far_hbm.at[done])
     if core == 0:
         dq_ref[...] = total
     else:
@@ -248,35 +251,28 @@
         out_ref[:, j * D : (j + 1) * D] = turned_ref[:, j * D : (j + 1) * D].T
 
 
-def self_kernel(heads, pay_ref, qs_ref, dos_ref, lse_ref, delta_ref, self_ref, dq_ref):
+def far_kernel(heads, pay_ref, *refs):
+    kv_refs, doc_hbm = refs[:4], refs[4]
+    send_ref, dq_ref, qs_ref, dos_ref, lse_ref, delta_ref, doc_ref, sems = refs[5:]
+    parts = (pl.ds(0, 1), pl.ds(1, 3))
+    loads = [pltpu.make_async_copy(doc_hbm.at[at], doc_ref.at[at], sems.at[n]) for n, at in enumerate(parts)]
+    for load in loads:
+        load.start()
     wide = heads * D
     stack_heads(pay_ref, qs_ref, heads, 0)
     stack_heads(pay_ref, dos_ref, heads, wide)
     stats = pay_ref[:, 2 * wide + 2 * D :].astype(F32).T
     spread_rows(stats[:16] + stats[16:32] + stats[32:48], lse_ref, heads)
     spread_rows(stats[48:64] + stats[64:80] + stats[80:96], delta_ref, heads)
-    row = lanes((1, D))
-    key = sublanes((D, 1))
-    seen = (key <= row) & (key >= stats[96:97].astype(jnp.int32))
-    mask = jnp.concatenate([seen] * heads, axis=1)
-    keys = pay_ref[:, 2 * wide : 2 * wide + D]
-    values = pay_ref[:, 2 * wide + D : 2 * wide + 2 * D]
-    dq, dk, dv = pair_block(qs_ref, dos_ref, keys, values, lse_ref[...], delta_ref[...], mask)
-    self_ref[:, :D] = dk.astype(BF)
-    self_ref[:, D:] = dv.astype(BF)
-    dq_ref[...] = dq
-
-
-def far_kernel(qs_ref, dos_ref, lse_ref, delta_ref, dq_in, *refs):
-    kv_refs, doc_ref = refs[:4], refs[4]
-    send_ref, dq_ref = refs[5:]
     lse, delta = lse_ref[...], delta_ref[...]
-    total = dq_in[...]
+    total = None
     for n in range(4):
         dq, dk, dv = pair_block(qs_ref, dos_ref, *both(kv_refs[n]), lse, delta, None)
+        if n < 2:
+            loads[n].wait()
         send_ref[n, :, :D] = (dk + doc_ref[n, :, :D]).astype(BF)
         send_ref[n, :, D:] = (dv + doc_ref[n, :, D:]).astype(BF)
-        total = total + dq
+        total = dq if total is None else total + dq
     dq_ref[...] = total
 
 
@@ -304,37 +300,65 @@
     dq_ref[...] = column(1, qs_ref, dos_ref, lse_ref[...], delta_ref[...], kv_refs, dq_in[...], store)
 
 
-def own_kernel(qs_ref, dos_ref, lse_ref, delta_ref, dq_in, *refs):
+def own_kernel(heads, qs_ref, dos_ref, lse_ref, delta_ref, dq_in, pay_ref, *refs):
     kv_refs = refs[:2]
-    out_ref, dq_ref = refs[2:]
+    out_ref, self_ref, dq_ref = refs[2:]
+    wide = heads * D
+    lse, delta = lse_ref[...], delta_ref[...]
+    stats = pay_ref[:, 2 * wide + 2 * D :].astype(F32).T
+    row = lanes((1, D))
+    key = sublanes((D, 1))
+    seen = (key <= row) & (key >= stats[96:97].astype(jnp.int32))
+    mask = jnp.concatenate([seen] * heads, axis=1)
+    keys = pay_ref[:, 2 * wide : 2 * wide + D]
+    values = pay_ref[:, 2 * wide + D : 2 * wide + 2 * D]
+    dq, dk, dv = pair_block(qs_ref, dos_ref, keys, values, lse, delta, mask)
+    self_ref[:, :D] = dk.astype(BF)
+    self_ref[:, D:] = dv.astype(BF)
 
     def store(n, cut, grad):
         out_ref[n, :, cut] = grad
 
-    dq_ref[...] = column(0, qs_ref, dos_ref, lse_ref[...], delta_ref[...], kv_refs, dq_in[...], store)
-
-
-def last_kernel(heads, groups, qs_ref, dos_ref, lse_ref, delta_ref, dq_in, self_ref, *refs):
+    dq_ref[...] = column(0, qs_ref, dos_ref, lse, delta, kv_refs, dq_in[...] + dq, store)
+
+
+def last_kernel(heads, groups, qs_ref, dos_ref, lse_ref, delta_ref, dq_in, self_ref, low_ref, core_ref, doc_ref, *refs):
     kv_refs = refs[:2]
-    out_ref, back_ref = refs[2:]
+    out_ref, back_hbm, back_ref, sems = refs[2:]
     wide = heads * D
-
-    def store(n, cut, grad):
-        out_ref[n, :, cut] = grad
-
-    total = column(0, qs_ref, dos_ref, lse_ref[...], delta_ref[...], kv_refs, dq_in[...], store)
     each = D // groups
+    copies = []
+
+    def send(at, size):
+        cut = (slice(None), slice(None), pl.ds(at, size))
+        copies.append(pltpu.make_async_copy(back_ref.at[cut], back_hbm.at[cut], sems.at[len(copies)]))
+        copies[-1].start()
+
     for g in range(groups):
         back_ref[g, :, wide:] = self_ref[g * each : (g + 1) * each]
+    send(wide, 2 * D)
+
+    def other(n, cut):
+        return doc_ref[n, :, cut] + core_ref[n, :D, cut].astype(F32)
+
+    def store(n, cut, grad):
+        out_ref[n + 2, :, cut] = grad + other(n + 2, cut)
+
+    total = column(0, qs_ref, dos_ref, lse_ref[...], delta_ref[...], kv_refs, dq_in[...], store)
     for j, part in enumerate(unstack_query_grad(total, heads)):
         for g in range(groups):
             back_ref[g, :, j * D : (j + 1) * D] = part[g * each : (g + 1) * each]
-
-
-def held_kernel(low_ref, high_ref, doc_ref, core_ref, chip_ref, keep_ref, *send_refs):
+        if j % 4 == 3:
+            send((j - 3) * D, 4 * D)
+    for n in range(2):
+        out_ref[n] = low_ref[n] + other(n, slice(0, 2 * D))
+    for copy in copies:
+        copy.wait()
+
+
+def held_kernel(own_ref, chip_ref, keep_ref, *send_refs):
     for n in range(4):
-        own = low_ref[n] if n < 2 else high_ref[n - 2]
-        held = own + doc_ref[n] + core_ref[n, :D].astype(F32) + chip_ref[n].astype(F32)
+        held = own_ref[n] + chip_ref[n].astype(F32)
         if n == 0:
             keep_ref[...] = held
         else:
@@ -397,19 +421,19 @@
             pltpu.HBM((groups, each, 2 * wide + 3 * D), BF),
             jax.ShapeDtypeStruct((4 * rows, D), BF),
         ),
-        in_specs=[smem()] + [hbm()] * 8,
+        in_specs=[hbm()] * 9,
         out_specs=(hbm(), vmem()),
         scratch_shapes=[asking, asking, asking, narrow, narrow, pltpu.VMEM((each, heads * groups), F32)]
-        + [pltpu.VMEM((groups, each, D), BF), both_parts, both_parts, pltpu.SemaphoreType.DMA((9 + 4 * groups,))],
+        + [pltpu.SMEM(question_lengths.shape, jnp.int32), pltpu.VMEM((groups, each, D), BF), both_parts, both_parts]
+        + [pltpu.SemaphoreType.DMA((10 + 4 * groups,))],
         compiler_params=SHARED,
         cost_estimate=cost(5),
     )(
-        question_lengths,
         *[
             pltpu.with_memory_space_constraint(x, pltpu.HBM)
             for x in (
-                question_outgrad, question_output, question_query_matrix, question_key_matrix, question_value_matrix,
-                question_excess, document_key_matrix, document_value_matrix,
+                question_lengths, question_outgrad, question_output, question_query_matrix, question_key_matrix,
+                question_value_matrix, question_excess, document_key_matrix, document_value_matrix,
             )
         ],
     )
@@ -444,32 +468,42 @@
         block_order, *mine, document_query_matrix, document_output, document_outgrad, document_excess.T,
     )
     far_doc, doc_turned = document(1, [], [double, ((D, stacked), BF)], block_order, *theirs, *doc_state, dq)
-    *state, own_self, dq = call(
-        1.5,
-        functools.partial(self_kernel, heads),
-        row_state + [((rows, 2 * D), BF), query_sum],
+    far, dq, *state = pl.pallas_call(
+        functools.partial(far_kernel, heads),
+        out_shape=tuple(jax.ShapeDtypeStruct(*out) for out in [((depth, 2 * rows, 2 * D), BF), query_sum] + row_state),
+        in_specs=[vmem()] * 5 + [hbm()],
+        out_specs=(vmem(),) * 6,
+        scratch_shapes=[pltpu.VMEM(*double), pltpu.SemaphoreType.DMA((2,))],
+        compiler_params=SHARED,
+        cost_estimate=cost(4.8),
+    )(asked, *theirs, pltpu.with_memory_space_constraint(far_doc, pltpu.HBM))
+    core_sum = other_core(far)
+    low, own_self, dq = call(
+        2,
+        functools.partial(own_kernel, heads),
+        [((2, rows, 2 * D), F32), ((rows, 2 * D), BF), query_sum],
         0,
-        asked,
-    )
-    far, dq = call(4.4, far_kernel, [((depth, 2 * rows, 2 * D), BF), query_sum], 0, *state, dq, *theirs, far_doc)
-    core_sum = other_core(far)
-    low, dq = call(1.5, own_kernel, [((2, rows, 2 * D), F32), query_sum], 0, *state, dq, *mine[:2])
+        *state, dq, asked, *mine[:2],
+    )
     near, dq = call(2.2, near_kernel, [((depth, rows, 2 * D), BF), query_sum], 0, *state, dq, core_sum, *mine, near_doc)
     chip_sum = other_chip(near)
-    high, back = call(
-        2,
+    returned = ((groups, each, wide + 2 * D), BF)
+    own, back = pl.pallas_call(
         functools.partial(last_kernel, heads, groups),
-        [((2, rows, 2 * D), F32), ((groups, each, wide + 2 * D), BF)],
-        0,
-        *state, dq, own_self, *mine[2:],
-    )
+        out_shape=(jax.ShapeDtypeStruct(*quarter), pltpu.HBM(*returned)),
+        in_specs=[vmem()] * 11,
+        out_specs=(vmem(), hbm()),
+        scratch_shapes=[pltpu.VMEM(*returned), pltpu.SemaphoreType.DMA((4,))],
+        compiler_params=SHARED,
+        cost_estimate=cost(2),
+    )(*state, dq, own_self, low, core_sum, own_doc, *mine[2:])
     back = lax.all_to_all(back, "head", 0, 0, tiled=True)
     keep, *sends = call(
         25,
         held_kernel,
         [((rows, 2 * D), F32)] + [((rows, 2 * D), BF)] * (depth - 1),
         0,
-        low, high, own_doc, core_sum, chip_sum,
+        own, chip_sum,
     )
     (document_query_grad,) = call(2, functools.partial(turn_kernel, heads), [flat], 0, doc_turned)
     arrived = [along_z(send, depth - 1 - n) for n, send in enumerate(sends)]

time: 64.8 us -> 62.4 us (0.963)
  waiting for transfers between devices: 7.99 us -> 6.57 us
  local copies, waits for them, and re-layouts: 1.15 us -> 0.05 us
    pallas_call x0 -> x2, Pallas kernels: none -> 7.07 us  [the longest x1 5.14 us: local(): pl.pallas_call(functools.partial(far_kernel, heads), out_shape=tuple((jax...]
    pallas_call x8 -> x5, Pallas kernels: 11.9 us -> 5.49 us  [call(): pl.pallas_call(body, out_shape=tuple((jax.ShapeDtypeStruct(s, t) for s, t...]
    all_to_all x1, waiting for transfers between devices: 1.82 us -> 0.68 us  [local(): back = lax.all_to_all(back, 'head', 0, 0, tiled=True)]
    unnamed x20 -> x16, local copies, waits for them, and re-layouts: 1.12 us -> 0.03 us
    ppermute x3, waiting for transfers between devices: 0.01 us -> 0.71 us  [other_chip(): return lax.ppermute(x, 'ctx', [(i, i ^ 2) for i in range(ctx_size)])]
  transfers between devices with their start and end apart: 16 -> 16, of which waited for: 6 -> 6; matrix products, arithmetic and copies ran while one was open for 0% -> 0% of each run, Pallas kernels for 29% -> 30%
where the time goes in v4:
time: 62.4 us; the launch traced here: 61.8 us
  starting transfers between devices  27.6 us (44%)
  Pallas kernels  26.8 us (43%)
  waiting for transfers between devices  6.57 us (11%)
  between operations  0.82 us (1%)
    pallas_call x2, Pallas kernels, document(): pl.pallas_call(functools.partial(doc_kernel, core, heads, ctx_size), out_...  11.3 us
    ppermute x6, starting transfers between devices, along_z(): lax.ppermute(x, 'ctx', [(i, (i + 4 * d) % ctx_size) for i in range(ctx_si...  9.65 us
    all_to_all x1, starting transfers between devices, local(): back = lax.all_to_all(back, 'head', 0, 0, tiled=True)  6.96 us
    all_to_all x1, starting transfers between devices, local(): lax.all_to_all(payload, 'head', 0, 0, tiled=True).reshape(groups * each, -1)  6.8 us
    pallas_call x5, Pallas kernels, call(): pl.pallas_call(body, out_shape=tuple((jax.ShapeDtypeStruct(s, t) for s, t...  5.49 us
    pallas_call x1, Pallas kernels, local(): pl.pallas_call(functools.partial(far_kernel, heads), out_shape=tuple((jax...  5.14 us
    ppermute x6, waiting for transfers between devices, along_z(): lax.ppermute(x, 'ctx', [(i, (i + 4 * d) % ctx_size) for i in range(ctx_si...  4.58 us
    ppermute x3, starting transfers between devices, other_chip(): return lax.ppermute(x, 'ctx', [(i, i ^ 2) for i in range(ctx_size)])  2.99 us
  transfers between devices with their start and end apart: 16, of which 6 were waited for; matrix products, arithmetic and copies ran while one was open for 0% of the time, Pallas kernels for 30%

profile of v4, /device:TPU:0, one launch (start us, length us, event | category | flops | bytes accessed | tf_op | source)
XLA Modules:
  0.0 61.8 jit_solution(6968334369016609853)
XLA Ops:
  0.6 1.7 %collective-permute-start = (bf16[128,128]{1,0:T(8,128)(2,1)}, bf16[128,128]{1,0:T(8,128)(2,1)S(1)}, u32[]{:S(2)}, u32[]{:S(2)}) collective-permute-start(bf16[128,128]{1,0:T(8,128)(2,1)} %dk_ref.1), channel_id=1, source_target_pairs={{0,16},{8,24},{16,0},{24,8},{32,48},{40,56},{48,32},{56,40},{64,80... | collective-permute-start | bytes 98312 | tf_op jit(solution)/shard_map/ppermute | solution.py:409
  2.3 0.5 collective-permute-start.1
  2.7 2.9 %shard_map.181 = (bf16[8,16,3456]{2,1,0:T(8,128)(2,1)}, bf16[512,128]{1,0:T(8,128)(2,1)S(1)}) custom-call(s32[1,2]{1,0:T(1,128)} %len_hbm.1, bf16[16,12288]{1,0:T(8,128)(2,1)} %do_ref.1, bf16[16,12288]{1,0:T(8,128)(2,1)} %o_ref.1, bf16[16,12288]{1,0:T(8,128)(2,1)} %q_ref.1, bf16[16,1024]{1,0:T(8,128)(2,1)} %k_ref.1, bf16[16,1024]{1,0:T(8,128)(2,1)} %v_ref.1, ...), custom_call_target="tpu_custom_call" | custom-call | flops 5500000256 | tf_op jit(solution)/shard_map/pallas_call | solution.py:418
  5.7 0.7 %collective-permute-done.1 = bf16[128,128]{1,0:T(8,128)(2,1)S(1)} collective-permute-done((bf16[128,128]{1,0:T(8,128)(2,1)}, bf16[128,128]{1,0:T(8,128)(2,1)S(1)}, u32[]{:S(2)}, u32[]{:S(2)}) %collective-permute-start.1) | collective-permute-done | bytes 32800 | tf_op jit(solution)/shard_map/ppermute | solution.py:409
  6.4 4.0 %collective-permute-start.7 = (bf16[512,128]{1,0:T(8,128)(2,1)S(1)}, bf16[512,128]{1,0:T(8,128)(2,1)S(1)}, u32[]{:S(2)}, u32[]{:S(2)}) collective-permute-start(bf16[512,128]{1,0:T(8,128)(2,1)S(1)} %constant_dynamic-update-slice_fusion.refs_0_), channel_id=1, source_target_pairs={{0,96},{8,104},{16,112},{24,120},{32,0},{40,8},{48,16},{56,24},{64... | collective-permute-start | bytes 393224 | tf_op jit(solution)/shard_map/ppermute | solution.py:412
  10.5 1.3 %collective-permute-start.3 = (bf16[512,128]{1,0:T(8,128)(2,1)S(1)}, bf16[512,128]{1,0:T(8,128)(2,1)S(1)}, u32[]{:S(2)}, u32[]{:S(2)}) collective-permute-start(bf16[512,128]{1,0:T(8,128)(2,1)S(1)} %constant_dynamic-update-slice_fusion.refs_0_), channel_id=1, source_target_pairs={{0,32},{8,40},{16,48},{24,56},{32,64},{40,72},{48,80},{56,88},{64,... | collective-permute-start | bytes 393224 | tf_op jit(solution)/shard_map/ppermute | solution.py:412
  11.7 6.8 %all-to-all-start = ((bf16[8,16,3456]{2,1,0:T(8,128)(2,1)}), bf16[8,16,3456]{2,1,0:T(8,128)(2,1)S(1)}, u32[]{:S(2)}, u32[]{:S(2)}) async-start(bf16[8,16,3456]{2,1,0:T(8,128)(2,1)} %get-tuple-element.46), calls=%async_computation | async-start | bytes 1769472 | tf_op jit(solution)/shard_map/all_to_all | solution.py:445
  18.6 0.5 collective-permute-start.8
  19.2 0.4 collective-permute-start.4
  19.7 5.7 %shard_map.182 = (bf16[1536,128]{1,0:T(8,128)(2,1)S(1)}, bf16[1536,128]{1,0:T(8,128)(2,1)S(1)}, f32[1,1536]{1,0:T(1,128)S(1)}, f32[1,1536]{1,0:T(1,128)S(1)}, f3...) custom-call(s32[32]{0:T(128)S(1)} %copy-done.4, ...), custom_call_target="tpu_custom_call" | custom-call | flops 6600000000 | tf_op jit(solution)/shard_map/pallas_call | solution.py:454
  25.5 5.6 %shard_map.183 = (f32[4,256,256]{2,1,0:T(8,128)}, bf16[128,1536]{1,0:T(8,128)(2,1)}) custom-call(s32[32]{0:T(128)S(1)} %copy-done.4, bf16[512,128]{1,0:T(8,128)(2,1)S(1)} %collective-permute-done.2.refs_0_, bf16[512,128]{1,0:T(8,128)(2,1)S(1)} %collective-permute-done.4.refs_1_, bf16[512,128]{1,0:T(8,128)(2,1)S(1)} %collective-permute-done.6.refs_2_, ...), custom_call_target="tpu_custom_call" | custom-call | flops 6600000000 | tf_op jit(solution)/shard_map/pallas_call | solution.py:454
  31.4 5.1 %shard_map.185 = (bf16[4,256,256]{2,1,0:T(8,128)(2,1)S(1)}, f32[128,1536]{1,0:T(8,128)S(1)}, bf16[1536,128]{1,0:T(8,128)(2,1)S(1)}, bf16[1536,128]{1,0:T(8,128)(...) custom-call(bf16[128,3456]{1,0:T(8,128)(2,1)S(1)} %bitcast.2, ...), custom_call_target="tpu_custom_call" | custom-call | flops 5280000000 | tf_op jit(solution)/shard_map/pallas_call | solution.py:471
  36.7 1.7 %shard_map.186 = (f32[2,128,256]{2,1,0:T(8,128)S(1)}, bf16[128,256]{1,0:T(8,128)(2,1)S(1)}, f32[128,1536]{1,0:T(8,128)S(1)}) custom-call(bf16[1536,128]{1,0:T(8,128)(2,1)S(1)} %get-tuple-element.48.qs_ref, bf16[1536,128]{1,0:T(8,128)(2,1)S(1)} %get-tuple-element.49.dos_ref, f32[1,1536]{1,0:T(1,128)S(1)} %get-tuple-element.50.lse_ref, ...), custom_call_target="tpu_custom_call" | custom-call | flops 2200000000 | tf_op jit(solution)/shard_map/pallas_call | solution.py:49
  38.6 2.1 %shard_map.187 = (bf16[4,128,256]{2,1,0:T(8,128)(2,1)S(1)}, f32[128,1536]{1,0:T(8,128)S(1)}) custom-call(bf16[1536,128]{1,0:T(8,128)(2,1)S(1)} %get-tuple-element.48.qs_ref, bf16[1536,128]{1,0:T(8,128)(2,1)S(1)} %get-tuple-element.49.dos_ref, f32[1,1536]{1,0:T(1,128)S(1)} %get-tuple-element.50.lse_ref, f32[1,1536]{1,0:T(1,128)S(1)} %get-tuple-element.51.delta_ref, ...), custom_call_target="tpu_custom_call" | custom-call | flops 2420000000 | tf_op jit(solution)/shard_map/pallas_call | solution.py:49
  40.6 0.9 %collective-permute-start.10 = (bf16[4,128,256]{2,1,0:T(8,128)(2,1)S(1)}, bf16[4,128,256]{2,1,0:T(8,128)(2,1)S(1)}, u32[]{:S(2)}, u32[]{:S(2)}) collective-permute-start(bf16[4,128,256]{2,1,0:T(8,128)(2,1)S(1)} %get-tuple-element.62), channel_id=1, source_target_pairs={{0,16},{8,24},{16,0},{24,8},{32,48},{40,56},{48,32},{56,40},{64,80... | collective-permute-start | bytes 786440 | tf_op jit(solution)/shard_map/ppermute | solution.py:409
  41.5 1.9 %shard_map.188 = (f32[4,128,256]{2,1,0:T(8,128)S(1)}, bf16[8,16,1792]{2,1,0:T(8,128)(2,1)}) custom-call(bf16[1536,128]{1,0:T(8,128)(2,1)S(1)} %get-tuple-element.48.qs_ref, bf16[1536,128]{1,0:T(8,128)(2,1)S(1)} %get-tuple-element.49.dos_ref, f32[1,1536]{1,0:T(1,128)S(1)} %get-tuple-element.50.lse_ref, f32[1,1536]{1,0:T(1,128)S(1)} %get-tuple-element.51.delta_ref, ...), custom_call_target="tpu_custom_call" | custom-call | flops 2200000000 | tf_op jit(solution)/shard_map/pallas_call | solution.py:491
  43.5 7.0 %all-to-all-start.1 = ((bf16[8,16,1792]{2,1,0:T(8,128)(2,1)}), bf16[8,16,1792]{2,1,0:T(8,128)(2,1)S(1)}, u32[]{:S(2)}, u32[]{:S(2)}) async-start(bf16[8,16,1792]{2,1,0:T(8,128)(2,1)} %get-tuple-element.60), calls=%async_computation.1 | async-start | bytes 917504 | tf_op jit(solution)/shard_map/all_to_all | solution.py:500
  50.5 2.0 %collective-permute-start.11 = (bf16[128,256]{1,0:T(8,128)(2,1)S(1)}, bf16[128,256]{1,0:T(8,128)(2,1)S(1)}, u32[]{:S(2)}, u32[]{:S(2)}) collective-permute-start(bf16[128,256]{1,0:T(8,128)(2,1)S(1)} %get-tuple-element.64), channel_id=1, source_target_pairs={{0,96},{8,104},{16,112},{24,120},{32,0},{40,8},{48,16},{56,24},{64... | collective-permute-start | bytes 196616 | tf_op jit(solution)/shard_map/ppermute | solution.py:412
  52.6 2.3 %collective-permute-start.12 = (bf16[128,256]{1,0:T(8,128)(2,1)S(1)}, bf16[128,256]{1,0:T(8,128)(2,1)S(1)}, u32[]{:S(2)}, u32[]{:S(2)}) collective-permute-start(bf16[128,256]{1,0:T(8,128)(2,1)S(1)} %get-tuple-element.65), channel_id=1, source_target_pairs={{0,64},{8,72},{16,80},{24,88},{32,96},{40,104},{48,112},{56,120},{... | collective-permute-start | bytes 196616 | tf_op jit(solution)/shard_map/ppermute | solution.py:412
  54.9 0.9 %shard_map.184 = bf16[128,1536]{1,0:T(8,128)(2,1)} custom-call(bf16[128,1536]{1,0:T(8,128)(2,1)S(1)} %copy-done.7), custom_call_target="tpu_custom_call" | custom-call | flops 2200000000 | tf_op jit(solution)/shard_map/pallas_call | solution.py:49
  55.8 2.7 %collective-permute-done.12.refs_1_ = bf16[128,256]{1,0:T(8,128)(2,1)S(1)} collective-permute-done((bf16[128,256]{1,0:T(8,128)(2,1)S(1)}, bf16[128,256]{1,0:T(8,128)(2,1)S(1)}, u32[]{:S(2)}, u32[]{:S(2)}) %collective-permute-start.12) | collective-permute-done | bytes 65568 | tf_op jit(solution)/shard_map/ppermute | solution.py:412
  58.5 1.8 %collective-permute-done.13.refs_2_ = bf16[128,256]{1,0:T(8,128)(2,1)S(1)} collective-permute-done((bf16[128,256]{1,0:T(8,128)(2,1)S(1)}, bf16[128,256]{1,0:T(8,128)(2,1)S(1)}, u32[]{:S(2)}, u32[]{:S(2)}) %collective-permute-start.13) | collective-permute-done | bytes 65568 | tf_op jit(solution)/shard_map/ppermute | solution.py:412
  60.3 0.7 %all-to-all-done.1.back_ref = bf16[8,16,1792]{2,1,0:T(8,128)(2,1)S(1)} async-done(((bf16[8,16,1792]{2,1,0:T(8,128)(2,1)}), bf16[8,16,1792]{2,1,0:T(8,128)(2,1)S(1)}, u32[]{:S(2)}, u32[]{:S(2)}) %all-to-all-start.1) | async-done | bytes 458784 | tf_op jit(solution)/shard_map/all_to_all | solution.py:500
  61.0 0.8 %shard_map.190 = (bf16[16,12288]{1,0:T(8,128)(2,1)}, bf16[16,1024]{1,0:T(8,128)(2,1)}, bf16[16,1024]{1,0:T(8,128)(2,1)}, bf16[128,128]{1,0:T(8,128)(2,1)}, bf16[128,128]{1,0:T(8,128)(2,1)}) custom-call(bf16[8,16,1792]{2,1,0:T(8,128)(2,1)S(1)} %all-to-all-done.1.back_ref, f32[128,256]{1,0:T(8,128)S(1)} %get-tuple-element.63.keep_ref, ...), custom_call_target="tpu_custom_call" | custom-call | flops 880000000 | tf_op jit(solution)/shard_map/pallas_call | solution.py:49
  (36 shorter events, 1.0 us)
Async XLA Ops:
  0.6 5.0 %collective-permute-start = (bf16[128,128]{1,0:T(8,128)(2,1)}, bf16[128,128]{1,0:T(8,128)(2,1)S(1)}, u32[]{:S(2)}, u32[]{:S(2)}) collective-permute-start(bf16[128,128]{1,0:T(8,128)(2,1)} %dk_ref.1), channel_id=1, source_target_pairs={{0,16},{8,24},{16,0},{24,8},{32,48},{40,56},{48,32},{56,40},{64,80... | collective-permute-start | bytes 98312 | tf_op jit(solution)/shard_map/ppermute | solution.py:409
  2.3 4.1 %collective-permute-start.1 = (bf16[128,128]{1,0:T(8,128)(2,1)}, bf16[128,128]{1,0:T(8,128)(2,1)S(1)}, u32[]{:S(2)}, u32[]{:S(2)}) collective-permute-start(bf16[128,128]{1,0:T(8,128)(2,1)} %dv_ref.1), channel_id=1, source_target_pairs={{0,16},{8,24},{16,0},{24,8},{32,48},{40,56},{48,32},{56,40},{64,80... | collective-permute-start | bytes 98312 | tf_op jit(solution)/shard_map/ppermute | solution.py:409
  6.4 12.2 %collective-permute-start.7 = (bf16[512,128]{1,0:T(8,128)(2,1)S(1)}, bf16[512,128]{1,0:T(8,128)(2,1)S(1)}, u32[]{:S(2)}, u32[]{:S(2)}) collective-permute-start(bf16[512,128]{1,0:T(8,128)(2,1)S(1)} %constant_dynamic-update-slice_fusion.refs_0_), channel_id=1, source_target_pairs={{0,96},{8,104},{16,112},{24,120},{32,0},{40,8},{48,16},{56,24},{64... | collective-permute-start | bytes 393224 | tf_op jit(solution)/shard_map/ppermute | solution.py:412
  10.5 8.7 %collective-permute-start.5 = (bf16[512,128]{1,0:T(8,128)(2,1)S(1)}, bf16[512,128]{1,0:T(8,128)(2,1)S(1)}, u32[]{:S(2)}, u32[]{:S(2)}) collective-permute-start(bf16[512,128]{1,0:T(8,128)(2,1)S(1)} %constant_dynamic-update-slice_fusion.refs_0_), channel_id=1, source_target_pairs={{0,64},{8,72},{16,80},{24,88},{32,96},{40,104},{48,112},{56,120},{... | collective-permute-start | bytes 393224 | tf_op jit(solution)/shard_map/ppermute | solution.py:412
  10.5 8.8 %collective-permute-start.3 = (bf16[512,128]{1,0:T(8,128)(2,1)S(1)}, bf16[512,128]{1,0:T(8,128)(2,1)S(1)}, u32[]{:S(2)}, u32[]{:S(2)}) collective-permute-start(bf16[512,128]{1,0:T(8,128)(2,1)S(1)} %constant_dynamic-update-slice_fusion.refs_0_), channel_id=1, source_target_pairs={{0,32},{8,40},{16,48},{24,56},{32,64},{40,72},{48,80},{56,88},{64,... | collective-permute-start | bytes 393224 | tf_op jit(solution)/shard_map/ppermute | solution.py:412
  11.7 7.9 %copy-start = (bf16[128,1536]{1,0:T(8,128)(2,1)S(1)}, bf16[128,1536]{1,0:T(8,128)(2,1)}, u32[]{:S(2)}) copy-start(bf16[128,1536]{1,0:T(8,128)(2,1)} %refs_4_.1) | copy-start | bytes 1179652
  11.7 7.9 %copy-start.1 = (bf16[128,1536]{1,0:T(8,128)(2,1)S(1)}, bf16[128,1536]{1,0:T(8,128)(2,1)}, u32[]{:S(2)}) copy-start(bf16[128,1536]{1,0:T(8,128)(2,1)} %refs_5_.1) | copy-start | bytes 1179652
  11.7 7.9 %copy-start.2 = (bf16[128,1536]{1,0:T(8,128)(2,1)S(1)}, bf16[128,1536]{1,0:T(8,128)(2,1)}, u32[]{:S(2)}) copy-start(bf16[128,1536]{1,0:T(8,128)(2,1)} %refs_6_.1) | copy-start | bytes 1179652
  11.7 7.9 %copy-start.3 = (f32[128,12]{0,1:T(8,128)S(1)}, f32[128,12]{0,1:T(8,128)}, u32[]{:S(2)}) copy-start(f32[128,12]{0,1:T(8,128)} %param.21) | copy-start | bytes 18436
  11.7 19.7 %all-to-all-start = ((bf16[8,16,3456]{2,1,0:T(8,128)(2,1)}), bf16[8,16,3456]{2,1,0:T(8,128)(2,1)S(1)}, u32[]{:S(2)}, u32[]{:S(2)}) async-start(bf16[8,16,3456]{2,1,0:T(8,128)(2,1)} %get-tuple-element.46), calls=%async_computation | async-start | bytes 1769472 | tf_op jit(solution)/shard_map/all_to_all | solution.py:445
  18.5 1.1 %copy-start.4 = (s32[32]{0:T(128)S(1)}, s32[32]{0:T(128)}, u32[]{:S(2)}) copy-start(s32[32]{0:T(128)} %order_ref.3) | copy-start | bytes 388
  18.5 6.9 %collective-permute-start.2 = (bf16[512,128]{1,0:T(8,128)(2,1)S(1)}, bf16[512,128]{1,0:T(8,128)(2,1)S(1)}, u32[]{:S(2)}, u32[]{:S(2)}) collective-permute-start(bf16[512,128]{1,0:T(8,128)(2,1)S(1)} %constant_dynamic-update-slice_fusion.refs_0_), channel_id=1, source_target_pairs={{0,8},{8,0},{16,24},{24,16},{32,40},{40,32},{48,56},{56,48},{64,72... | collective-permute-start | bytes 393224 | tf_op jit(solution)/shard_map/ppermute | solution.py:406
  18.6 6.8 %collective-permute-start.8 = (bf16[512,128]{1,0:T(8,128)(2,1)S(1)}, bf16[512,128]{1,0:T(8,128)(2,1)S(1)}, u32[]{:S(2)}, u32[]{:S(2)}) collective-permute-start(bf16[512,128]{1,0:T(8,128)(2,1)S(1)} %collective-permute-done.7.refs_3_.refs_1_), channel_id=1, source_target_pairs={{0,8},{8,0},{16,24},{24,16},{32,40},{40,32},{48,56},{56,48},{64,72... | collective-permute-start | bytes 393224 | tf_op jit(solution)/shard_map/ppermute | solution.py:406
  19.1 6.3 %collective-permute-start.6 = (bf16[512,128]{1,0:T(8,128)(2,1)S(1)}, bf16[512,128]{1,0:T(8,128)(2,1)S(1)}, u32[]{:S(2)}, u32[]{:S(2)}) collective-permute-start(bf16[512,128]{1,0:T(8,128)(2,1)S(1)} %collective-permute-done.5.refs_2_.refs_0_), channel_id=1, source_target_pairs={{0,8},{8,0},{16,24},{24,16},{32,40},{40,32},{48,56},{56,48},{64,72... | collective-permute-start | bytes 393224 | tf_op jit(solution)/shard_map/ppermute | solution.py:406
  19.2 6.2 %collective-permute-start.4 = (bf16[512,128]{1,0:T(8,128)(2,1)S(1)}, bf16[512,128]{1,0:T(8,128)(2,1)S(1)}, u32[]{:S(2)}, u32[]{:S(2)}) collective-permute-start(bf16[512,128]{1,0:T(8,128)(2,1)S(1)} %collective-permute-done.3.refs_1_), channel_id=1, source_target_pairs={{0,8},{8,0},{16,24},{24,16},{32,40},{40,32},{48,56},{56,48},{64,72... | collective-permute-start | bytes 393224 | tf_op jit(solution)/shard_map/ppermute | solution.py:406
  36.6 2.0 %collective-permute-start.9 = (bf16[4,256,256]{2,1,0:T(8,128)(2,1)S(1)}, bf16[4,256,256]{2,1,0:T(8,128)(2,1)S(1)}, u32[]{:S(2)}, u32[]{:S(2)}) collective-permute-start(bf16[4,256,256]{2,1,0:T(8,128)(2,1)S(1)} %get-tuple-element.54), channel_id=1, source_target_pairs={{0,8},{8,0},{16,24},{24,16},{32,40},{40,32},{48,56},{56,48},{64,72... | collective-permute-start | bytes 1572872 | tf_op jit(solution)/shard_map/ppermute | solution.py:406
  36.7 1.9 %copy-start.6 = (f32[4,128,256]{2,1,0:T(8,128)S(1)}, f32[4,128,256]{2,1,0:T(8,128)}, u32[]{:S(2)}) copy-start(f32[4,128,256]{2,1,0:T(8,128)} %get-tuple-element.55.refs_4_) | copy-start | bytes 1572868
  38.6 3.0 %copy-start.5 = (f32[4,128,256]{2,1,0:T(8,128)S(1)}, f32[4,128,256]{2,1,0:T(8,128)}, u32[]{:S(2)}) copy-start(f32[4,128,256]{2,1,0:T(8,128)} %get-tuple-element.59.doc_ref) | copy-start | bytes 1572868
  40.6 9.8 %collective-permute-start.10 = (bf16[4,128,256]{2,1,0:T(8,128)(2,1)S(1)}, bf16[4,128,256]{2,1,0:T(8,128)(2,1)S(1)}, u32[]{:S(2)}, u32[]{:S(2)}) collective-permute-start(bf16[4,128,256]{2,1,0:T(8,128)(2,1)S(1)} %get-tuple-element.62), channel_id=1, source_target_pairs={{0,16},{8,24},{16,0},{24,8},{32,48},{40,56},{48,32},{56,40},{64,80... | collective-permute-start | bytes 786440 | tf_op jit(solution)/shard_map/ppermute | solution.py:409
  43.5 17.6 %all-to-all-start.1 = ((bf16[8,16,1792]{2,1,0:T(8,128)(2,1)}), bf16[8,16,1792]{2,1,0:T(8,128)(2,1)S(1)}, u32[]{:S(2)}, u32[]{:S(2)}) async-start(bf16[8,16,1792]{2,1,0:T(8,128)(2,1)} %get-tuple-element.60), calls=%async_computation.1 | async-start | bytes 917504 | tf_op jit(solution)/shard_map/all_to_all | solution.py:500
  50.4 4.4 %copy-start.7 = (bf16[128,1536]{1,0:T(8,128)(2,1)S(1)}, bf16[128,1536]{1,0:T(8,128)(2,1)}, u32[]{:S(2)}) copy-start(bf16[128,1536]{1,0:T(8,128)(2,1)} %get-tuple-element.45.turned_ref) | copy-start | bytes 1179652
  50.5 5.3 %collective-permute-start.11 = (bf16[128,256]{1,0:T(8,128)(2,1)S(1)}, bf16[128,256]{1,0:T(8,128)(2,1)S(1)}, u32[]{:S(2)}, u32[]{:S(2)}) collective-permute-start(bf16[128,256]{1,0:T(8,128)(2,1)S(1)} %get-tuple-element.64), channel_id=1, source_target_pairs={{0,96},{8,104},{16,112},{24,120},{32,0},{40,8},{48,16},{56,24},{64... | collective-permute-start | bytes 196616 | tf_op jit(solution)/shard_map/ppermute | solution.py:412
  52.6 6.0 %collective-permute-start.12 = (bf16[128,256]{1,0:T(8,128)(2,1)S(1)}, bf16[128,256]{1,0:T(8,128)(2,1)S(1)}, u32[]{:S(2)}, u32[]{:S(2)}) collective-permute-start(bf16[128,256]{1,0:T(8,128)(2,1)S(1)} %get-tuple-element.65), channel_id=1, source_target_pairs={{0,64},{8,72},{16,80},{24,88},{32,96},{40,104},{48,112},{56,120},{... | collective-permute-start | bytes 196616 | tf_op jit(solution)/shard_map/ppermute | solution.py:412
  54.9 5.5 %collective-permute-start.13 = (bf16[128,256]{1,0:T(8,128)(2,1)S(1)}, bf16[128,256]{1,0:T(8,128)(2,1)S(1)}, u32[]{:S(2)}, u32[]{:S(2)}) collective-permute-start(bf16[128,256]{1,0:T(8,128)(2,1)S(1)} %get-tuple-element.66), channel_id=1, source_target_pairs={{0,32},{8,40},{16,48},{24,56},{32,64},{40,72},{48,80},{56,88},{64,... | collective-permute-start | bytes 196616 | tf_op jit(solution)/shard_map/ppermute | solution.py:412

commit v5 on v4

--- a/solution.py
+++ b/solution.py
@@ -109,7 +109,7 @@
 
 
 def pack_kernel(heads, groups, total, len_hbm, do_ref, o_ref, q_ref, k_ref, v_ref, ex_ref, dk_ref, dv_ref, pay_ref, kv_ref, *refs):
-    grad, out, query, keys, values, buf, len_ref, packed, high, low, sems = refs
+    grad, out, query, keys, values, buf, len_ref, block, high, low, sems = refs
     rows = out.shape[0]
     wide = heads * D
     pairs = (
@@ -121,20 +121,21 @@
         load.start()
     sends = []
 
-    def send(source, to, size):
+    def send(to, size):
+        cut = (slice(None), slice(None), pl.ds(to, size))
+        sends.append(pltpu.make_async_copy(block.at[cut], pay_ref.at[cut], sems.at[len(pairs) + len(sends)]))
+        sends[-1].start()
+
+    def place(source, to, size):
         for g in range(groups):
-            part = pay_ref.at[g, :, pl.ds(to, size)]
-            sends.append(pltpu.make_async_copy(source.at[:, pl.ds(g * size, size)], part, sems.at[len(pairs) + len(sends)]))
-            sends[-1].start()
+            block[g, :, to : to + size] = source[:, g * size : (g + 1) * size]
 
     loads[0].wait()
-    send(grad, wide, wide)
+    place(grad, wide, wide)
+    send(wide, wide)
     loads[2].wait()
-    send(query, 0, wide)
-    loads[3].wait()
-    send(keys, 2 * wide, D)
-    loads[4].wait()
-    send(values, 2 * wide + D, D)
+    place(query, 0, wide)
+    send(0, wide)
     loads[1].wait()
     for g in range(groups):
         cut, at = slice(g * wide, (g + 1) * wide), slice(g * rows, (g + 1) * rows)
@@ -159,9 +160,12 @@
                 value = value - part
                 at = (3 * n + m) * 16
                 stats = stats + (pltpu.roll(part, at, 1) if at else part)
-        packed[g] = jnp.where(lane == 96, (row - within).astype(F32), stats).astype(BF)
-    sends.append(pltpu.make_async_copy(packed, pay_ref.at[:, :, pl.ds(2 * wide + 2 * D, D)], sems.at[len(pairs) + len(sends)]))
-    sends[-1].start()
+        block[g, :, 2 * wide + 2 * D :] = jnp.where(lane == 96, (row - within).astype(F32), stats).astype(BF)
+    loads[3].wait()
+    loads[4].wait()
+    place(keys, 2 * wide, D)
+    place(values, 2 * wide + D, D)
+    send(2 * wide, 3 * D)
     for copy in loads[7:] + sends:
         copy.wait()
 
@@ -169,7 +173,7 @@
 def doc_keys(order_ref, me, ctx_size, piece):
     core, z = piece
     place, low, step = me // 4, (me // 2) % 2, ctx_size // 4
-    depth = lax.rem(place + step - z, step)
+    depth = lax.rem(place + z, step)
     return [(depth * 2 + (low ^ x if isinstance(low, int) else lax.bitwise_xor(low, x))) * 2 + lax.bitwise_xor(lax.rem(me, 2), core) for x in range(2)]
 
 
@@ -184,16 +188,19 @@
 
 def doc_kernel(core, heads, ctx_size, order_ref, *refs):
     kv_refs, refs = refs[:4], refs[4:]
-    if core == 0:
-        q_ref, o_ref, do_ref, ex_ref, *state, dq_ref, near_hbm, own_hbm, near_ref, own_ref, sems = refs
-    else:
-        *state, dq_in, far_hbm, dq_hbm, far_ref, dq_ref, sems = refs
-    qs_ref, dos_ref, lse_ref, delta_ref = state
     stores = []
 
     def store(source, to):
         stores.append(pltpu.make_async_copy(source, to, sems.at[len(stores)]))
         stores[-1].start()
+
+    if core == 0:
+        q_ref, o_ref, do_ref, ex_ref, *state, dq_ref, near_ref, own_ref = refs
+    else:
+        *state, dq_in, near_ref, own_ref, far_hbm, dq_hbm, near_hbm, own_hbm, far_ref, dq_ref, sems = refs
+        store(near_ref, near_hbm)
+        store(own_ref, own_hbm)
+    qs_ref, dos_ref, lse_ref, delta_ref = state
 
     me = lax.axis_index("ctx")
     rows = heads * D
@@ -228,15 +235,11 @@
                 own_ref[depth, :, cut] = grad[:D]
                 near_ref[depth, :, cut] = grad[D:]
             else:
-                far_ref[depth, :, cut] = grad
+                far_ref[depth, :, cut] = grad.astype(BF)
         total = dq if total is None else total + dq
-        if depth % 2 == 1:
+        if core == 1 and depth % 2 == 1:
             done = pl.ds(depth - 1, 2)
-            if core == 0:
-                store(own_ref.at[done], own_hbm.at[done])
-                store(near_ref.at[done], near_hbm.at[done])
-            else:
-                store(far_ref.at[done], far_hbm.at[done])
+            store(far_ref.at[done], far_hbm.at[done])
     if core == 0:
         dq_ref[...] = total
     else:
@@ -252,12 +255,7 @@
 
 
 def far_kernel(heads, pay_ref, *refs):
-    kv_refs, doc_hbm = refs[:4], refs[4]
-    send_ref, dq_ref, qs_ref, dos_ref, lse_ref, delta_ref, doc_ref, sems = refs[5:]
-    parts = (pl.ds(0, 1), pl.ds(1, 3))
-    loads = [pltpu.make_async_copy(doc_hbm.at[at], doc_ref.at[at], sems.at[n]) for n, at in enumerate(parts)]
-    for load in loads:
-        load.start()
+    kv_refs, (send_ref, dq_ref, qs_ref, dos_ref, lse_ref, delta_ref) = refs[:4], refs[4:]
     wide = heads * D
     stack_heads(pay_ref, qs_ref, heads, 0)
     stack_heads(pay_ref, dos_ref, heads, wide)
@@ -268,10 +266,8 @@
     total = None
     for n in range(4):
         dq, dk, dv = pair_block(qs_ref, dos_ref, *both(kv_refs[n]), lse, delta, None)
-        if n < 2:
-            loads[n].wait()
-        send_ref[n, :, :D] = (dk + doc_ref[n, :, :D]).astype(BF)
-        send_ref[n, :, D:] = (dv + doc_ref[n, :, D:]).astype(BF)
+        send_ref[n, :, :D] = dk.astype(BF)
+        send_ref[n, :, D:] = dv.astype(BF)
         total = dq if total is None else total + dq
     dq_ref[...] = total
 
@@ -290,12 +286,12 @@
     return total
 
 
-def near_kernel(qs_ref, dos_ref, lse_ref, delta_ref, dq_in, core_ref, *refs):
+def near_kernel(qs_ref, dos_ref, lse_ref, delta_ref, dq_in, core_ref, core_doc_ref, *refs):
     kv_refs, doc_ref = refs[:4], refs[4]
     send_ref, dq_ref = refs[5:]
 
     def store(n, cut, grad):
-        send_ref[n, :, cut] = (grad + doc_ref[n, :, cut] + core_ref[n, D:, cut].astype(F32)).astype(BF)
+        send_ref[n, :, cut] = (grad + doc_ref[n, :, cut] + core_ref[n, D:, cut].astype(F32) + core_doc_ref[n, D:, cut].astype(F32)).astype(BF)
 
     dq_ref[...] = column(1, qs_ref, dos_ref, lse_ref[...], delta_ref[...], kv_refs, dq_in[...], store)
 
@@ -322,7 +318,7 @@
     dq_ref[...] = column(0, qs_ref, dos_ref, lse, delta, kv_refs, dq_in[...] + dq, store)
 
 
-def last_kernel(heads, groups, qs_ref, dos_ref, lse_ref, delta_ref, dq_in, self_ref, low_ref, core_ref, doc_ref, *refs):
+def last_kernel(heads, groups, qs_ref, dos_ref, lse_ref, delta_ref, dq_in, self_ref, low_ref, core_ref, core_doc_ref, doc_ref, *refs):
     kv_refs = refs[:2]
     out_ref, back_hbm, back_ref, sems = refs[2:]
     wide = heads * D
@@ -339,7 +335,7 @@
     send(wide, 2 * D)
 
     def other(n, cut):
-        return doc_ref[n, :, cut] + core_ref[n, :D, cut].astype(F32)
+        return doc_ref[n, :, cut] + core_ref[n, :D, cut].astype(F32) + core_doc_ref[n, :D, cut].astype(F32)
 
     def store(n, cut, grad):
         out_ref[n + 2, :, cut] = grad + other(n + 2, cut)
@@ -424,8 +420,8 @@
         in_specs=[hbm()] * 9,
         out_specs=(hbm(), vmem()),
         scratch_shapes=[asking, asking, asking, narrow, narrow, pltpu.VMEM((each, heads * groups), F32)]
-        + [pltpu.SMEM(question_lengths.shape, jnp.int32), pltpu.VMEM((groups, each, D), BF), both_parts, both_parts]
-        + [pltpu.SemaphoreType.DMA((10 + 4 * groups,))],
+        + [pltpu.SMEM(question_lengths.shape, jnp.int32), pltpu.VMEM((groups, each, 2 * wide + 3 * D), BF), both_parts, both_parts]
+        + [pltpu.SemaphoreType.DMA((12,))],
         compiler_params=SHARED,
         cost_estimate=cost(5),
     )(
@@ -440,43 +436,37 @@
     here = kv
     for n, part in enumerate(chip):
         here = lax.dynamic_update_slice(here, part, ((2 + n) * rows, 0))
-    mine = [here] + [along_z(here, d) for d in range(1, depth)]
+    mine = [here] + [along_z(here, depth - d) for d in range(1, depth)]
     theirs = [other_core(piece) for piece in mine]
     asked = lax.all_to_all(payload, "head", 0, 0, tiled=True).reshape(groups * each, -1)
 
     quarter = ((depth, rows, 2 * D), F32)
-    double = ((depth, 2 * rows, 2 * D), F32)
+    double = ((depth, 2 * rows, 2 * D), BF)
     row_state = [((stacked, D), BF), ((stacked, D), BF), ((1, stacked), F32), ((1, stacked), F32)]
     query_sum = ((D, stacked), F32)
     flat = ((rows, wide), BF)
 
-    def document(core, outs, partial, *args):
-        return pl.pallas_call(
-            functools.partial(doc_kernel, core, heads, ctx_size),
-            out_shape=tuple(jax.ShapeDtypeStruct(*out) for out in outs) + tuple(pltpu.HBM(*out) for out in partial),
-            in_specs=[smem()] + [vmem()] * (len(args) - 1),
-            out_specs=(vmem(),) * len(outs) + (hbm(),) * len(partial),
-            scratch_shapes=[pltpu.VMEM(*out) for out in partial] + [pltpu.SemaphoreType.DMA((8,))],
-            compiler_params=SHARED,
-            cost_estimate=cost(6),
-        )(*args)
-
-    *doc_state, dq, near_doc, own_doc = document(
-        0,
-        row_state + [query_sum],
-        [quarter, quarter],
+    *doc_state, dq, near_doc, own_doc = call(
+        6,
+        functools.partial(doc_kernel, 0, heads, ctx_size),
+        row_state + [query_sum, quarter, quarter],
+        1,
         block_order, *mine, document_query_matrix, document_output, document_outgrad, document_excess.T,
     )
-    far_doc, doc_turned = document(1, [], [double, ((D, stacked), BF)], block_order, *theirs, *doc_state, dq)
-    far, dq, *state = pl.pallas_call(
-        functools.partial(far_kernel, heads),
-        out_shape=tuple(jax.ShapeDtypeStruct(*out) for out in [((depth, 2 * rows, 2 * D), BF), query_sum] + row_state),
-        in_specs=[vmem()] * 5 + [hbm()],
-        out_specs=(vmem(),) * 6,
-        scratch_shapes=[pltpu.VMEM(*double), pltpu.SemaphoreType.DMA((2,))],
+    turned = ((D, stacked), BF)
+    far_doc, doc_turned, near_doc, own_doc = pl.pallas_call(
+        functools.partial(doc_kernel, 1, heads, ctx_size),
+        out_shape=tuple(pltpu.HBM(*out) for out in (double, turned, quarter, quarter)),
+        in_specs=[smem()] + [vmem()] * 11,
+        out_specs=(hbm(),) * 4,
+        scratch_shapes=[pltpu.VMEM(*double), pltpu.VMEM(*turned), pltpu.SemaphoreType.DMA((5,))],
         compiler_params=SHARED,
-        cost_estimate=cost(4.8),
-    )(asked, *theirs, pltpu.with_memory_space_constraint(far_doc, pltpu.HBM))
+        cost_estimate=cost(6),
+    )(block_order, *theirs, *doc_state, dq, near_doc, own_doc)
+    core_doc = other_core(far_doc)
+    far, dq, *state = call(
+        4.8, functools.partial(far_kernel, heads), [double, query_sum] + row_state, 0, asked, *theirs
+    )
     core_sum = other_core(far)
     low, own_self, dq = call(
         2,
@@ -485,18 +475,18 @@
         0,
         *state, dq, asked, *mine[:2],
     )
-    near, dq = call(2.2, near_kernel, [((depth, rows, 2 * D), BF), query_sum], 0, *state, dq, core_sum, *mine, near_doc)
+    near, dq = call(2.2, near_kernel, [((depth, rows, 2 * D), BF), query_sum], 0, *state, dq, core_sum, core_doc, *mine, near_doc)
     chip_sum = other_chip(near)
     returned = ((groups, each, wide + 2 * D), BF)
     own, back = pl.pallas_call(
         functools.partial(last_kernel, heads, groups),
         out_shape=(jax.ShapeDtypeStruct(*quarter), pltpu.HBM(*returned)),
-        in_specs=[vmem()] * 11,
+        in_specs=[vmem()] * 12,
         out_specs=(vmem(), hbm()),
         scratch_shapes=[pltpu.VMEM(*returned), pltpu.SemaphoreType.DMA((4,))],
         compiler_params=SHARED,
         cost_estimate=cost(2),
-    )(*state, dq, own_self, low, core_sum, own_doc, *mine[2:])
+    )(*state, dq, own_self, low, core_sum, core_doc, own_doc, *mine[2:])
     back = lax.all_to_all(back, "head", 0, 0, tiled=True)
     keep, *sends = call(
         25,
@@ -506,7 +496,7 @@
         own, chip_sum,
     )
     (document_query_grad,) = call(2, functools.partial(turn_kernel, heads), [flat], 0, doc_turned)
-    arrived = [along_z(send, depth - 1 - n) for n, send in enumerate(sends)]
+    arrived = [along_z(send, n + 1) for n, send in enumerate(sends)]
     question_query_grad, question_keys_grad, question_values_grad, document_keys_grad, document_values_grad = call(
         0.8,
         functools.partial(unpack_kernel, heads, groups),

time: 62.4 us -> 60.5 us (0.970)
  Pallas kernels: 26.8 us -> 24.4 us
  starting transfers between devices: 27.6 us -> 28.3 us
    pallas_call x3 -> x1, Pallas kernels: 16.5 us -> 5.38 us  [local(): pl.pallas_call(functools.partial(doc_kernel, 1, heads, ctx_size), out_sha...]
    pallas_call x5 -> x7, Pallas kernels: 5.49 us -> 14.3 us  [call(): pl.pallas_call(body, out_shape=tuple((jax.ShapeDtypeStruct(s, t) for s, t...]
    ppermute x6, waiting for transfers between devices: 4.58 us -> 2.11 us  [along_z(): lax.ppermute(x, 'ctx', [(i, (i + 4 * d) % ctx_size) for i in range(ctx_si...]
    all_to_all x1, waiting for transfers between devices: 0.68 us -> 2.46 us  [local(): back = lax.all_to_all(back, 'head', 0, 0, tiled=True)]
    ppermute x6, starting transfers between devices: 9.65 us -> 10.4 us  [along_z(): lax.ppermute(x, 'ctx', [(i, (i + 4 * d) % ctx_size) for i in range(ctx_si...]
    ppermute x5 -> x6, starting transfers between devices: 1.17 us -> 1.73 us  [other_core(): return lax.ppermute(x, 'ctx', [(i, i ^ 1) for i in range(ctx_size)])]
  transfers between devices with their start and end apart: 16 -> 17, of which waited for: 6 -> 5; matrix products, arithmetic and copies ran while one was open for 0% -> 0% of each run, Pallas kernels for 30% -> 36%
where the time goes in v5:
time: 60.5 us; the launch traced here: 60 us
  starting transfers between devices  28.3 us (47%)
  Pallas kernels  24.4 us (40%)
  waiting for transfers between devices  6.5 us (11%)
  between operations  0.83 us (1%)
    pallas_call x7, Pallas kernels, call(): pl.pallas_call(body, out_shape=tuple((jax.ShapeDtypeStruct(s, t) for s, t...  14.3 us
    ppermute x6, starting transfers between devices, along_z(): lax.ppermute(x, 'ctx', [(i, (i + 4 * d) % ctx_size) for i in range(ctx_si...  10.4 us
    all_to_all x1, starting transfers between devices, local(): lax.all_to_all(payload, 'head', 0, 0, tiled=True).reshape(groups * each, -1)  6.8 us
    all_to_all x1, starting transfers between devices, local(): back = lax.all_to_all(back, 'head', 0, 0, tiled=True)  6.41 us
    pallas_call x1, Pallas kernels, local(): pl.pallas_call(functools.partial(doc_kernel, 1, heads, ctx_size), out_sha...  5.38 us
    ppermute x3, starting transfers between devices, other_chip(): return lax.ppermute(x, 'ctx', [(i, i ^ 2) for i in range(ctx_size)])  2.98 us
    pallas_call x1, Pallas kernels, local(): pl.pallas_call(functools.partial(pack_kernel, heads, groups, total_doc),...  2.71 us
    all_to_all x1, waiting for transfers between devices, local(): back = lax.all_to_all(back, 'head', 0, 0, tiled=True)  2.46 us
  transfers between devices with their start and end apart: 17, of which 5 were waited for; matrix products, arithmetic and copies ran while one was open for 0% of the time, Pallas kernels for 36%

profile of v5, /device:TPU:0, one launch (start us, length us, event | category | flops | bytes accessed | tf_op | source)
XLA Modules:
  0.0 60.0 jit_solution(16399660962966147940)
XLA Ops:
  0.6 1.7 %collective-permute-start = (bf16[128,128]{1,0:T(8,128)(2,1)}, bf16[128,128]{1,0:T(8,128)(2,1)S(1)}, u32[]{:S(2)}, u32[]{:S(2)}) collective-permute-start(bf16[128,128]{1,0:T(8,128)(2,1)} %dk_ref.1), channel_id=1, source_target_pairs={{0,16},{8,24},{16,0},{24,8},{32,48},{40,56},{48,32},{56,40},{64,80... | collective-permute-start | bytes 98312 | tf_op jit(solution)/shard_map/ppermute | solution.py:405
  2.7 2.7 %shard_map.181 = (bf16[8,16,3456]{2,1,0:T(8,128)(2,1)}, bf16[512,128]{1,0:T(8,128)(2,1)S(1)}) custom-call(s32[1,2]{1,0:T(1,128)} %len_hbm.1, bf16[16,12288]{1,0:T(8,128)(2,1)} %do_ref.1, bf16[16,12288]{1,0:T(8,128)(2,1)} %o_ref.1, bf16[16,12288]{1,0:T(8,128)(2,1)} %q_ref.1, bf16[16,1024]{1,0:T(8,128)(2,1)} %k_ref.1, bf16[16,1024]{1,0:T(8,128)(2,1)} %v_ref.1, ...), custom_call_target="tpu_custom_call" | custom-call | flops 5500000256 | tf_op jit(solution)/shard_map/pallas_call | solution.py:414
  5.5 0.9 %collective-permute-done.1 = bf16[128,128]{1,0:T(8,128)(2,1)S(1)} collective-permute-done((bf16[128,128]{1,0:T(8,128)(2,1)}, bf16[128,128]{1,0:T(8,128)(2,1)S(1)}, u32[]{:S(2)}, u32[]{:S(2)}) %collective-permute-start.1) | collective-permute-done | bytes 32800 | tf_op jit(solution)/shard_map/ppermute | solution.py:405
  6.4 4.0 %collective-permute-start.3 = (bf16[512,128]{1,0:T(8,128)(2,1)S(1)}, bf16[512,128]{1,0:T(8,128)(2,1)S(1)}, u32[]{:S(2)}, u32[]{:S(2)}) collective-permute-start(bf16[512,128]{1,0:T(8,128)(2,1)S(1)} %constant_dynamic-update-slice_fusion.refs_0_), channel_id=1, source_target_pairs={{0,96},{8,104},{16,112},{24,120},{32,0},{40,8},{48,16},{56,24},{64... | collective-permute-start | bytes 393224 | tf_op jit(solution)/shard_map/ppermute | solution.py:408
  10.5 1.3 %collective-permute-start.7 = (bf16[512,128]{1,0:T(8,128)(2,1)S(1)}, bf16[512,128]{1,0:T(8,128)(2,1)S(1)}, u32[]{:S(2)}, u32[]{:S(2)}) collective-permute-start(bf16[512,128]{1,0:T(8,128)(2,1)S(1)} %constant_dynamic-update-slice_fusion.refs_0_), channel_id=1, source_target_pairs={{0,32},{8,40},{16,48},{24,56},{32,64},{40,72},{48,80},{56,88},{64,... | collective-permute-start | bytes 393224 | tf_op jit(solution)/shard_map/ppermute | solution.py:408
  11.7 6.8 %all-to-all-start = ((bf16[8,16,3456]{2,1,0:T(8,128)(2,1)}), bf16[8,16,3456]{2,1,0:T(8,128)(2,1)S(1)}, u32[]{:S(2)}, u32[]{:S(2)}) async-start(bf16[8,16,3456]{2,1,0:T(8,128)(2,1)} %get-tuple-element.50), calls=%async_computation | async-start | bytes 1769472 | tf_op jit(solution)/shard_map/all_to_all | solution.py:441
  18.6 0.5 collective-permute-start.4
  19.7 4.8 %shard_map.182 = (bf16[1536,128]{1,0:T(8,128)(2,1)S(1)}, bf16[1536,128]{1,0:T(8,128)(2,1)S(1)}, f32[1,1536]{1,0:T(1,128)S(1)}, f32[1,1536]{1,0:T(1,128)S(1)}, f3...) custom-call(s32[32]{0:T(128)S(1)} %copy-done.4, ...), custom_call_target="tpu_custom_call" | custom-call | flops 6600000000 | tf_op jit(solution)/shard_map/pallas_call | solution.py:49
  24.5 5.4 %shard_map.183 = (bf16[4,256,256]{2,1,0:T(8,128)(2,1)}, bf16[128,1536]{1,0:T(8,128)(2,1)}, f32[4,128,256]{2,1,0:T(8,128)}, f32[4,128,256]{2,1,0:T(8,128)}) custom-call(s32[32]{0:T(128)S(1)} %copy-done.4, bf16[512,128]{1,0:T(8,128)(2,1)S(1)} %collective-permute-done.2.refs_0_, bf16[512,128]{1,0:T(8,128)(2,1)S(1)} %collective-permute-done.4.refs_1_, ...), custom_call_target="tpu_custom_call" | custom-call | flops 6600000000 | tf_op jit(solution)/shard_map/pallas_call | solution.py:457
  29.9 0.6 collective-permute-start.10
  30.5 0.8 %all-to-all-done = bf16[8,16,3456]{2,1,0:T(8,128)(2,1)S(1)} async-done(((bf16[8,16,3456]{2,1,0:T(8,128)(2,1)}), bf16[8,16,3456]{2,1,0:T(8,128)(2,1)S(1)}, u32[]{:S(2)}, u32[]{:S(2)}) %all-to-all-start) | async-done | bytes 884768 | tf_op jit(solution)/shard_map/all_to_all | solution.py:441
  31.3 4.0 %shard_map.185 = (bf16[4,256,256]{2,1,0:T(8,128)(2,1)S(1)}, f32[128,1536]{1,0:T(8,128)S(1)}, bf16[1536,128]{1,0:T(8,128)(2,1)S(1)}, bf16[1536,128]{1,0:T(8,128)(...) custom-call(bf16[128,3456]{1,0:T(8,128)(2,1)S(1)} %bitcast.2, ...), custom_call_target="tpu_custom_call" | custom-call | flops 5280000000 | tf_op jit(solution)/shard_map/pallas_call | solution.py:49
  35.4 1.6 %shard_map.186 = (f32[2,128,256]{2,1,0:T(8,128)S(1)}, bf16[128,256]{1,0:T(8,128)(2,1)S(1)}, f32[128,1536]{1,0:T(8,128)S(1)}) custom-call(bf16[1536,128]{1,0:T(8,128)(2,1)S(1)} %get-tuple-element.51.qs_ref, bf16[1536,128]{1,0:T(8,128)(2,1)S(1)} %get-tuple-element.52.dos_ref, f32[1,1536]{1,0:T(1,128)S(1)} %get-tuple-element.53.lse_ref, ...), custom_call_target="tpu_custom_call" | custom-call | flops 2200000000 | tf_op jit(solution)/shard_map/pallas_call | solution.py:49
  37.3 2.1 %shard_map.187 = (bf16[4,128,256]{2,1,0:T(8,128)(2,1)S(1)}, f32[128,1536]{1,0:T(8,128)S(1)}) custom-call(bf16[1536,128]{1,0:T(8,128)(2,1)S(1)} %get-tuple-element.51.qs_ref, bf16[1536,128]{1,0:T(8,128)(2,1)S(1)} %get-tuple-element.52.dos_ref, f32[1,1536]{1,0:T(1,128)S(1)} %get-tuple-element.53.lse_ref, f32[1,1536]{1,0:T(1,128)S(1)} %get-tuple-element.54.delta_ref, ...), custom_call_target="tpu_custom_call" | custom-call | flops 2420000000 | tf_op jit(solution)/shard_map/pallas_call | solution.py:49
  39.4 0.9 %collective-permute-start.11 = (bf16[4,128,256]{2,1,0:T(8,128)(2,1)S(1)}, bf16[4,128,256]{2,1,0:T(8,128)(2,1)S(1)}, u32[]{:S(2)}, u32[]{:S(2)}) collective-permute-start(bf16[4,128,256]{2,1,0:T(8,128)(2,1)S(1)} %get-tuple-element.66), channel_id=1, source_target_pairs={{0,16},{8,24},{16,0},{24,8},{32,48},{40,56},{48,32},{56,40},{64,80... | collective-permute-start | bytes 786440 | tf_op jit(solution)/shard_map/ppermute | solution.py:405
  40.2 1.9 %shard_map.188 = (f32[4,128,256]{2,1,0:T(8,128)S(1)}, bf16[8,16,1792]{2,1,0:T(8,128)(2,1)}) custom-call(bf16[1536,128]{1,0:T(8,128)(2,1)S(1)} %get-tuple-element.51.qs_ref, bf16[1536,128]{1,0:T(8,128)(2,1)S(1)} %get-tuple-element.52.dos_ref, f32[1,1536]{1,0:T(1,128)S(1)} %get-tuple-element.53.lse_ref, f32[1,1536]{1,0:T(1,128)S(1)} %get-tuple-element.54.delta_ref, ...), custom_call_target="tpu_custom_call" | custom-call | flops 2200000000 | tf_op jit(solution)/shard_map/pallas_call | solution.py:481
  42.2 6.4 %all-to-all-start.1 = ((bf16[8,16,1792]{2,1,0:T(8,128)(2,1)}), bf16[8,16,1792]{2,1,0:T(8,128)(2,1)S(1)}, u32[]{:S(2)}, u32[]{:S(2)}) async-start(bf16[8,16,1792]{2,1,0:T(8,128)(2,1)} %get-tuple-element.64), calls=%async_computation.1 | async-start | bytes 917504 | tf_op jit(solution)/shard_map/all_to_all | solution.py:490
  48.7 2.3 %collective-permute-start.12 = (bf16[128,256]{1,0:T(8,128)(2,1)S(1)}, bf16[128,256]{1,0:T(8,128)(2,1)S(1)}, u32[]{:S(2)}, u32[]{:S(2)}) collective-permute-start(bf16[128,256]{1,0:T(8,128)(2,1)S(1)} %get-tuple-element.68), channel_id=1, source_target_pairs={{0,32},{8,40},{16,48},{24,56},{32,64},{40,72},{48,80},{56,88},{64,... | collective-permute-start | bytes 196616 | tf_op jit(solution)/shard_map/ppermute | solution.py:408
  51.0 1.2 %collective-permute-start.13 = (bf16[128,256]{1,0:T(8,128)(2,1)S(1)}, bf16[128,256]{1,0:T(8,128)(2,1)S(1)}, u32[]{:S(2)}, u32[]{:S(2)}) collective-permute-start(bf16[128,256]{1,0:T(8,128)(2,1)S(1)} %get-tuple-element.69), channel_id=1, source_target_pairs={{0,64},{8,72},{16,80},{24,88},{32,96},{40,104},{48,112},{56,120},{... | collective-permute-start | bytes 196616 | tf_op jit(solution)/shard_map/ppermute | solution.py:408
  52.2 1.5 %collective-permute-start.14 = (bf16[128,256]{1,0:T(8,128)(2,1)S(1)}, bf16[128,256]{1,0:T(8,128)(2,1)S(1)}, u32[]{:S(2)}, u32[]{:S(2)}) collective-permute-start(bf16[128,256]{1,0:T(8,128)(2,1)S(1)} %get-tuple-element.70), channel_id=1, source_target_pairs={{0,96},{8,104},{16,112},{24,120},{32,0},{40,8},{48,16},{56,24},{64... | collective-permute-start | bytes 196616 | tf_op jit(solution)/shard_map/ppermute | solution.py:408
  53.7 0.9 %shard_map.184 = bf16[128,1536]{1,0:T(8,128)(2,1)} custom-call(bf16[128,1536]{1,0:T(8,128)(2,1)S(1)} %copy-done.7), custom_call_target="tpu_custom_call" | custom-call | flops 2200000000 | tf_op jit(solution)/shard_map/pallas_call | solution.py:49
  54.6 2.1 %collective-permute-done.13.refs_1_ = bf16[128,256]{1,0:T(8,128)(2,1)S(1)} collective-permute-done((bf16[128,256]{1,0:T(8,128)(2,1)S(1)}, bf16[128,256]{1,0:T(8,128)(2,1)S(1)}, u32[]{:S(2)}, u32[]{:S(2)}) %collective-permute-start.13) | collective-permute-done | bytes 65568 | tf_op jit(solution)/shard_map/ppermute | solution.py:408
  56.7 2.5 %all-to-all-done.1.back_ref = bf16[8,16,1792]{2,1,0:T(8,128)(2,1)S(1)} async-done(((bf16[8,16,1792]{2,1,0:T(8,128)(2,1)}), bf16[8,16,1792]{2,1,0:T(8,128)(2,1)S(1)}, u32[]{:S(2)}, u32[]{:S(2)}) %all-to-all-start.1) | async-done | bytes 458784 | tf_op jit(solution)/shard_map/all_to_all | solution.py:490
  59.2 0.8 %shard_map.190 = (bf16[16,12288]{1,0:T(8,128)(2,1)}, bf16[16,1024]{1,0:T(8,128)(2,1)}, bf16[16,1024]{1,0:T(8,128)(2,1)}, bf16[128,128]{1,0:T(8,128)(2,1)}, bf16[128,128]{1,0:T(8,128)(2,1)}) custom-call(bf16[8,16,1792]{2,1,0:T(8,128)(2,1)S(1)} %all-to-all-done.1.back_ref, f32[128,256]{1,0:T(8,128)S(1)} %get-tuple-element.67.keep_ref, ...), custom_call_target="tpu_custom_call" | custom-call | flops 880000000 | tf_op jit(solution)/shard_map/pallas_call | solution.py:49
  (38 shorter events, 1.5 us)
Async XLA Ops:
  0.6 4.8 %collective-permute-start = (bf16[128,128]{1,0:T(8,128)(2,1)}, bf16[128,128]{1,0:T(8,128)(2,1)S(1)}, u32[]{:S(2)}, u32[]{:S(2)}) collective-permute-start(bf16[128,128]{1,0:T(8,128)(2,1)} %dk_ref.1), channel_id=1, source_target_pairs={{0,16},{8,24},{16,0},{24,8},{32,48},{40,56},{48,32},{56,40},{64,80... | collective-permute-start | bytes 98312 | tf_op jit(solution)/shard_map/ppermute | solution.py:405
  2.3 4.1 %collective-permute-start.1 = (bf16[128,128]{1,0:T(8,128)(2,1)}, bf16[128,128]{1,0:T(8,128)(2,1)S(1)}, u32[]{:S(2)}, u32[]{:S(2)}) collective-permute-start(bf16[128,128]{1,0:T(8,128)(2,1)} %dv_ref.1), channel_id=1, source_target_pairs={{0,16},{8,24},{16,0},{24,8},{32,48},{40,56},{48,32},{56,40},{64,80... | collective-permute-start | bytes 98312 | tf_op jit(solution)/shard_map/ppermute | solution.py:405
  6.4 12.2 %collective-permute-start.3 = (bf16[512,128]{1,0:T(8,128)(2,1)S(1)}, bf16[512,128]{1,0:T(8,128)(2,1)S(1)}, u32[]{:S(2)}, u32[]{:S(2)}) collective-permute-start(bf16[512,128]{1,0:T(8,128)(2,1)S(1)} %constant_dynamic-update-slice_fusion.refs_0_), channel_id=1, source_target_pairs={{0,96},{8,104},{16,112},{24,120},{32,0},{40,8},{48,16},{56,24},{64... | collective-permute-start | bytes 393224 | tf_op jit(solution)/shard_map/ppermute | solution.py:408
  10.5 8.7 %collective-permute-start.5 = (bf16[512,128]{1,0:T(8,128)(2,1)S(1)}, bf16[512,128]{1,0:T(8,128)(2,1)S(1)}, u32[]{:S(2)}, u32[]{:S(2)}) collective-permute-start(bf16[512,128]{1,0:T(8,128)(2,1)S(1)} %constant_dynamic-update-slice_fusion.refs_0_), channel_id=1, source_target_pairs={{0,64},{8,72},{16,80},{24,88},{32,96},{40,104},{48,112},{56,120},{... | collective-permute-start | bytes 393224 | tf_op jit(solution)/shard_map/ppermute | solution.py:408
  10.5 8.8 %collective-permute-start.7 = (bf16[512,128]{1,0:T(8,128)(2,1)S(1)}, bf16[512,128]{1,0:T(8,128)(2,1)S(1)}, u32[]{:S(2)}, u32[]{:S(2)}) collective-permute-start(bf16[512,128]{1,0:T(8,128)(2,1)S(1)} %constant_dynamic-update-slice_fusion.refs_0_), channel_id=1, source_target_pairs={{0,32},{8,40},{16,48},{24,56},{32,64},{40,72},{48,80},{56,88},{64,... | collective-permute-start | bytes 393224 | tf_op jit(solution)/shard_map/ppermute | solution.py:408
  11.7 7.9 %copy-start = (bf16[128,1536]{1,0:T(8,128)(2,1)S(1)}, bf16[128,1536]{1,0:T(8,128)(2,1)}, u32[]{:S(2)}) copy-start(bf16[128,1536]{1,0:T(8,128)(2,1)} %refs_4_.1) | copy-start | bytes 1179652
  11.7 7.9 %copy-start.1 = (bf16[128,1536]{1,0:T(8,128)(2,1)S(1)}, bf16[128,1536]{1,0:T(8,128)(2,1)}, u32[]{:S(2)}) copy-start(bf16[128,1536]{1,0:T(8,128)(2,1)} %refs_5_.1) | copy-start | bytes 1179652
  11.7 7.9 %copy-start.2 = (bf16[128,1536]{1,0:T(8,128)(2,1)S(1)}, bf16[128,1536]{1,0:T(8,128)(2,1)}, u32[]{:S(2)}) copy-start(bf16[128,1536]{1,0:T(8,128)(2,1)} %refs_6_.1) | copy-start | bytes 1179652
  11.7 7.9 %copy-start.3 = (f32[128,12]{0,1:T(8,128)S(1)}, f32[128,12]{0,1:T(8,128)}, u32[]{:S(2)}) copy-start(f32[128,12]{0,1:T(8,128)} %param.21) | copy-start | bytes 18436
  11.7 19.5 %all-to-all-start = ((bf16[8,16,3456]{2,1,0:T(8,128)(2,1)}), bf16[8,16,3456]{2,1,0:T(8,128)(2,1)S(1)}, u32[]{:S(2)}, u32[]{:S(2)}) async-start(bf16[8,16,3456]{2,1,0:T(8,128)(2,1)} %get-tuple-element.50), calls=%async_computation | async-start | bytes 1769472 | tf_op jit(solution)/shard_map/all_to_all | solution.py:441
  18.5 6.0 %collective-permute-start.2 = (bf16[512,128]{1,0:T(8,128)(2,1)S(1)}, bf16[512,128]{1,0:T(8,128)(2,1)S(1)}, u32[]{:S(2)}, u32[]{:S(2)}) collective-permute-start(bf16[512,128]{1,0:T(8,128)(2,1)S(1)} %constant_dynamic-update-slice_fusion.refs_0_), channel_id=1, source_target_pairs={{0,8},{8,0},{16,24},{24,16},{32,40},{40,32},{48,56},{56,48},{64,72... | collective-permute-start | bytes 393224 | tf_op jit(solution)/shard_map/ppermute | solution.py:402
  18.6 5.9 %collective-permute-start.4 = (bf16[512,128]{1,0:T(8,128)(2,1)S(1)}, bf16[512,128]{1,0:T(8,128)(2,1)S(1)}, u32[]{:S(2)}, u32[]{:S(2)}) collective-permute-start(bf16[512,128]{1,0:T(8,128)(2,1)S(1)} %collective-permute-done.3.refs_1_), channel_id=1, source_target_pairs={{0,8},{8,0},{16,24},{24,16},{32,40},{40,32},{48,56},{56,48},{64,72... | collective-permute-start | bytes 393224 | tf_op jit(solution)/shard_map/ppermute | solution.py:402
  19.1 5.4 %collective-permute-start.6 = (bf16[512,128]{1,0:T(8,128)(2,1)S(1)}, bf16[512,128]{1,0:T(8,128)(2,1)S(1)}, u32[]{:S(2)}, u32[]{:S(2)}) collective-permute-start(bf16[512,128]{1,0:T(8,128)(2,1)S(1)} %collective-permute-done.5.refs_2_.refs_0_), channel_id=1, source_target_pairs={{0,8},{8,0},{16,24},{24,16},{32,40},{40,32},{48,56},{56,48},{64,72... | collective-permute-start | bytes 393224 | tf_op jit(solution)/shard_map/ppermute | solution.py:402
  19.2 5.3 %collective-permute-start.8 = (bf16[512,128]{1,0:T(8,128)(2,1)S(1)}, bf16[512,128]{1,0:T(8,128)(2,1)S(1)}, u32[]{:S(2)}, u32[]{:S(2)}) collective-permute-start(bf16[512,128]{1,0:T(8,128)(2,1)S(1)} %collective-permute-done.7.refs_3_.refs_1_), channel_id=1, source_target_pairs={{0,8},{8,0},{16,24},{24,16},{32,40},{40,32},{48,56},{56,48},{64,72... | collective-permute-start | bytes 393224 | tf_op jit(solution)/shard_map/ppermute | solution.py:402
  29.9 7.1 %collective-permute-start.10 = (bf16[4,256,256]{2,1,0:T(8,128)(2,1)}, bf16[4,256,256]{2,1,0:T(8,128)(2,1)S(1)}, u32[]{:S(2)}, u32[]{:S(2)}) collective-permute-start(bf16[4,256,256]{2,1,0:T(8,128)(2,1)} %get-tuple-element.58), channel_id=1, source_target_pairs={{0,8},{8,0},{16,24},{24,16},{32,40},{40,32},{48,56},{56,48},{64,72... | collective-permute-start | bytes 1572872 | tf_op jit(solution)/shard_map/ppermute | solution.py:402
  35.3 2.0 %collective-permute-start.9 = (bf16[4,256,256]{2,1,0:T(8,128)(2,1)S(1)}, bf16[4,256,256]{2,1,0:T(8,128)(2,1)S(1)}, u32[]{:S(2)}, u32[]{:S(2)}) collective-permute-start(bf16[4,256,256]{2,1,0:T(8,128)(2,1)S(1)} %get-tuple-element.57), channel_id=1, source_target_pairs={{0,8},{8,0},{16,24},{24,16},{32,40},{40,32},{48,56},{56,48},{64,72... | collective-permute-start | bytes 1572872 | tf_op jit(solution)/shard_map/ppermute | solution.py:402
  35.4 1.9 %copy-start.6 = (f32[4,128,256]{2,1,0:T(8,128)S(1)}, f32[4,128,256]{2,1,0:T(8,128)}, u32[]{:S(2)}) copy-start(f32[4,128,256]{2,1,0:T(8,128)} %get-tuple-element.59.refs_4_) | copy-start | bytes 1572868
  37.3 3.0 %copy-start.5 = (f32[4,128,256]{2,1,0:T(8,128)S(1)}, f32[4,128,256]{2,1,0:T(8,128)}, u32[]{:S(2)}) copy-start(f32[4,128,256]{2,1,0:T(8,128)} %get-tuple-element.63.doc_ref) | copy-start | bytes 1572868
  39.4 9.2 %collective-permute-start.11 = (bf16[4,128,256]{2,1,0:T(8,128)(2,1)S(1)}, bf16[4,128,256]{2,1,0:T(8,128)(2,1)S(1)}, u32[]{:S(2)}, u32[]{:S(2)}) collective-permute-start(bf16[4,128,256]{2,1,0:T(8,128)(2,1)S(1)} %get-tuple-element.66), channel_id=1, source_target_pairs={{0,16},{8,24},{16,0},{24,8},{32,48},{40,56},{48,32},{56,40},{64,80... | collective-permute-start | bytes 786440 | tf_op jit(solution)/shard_map/ppermute | solution.py:405
  42.2 17.0 %all-to-all-start.1 = ((bf16[8,16,1792]{2,1,0:T(8,128)(2,1)}), bf16[8,16,1792]{2,1,0:T(8,128)(2,1)S(1)}, u32[]{:S(2)}, u32[]{:S(2)}) async-start(bf16[8,16,1792]{2,1,0:T(8,128)(2,1)} %get-tuple-element.64), calls=%async_computation.1 | async-start | bytes 917504 | tf_op jit(solution)/shard_map/all_to_all | solution.py:490
  48.6 5.1 %copy-start.7 = (bf16[128,1536]{1,0:T(8,128)(2,1)S(1)}, bf16[128,1536]{1,0:T(8,128)(2,1)}, u32[]{:S(2)}) copy-start(bf16[128,1536]{1,0:T(8,128)(2,1)} %get-tuple-element.49.turned_ref) | copy-start | bytes 1179652
  48.7 6.0 %collective-permute-start.12 = (bf16[128,256]{1,0:T(8,128)(2,1)S(1)}, bf16[128,256]{1,0:T(8,128)(2,1)S(1)}, u32[]{:S(2)}, u32[]{:S(2)}) collective-permute-start(bf16[128,256]{1,0:T(8,128)(2,1)S(1)} %get-tuple-element.68), channel_id=1, source_target_pairs={{0,32},{8,40},{16,48},{24,56},{32,64},{40,72},{48,80},{56,88},{64,... | collective-permute-start | bytes 196616 | tf_op jit(solution)/shard_map/ppermute | solution.py:408
  51.0 5.8 %collective-permute-start.13 = (bf16[128,256]{1,0:T(8,128)(2,1)S(1)}, bf16[128,256]{1,0:T(8,128)(2,1)S(1)}, u32[]{:S(2)}, u32[]{:S(2)}) collective-permute-start(bf16[128,256]{1,0:T(8,128)(2,1)S(1)} %get-tuple-element.69), channel_id=1, source_target_pairs={{0,64},{8,72},{16,80},{24,88},{32,96},{40,104},{48,112},{56,120},{... | collective-permute-start | bytes 196616 | tf_op jit(solution)/shard_map/ppermute | solution.py:408
  52.2 4.6 %collective-permute-start.14 = (bf16[128,256]{1,0:T(8,128)(2,1)S(1)}, bf16[128,256]{1,0:T(8,128)(2,1)S(1)}, u32[]{:S(2)}, u32[]{:S(2)}) collective-permute-start(bf16[128,256]{1,0:T(8,128)(2,1)S(1)} %get-tuple-element.70), channel_id=1, source_target_pairs={{0,96},{8,104},{16,112},{24,120},{32,0},{40,8},{48,16},{56,24},{64... | collective-permute-start | bytes 196616 | tf_op jit(solution)/shard_map/ppermute | solution.py:408
  (1 other events, 1.1 us)

commit v6 on v5

--- a/solution.py
+++ b/solution.py
@@ -71,8 +71,12 @@
     dscore = (prob * (dprob - delta)).astype(BF)
     dv = dot(prob.astype(BF), dos_ref[...], 1, 0)
     dk = dot(dscore, qs_ref[...], 1, 0) * SCALE
-    dq = dot(keys, dscore, 0, 0)
-    return dq, dk, dv
+    return (keys, dscore), dk, dv
+
+
+def spread(blocks):
+    keys, dscore = (jnp.concatenate(part, axis=0) for part in zip(*blocks))
+    return dot(keys, dscore, 0, 0)
 
 
 def both(ref):
@@ -197,7 +201,7 @@
     if core == 0:
         q_ref, o_ref, do_ref, ex_ref, *state, dq_ref, near_ref, own_ref = refs
     else:
-        *state, dq_in, near_ref, own_ref, far_hbm, dq_hbm, near_hbm, own_hbm, far_ref, dq_ref, sems = refs
+        *state, dq_in, near_ref, own_ref, far_ref, dq_ref, near_hbm, own_hbm, sems = refs
         store(near_ref, near_hbm)
         store(own_ref, own_hbm)
     qs_ref, dos_ref, lse_ref, delta_ref = state
@@ -218,7 +222,7 @@
         spread_rows(dot(ones, high, 1, 1) + dot(ones, low, 1, 1), delta_ref, heads)
     lse = lse_ref[...]
     delta = delta_ref[...]
-    total = None
+    total, blocks = None, []
     for depth in range(4):
         owners = doc_keys(order_ref, me, ctx_size, (core, depth))
         shift = [row for o in owners for row in doc_lse(order_ref, me, o, lse, lane_half)]
@@ -228,7 +232,8 @@
             key_pos = jnp.where(key < half, order_ref[2 * me] * half + key, order_ref[2 * me + 1] * half + key - half)
             row_pos = jnp.where(lane_half, order_ref[2 * me + 1] * half + lane - half, order_ref[2 * me] * half + lane)
             mask = jnp.where(key < D, key_pos, -1) <= row_pos
-        dq, dk, dv = pair_block(qs_ref, dos_ref, *both(kv_refs[depth]), shift, delta, mask)
+        block, dk, dv = pair_block(qs_ref, dos_ref, *both(kv_refs[depth]), shift, delta, mask)
+        blocks.append(block)
         for side, grad in enumerate((dk, dv)):
             cut = slice(side * D, (side + 1) * D)
             if core == 0:
@@ -236,15 +241,13 @@
                 near_ref[depth, :, cut] = grad[D:]
             else:
                 far_ref[depth, :, cut] = grad.astype(BF)
-        total = dq if total is None else total + dq
-        if core == 1 and depth % 2 == 1:
-            done = pl.ds(depth - 1, 2)
-            store(far_ref.at[done], far_hbm.at[done])
+        if len(blocks) == 2:
+            dq, blocks = spread(blocks), []
+            total = dq if total is None else total + dq
     if core == 0:
         dq_ref[...] = total
     else:
         dq_ref[...] = ((total + dq_in[...]) * SCALE).astype(BF)
-        store(dq_ref, dq_hbm)
     for copy in stores:
         copy.wait()
 
@@ -263,27 +266,31 @@
     spread_rows(stats[:16] + stats[16:32] + stats[32:48], lse_ref, heads)
     spread_rows(stats[48:64] + stats[64:80] + stats[80:96], delta_ref, heads)
     lse, delta = lse_ref[...], delta_ref[...]
-    total = None
+    total, blocks = None, []
     for n in range(4):
-        dq, dk, dv = pair_block(qs_ref, dos_ref, *both(kv_refs[n]), lse, delta, None)
+        block, dk, dv = pair_block(qs_ref, dos_ref, *both(kv_refs[n]), lse, delta, None)
         send_ref[n, :, :D] = dk.astype(BF)
         send_ref[n, :, D:] = dv.astype(BF)
-        total = dq if total is None else total + dq
+        blocks.append(block)
+        if len(blocks) == 2:
+            dq, blocks = spread(blocks), []
+            total = dq if total is None else total + dq
     dq_ref[...] = total
 
 
-def column(x, qs_ref, dos_ref, lse, delta, kv_refs, total, store):
+def column(x, qs_ref, dos_ref, lse, delta, kv_refs, total, store, blocks=()):
+    blocks = list(blocks)
     for pair in range(len(kv_refs) // 2):
         refs = [kv_refs[2 * pair + m] for m in range(2)]
         keys = jnp.concatenate([ref[2 * x * D : 2 * x * D + D] for ref in refs], axis=0)
         values = jnp.concatenate([ref[2 * x * D + D : 2 * x * D + 2 * D] for ref in refs], axis=0)
-        dq, dk, dv = pair_block(qs_ref, dos_ref, keys, values, lse, delta, None)
+        block, dk, dv = pair_block(qs_ref, dos_ref, keys, values, lse, delta, None)
         for m in range(2):
             part = slice(m * D, (m + 1) * D)
             store(2 * pair + m, slice(0, D), dk[part])
             store(2 * pair + m, slice(D, 2 * D), dv[part])
-        total = total + dq
-    return total
+        blocks.append(block)
+    return total + spread(blocks)
 
 
 def near_kernel(qs_ref, dos_ref, lse_ref, delta_ref, dq_in, core_ref, core_doc_ref, *refs):
@@ -308,14 +315,14 @@
     mask = jnp.concatenate([seen] * heads, axis=1)
     keys = pay_ref[:, 2 * wide : 2 * wide + D]
     values = pay_ref[:, 2 * wide + D : 2 * wide + 2 * D]
-    dq, dk, dv = pair_block(qs_ref, dos_ref, keys, values, lse, delta, mask)
+    block, dk, dv = pair_block(qs_ref, dos_ref, keys, values, lse, delta, mask)
     self_ref[:, :D] = dk.astype(BF)
     self_ref[:, D:] = dv.astype(BF)
 
     def store(n, cut, grad):
         out_ref[n, :, cut] = grad
 
-    dq_ref[...] = column(0, qs_ref, dos_ref, lse, delta, kv_refs, dq_in[...] + dq, store)
+    dq_ref[...] = column(0, qs_ref, dos_ref, lse, delta, kv_refs, dq_in[...], store, [block])
 
 
 def last_kernel(heads, groups, qs_ref, dos_ref, lse_ref, delta_ref, dq_in, self_ref, low_ref, core_ref, core_doc_ref, doc_ref, *refs):
@@ -456,10 +463,11 @@
     turned = ((D, stacked), BF)
     far_doc, doc_turned, near_doc, own_doc = pl.pallas_call(
         functools.partial(doc_kernel, 1, heads, ctx_size),
-        out_shape=tuple(pltpu.HBM(*out) for out in (double, turned, quarter, quarter)),
+        out_shape=tuple(jax.ShapeDtypeStruct(*out) for out in (double, turned))
+        + tuple(pltpu.HBM(*out) for out in (quarter, quarter)),
         in_specs=[smem()] + [vmem()] * 11,
-        out_specs=(hbm(),) * 4,
-        scratch_shapes=[pltpu.VMEM(*double), pltpu.VMEM(*turned), pltpu.SemaphoreType.DMA((5,))],
+        out_specs=(vmem(), vmem(), hbm(), hbm()),
+        scratch_shapes=[pltpu.SemaphoreType.DMA((2,))],
         compiler_params=SHARED,
         cost_estimate=cost(6),
     )(block_order, *theirs, *doc_state, dq, near_doc, own_doc)

time: 60.5 us -> 59.9 us (0.990)
  Pallas kernels: 24.4 us -> 23.7 us
    pallas_call x1, Pallas kernels: 5.38 us -> 4.73 us  [local(): pl.pallas_call(functools.partial(doc_kernel, 1, heads, ctx_size), out_sha...]
    all_to_all x1, waiting for transfers between devices: 0.76 us -> 1.4 us  [local(): lax.all_to_all(payload, 'head', 0, 0, tiled=True).reshape(groups * each, -1)]
    all_to_all x1, starting transfers between devices: 6.41 us -> 5.78 us  [local(): back = lax.all_to_all(back, 'head', 0, 0, tiled=True)]
  transfers between devices with their start and end apart: 17 -> 17, of which waited for: 5 -> 5; matrix products, arithmetic and copies ran while one was open for 0% -> 0% of each run, Pallas kernels for 36% -> 35%
where the time goes in v6:
time: 59.9 us; the launch traced here: 59.4 us
  starting transfers between devices  27.8 us (46%)
  Pallas kernels  23.7 us (40%)
  waiting for transfers between devices  6.95 us (12%)
  between operations  0.82 us (1%)
    pallas_call x7, Pallas kernels, call(): pl.pallas_call(body, out_shape=tuple((jax.ShapeDtypeStruct(s, t) for s, t...  14.3 us
    ppermute x6, starting transfers between devices, along_z(): lax.ppermute(x, 'ctx', [(i, (i + 4 * d) % ctx_size) for i in range(ctx_si...  10.5 us
    all_to_all x1, starting transfers between devices, local(): lax.all_to_all(payload, 'head', 0, 0, tiled=True).reshape(groups * each, -1)  6.8 us
    all_to_all x1, starting transfers between devices, local(): back = lax.all_to_all(back, 'head', 0, 0, tiled=True)  5.78 us
    pallas_call x1, Pallas kernels, local(): pl.pallas_call(functools.partial(doc_kernel, 1, heads, ctx_size), out_sha...  4.73 us
    ppermute x3, starting transfers between devices, other_chip(): return lax.ppermute(x, 'ctx', [(i, i ^ 2) for i in range(ctx_size)])  2.98 us
    pallas_call x1, Pallas kernels, local(): pl.pallas_call(functools.partial(pack_kernel, heads, groups, total_doc),...  2.71 us
    all_to_all x1, waiting for transfers between devices, local(): back = lax.all_to_all(back, 'head', 0, 0, tiled=True)  2.47 us
  transfers between devices with their start and end apart: 17, of which 5 were waited for; matrix products, arithmetic and copies ran while one was open for 0% of the time, Pallas kernels for 35%

profile of v6, /device:TPU:0, one launch (start us, length us, event | category | flops | bytes accessed | tf_op | source)
XLA Modules:
  0.0 59.4 jit_solution(16303118043480834166)
XLA Ops:
  0.6 1.7 %collective-permute-start = (bf16[128,128]{1,0:T(8,128)(2,1)}, bf16[128,128]{1,0:T(8,128)(2,1)S(1)}, u32[]{:S(2)}, u32[]{:S(2)}) collective-permute-start(bf16[128,128]{1,0:T(8,128)(2,1)} %dk_ref.1), channel_id=1, source_target_pairs={{0,16},{8,24},{16,0},{24,8},{32,48},{40,56},{48,32},{56,40},{64,80... | collective-permute-start | bytes 98312 | tf_op jit(solution)/shard_map/ppermute | solution.py:412
  2.7 2.7 %shard_map.181 = (bf16[8,16,3456]{2,1,0:T(8,128)(2,1)}, bf16[512,128]{1,0:T(8,128)(2,1)S(1)}) custom-call(s32[1,2]{1,0:T(1,128)} %len_hbm.1, bf16[16,12288]{1,0:T(8,128)(2,1)} %do_ref.1, bf16[16,12288]{1,0:T(8,128)(2,1)} %o_ref.1, bf16[16,12288]{1,0:T(8,128)(2,1)} %q_ref.1, bf16[16,1024]{1,0:T(8,128)(2,1)} %k_ref.1, bf16[16,1024]{1,0:T(8,128)(2,1)} %v_ref.1, ...), custom_call_target="tpu_custom_call" | custom-call | flops 5500000256 | tf_op jit(solution)/shard_map/pallas_call | solution.py:421
  5.5 0.9 %collective-permute-done.1 = bf16[128,128]{1,0:T(8,128)(2,1)S(1)} collective-permute-done((bf16[128,128]{1,0:T(8,128)(2,1)}, bf16[128,128]{1,0:T(8,128)(2,1)S(1)}, u32[]{:S(2)}, u32[]{:S(2)}) %collective-permute-start.1) | collective-permute-done | bytes 32800 | tf_op jit(solution)/shard_map/ppermute | solution.py:412
  6.4 4.0 %collective-permute-start.3 = (bf16[512,128]{1,0:T(8,128)(2,1)S(1)}, bf16[512,128]{1,0:T(8,128)(2,1)S(1)}, u32[]{:S(2)}, u32[]{:S(2)}) collective-permute-start(bf16[512,128]{1,0:T(8,128)(2,1)S(1)} %constant_dynamic-update-slice_fusion.refs_0_), channel_id=1, source_target_pairs={{0,96},{8,104},{16,112},{24,120},{32,0},{40,8},{48,16},{56,24},{64... | collective-permute-start | bytes 393224 | tf_op jit(solution)/shard_map/ppermute | solution.py:415
  10.5 1.3 %collective-permute-start.7 = (bf16[512,128]{1,0:T(8,128)(2,1)S(1)}, bf16[512,128]{1,0:T(8,128)(2,1)S(1)}, u32[]{:S(2)}, u32[]{:S(2)}) collective-permute-start(bf16[512,128]{1,0:T(8,128)(2,1)S(1)} %constant_dynamic-update-slice_fusion.refs_0_), channel_id=1, source_target_pairs={{0,32},{8,40},{16,48},{24,56},{32,64},{40,72},{48,80},{56,88},{64,... | collective-permute-start | bytes 393224 | tf_op jit(solution)/shard_map/ppermute | solution.py:415
  11.7 6.8 %all-to-all-start = ((bf16[8,16,3456]{2,1,0:T(8,128)(2,1)}), bf16[8,16,3456]{2,1,0:T(8,128)(2,1)S(1)}, u32[]{:S(2)}, u32[]{:S(2)}) async-start(bf16[8,16,3456]{2,1,0:T(8,128)(2,1)} %get-tuple-element.50), calls=%async_computation | async-start | bytes 1769472 | tf_op jit(solution)/shard_map/all_to_all | solution.py:448
  18.6 0.5 collective-permute-start.4
  19.7 4.8 %shard_map.182 = (bf16[1536,128]{1,0:T(8,128)(2,1)S(1)}, bf16[1536,128]{1,0:T(8,128)(2,1)S(1)}, f32[1,1536]{1,0:T(1,128)S(1)}, f32[1,1536]{1,0:T(1,128)S(1)}, f3...) custom-call(s32[32]{0:T(128)S(1)} %copy-done.4, ...), custom_call_target="tpu_custom_call" | custom-call | flops 6600000000 | tf_op jit(solution)/shard_map/pallas_call | solution.py:49
  24.5 4.7 %shard_map.183 = (bf16[4,256,256]{2,1,0:T(8,128)(2,1)S(1)}, bf16[128,1536]{1,0:T(8,128)(2,1)S(1)}, f32[4,128,256]{2,1,0:T(8,128)}, f32[4,128,256]{2,1,0:T(8,128)}) custom-call(s32[32]{0:T(128)S(1)} %copy-done.4, bf16[512,128]{1,0:T(8,128)(2,1)S(1)} %collective-permute-done.2.refs_0_, bf16[512,128]{1,0:T(8,128)(2,1)S(1)} %collective-permute-done.4.refs_1_, ...), custom_call_target="tpu_custom_call" | custom-call | flops 6600000000 | tf_op jit(solution)/shard_map/pallas_call | solution.py:464
  29.3 0.6 collective-permute-start.10
  29.8 1.4 %all-to-all-done = bf16[8,16,3456]{2,1,0:T(8,128)(2,1)S(1)} async-done(((bf16[8,16,3456]{2,1,0:T(8,128)(2,1)}), bf16[8,16,3456]{2,1,0:T(8,128)(2,1)S(1)}, u32[]{:S(2)}, u32[]{:S(2)}) %all-to-all-start) | async-done | bytes 884768 | tf_op jit(solution)/shard_map/all_to_all | solution.py:448
  31.3 4.0 %shard_map.185 = (bf16[4,256,256]{2,1,0:T(8,128)(2,1)S(1)}, f32[128,1536]{1,0:T(8,128)S(1)}, bf16[1536,128]{1,0:T(8,128)(2,1)S(1)}, bf16[1536,128]{1,0:T(8,128)(...) custom-call(bf16[128,3456]{1,0:T(8,128)(2,1)S(1)} %bitcast.2, ...), custom_call_target="tpu_custom_call" | custom-call | flops 5280000000 | tf_op jit(solution)/shard_map/pallas_call | solution.py:49
  35.4 1.7 %shard_map.186 = (f32[2,128,256]{2,1,0:T(8,128)S(1)}, bf16[128,256]{1,0:T(8,128)(2,1)S(1)}, f32[128,1536]{1,0:T(8,128)S(1)}) custom-call(bf16[1536,128]{1,0:T(8,128)(2,1)S(1)} %get-tuple-element.51.qs_ref, bf16[1536,128]{1,0:T(8,128)(2,1)S(1)} %get-tuple-element.52.dos_ref, f32[1,1536]{1,0:T(1,128)S(1)} %get-tuple-element.53.lse_ref, ...), custom_call_target="tpu_custom_call" | custom-call | flops 2200000000 | tf_op jit(solution)/shard_map/pallas_call | solution.py:49
  37.3 2.1 %shard_map.187 = (bf16[4,128,256]{2,1,0:T(8,128)(2,1)S(1)}, f32[128,1536]{1,0:T(8,128)S(1)}) custom-call(bf16[1536,128]{1,0:T(8,128)(2,1)S(1)} %get-tuple-element.51.qs_ref, bf16[1536,128]{1,0:T(8,128)(2,1)S(1)} %get-tuple-element.52.dos_ref, f32[1,1536]{1,0:T(1,128)S(1)} %get-tuple-element.53.lse_ref, f32[1,1536]{1,0:T(1,128)S(1)} %get-tuple-element.54.delta_ref, ...), custom_call_target="tpu_custom_call" | custom-call | flops 2420000000 | tf_op jit(solution)/shard_map/pallas_call | solution.py:49
  39.3 0.9 %collective-permute-start.11 = (bf16[4,128,256]{2,1,0:T(8,128)(2,1)S(1)}, bf16[4,128,256]{2,1,0:T(8,128)(2,1)S(1)}, u32[]{:S(2)}, u32[]{:S(2)}) collective-permute-start(bf16[4,128,256]{2,1,0:T(8,128)(2,1)S(1)} %get-tuple-element.66), channel_id=1, source_target_pairs={{0,16},{8,24},{16,0},{24,8},{32,48},{40,56},{48,32},{56,40},{64,80... | collective-permute-start | bytes 786440 | tf_op jit(solution)/shard_map/ppermute | solution.py:412
  40.2 1.9 %shard_map.188 = (f32[4,128,256]{2,1,0:T(8,128)S(1)}, bf16[8,16,1792]{2,1,0:T(8,128)(2,1)}) custom-call(bf16[1536,128]{1,0:T(8,128)(2,1)S(1)} %get-tuple-element.51.qs_ref, bf16[1536,128]{1,0:T(8,128)(2,1)S(1)} %get-tuple-element.52.dos_ref, f32[1,1536]{1,0:T(1,128)S(1)} %get-tuple-element.53.lse_ref, f32[1,1536]{1,0:T(1,128)S(1)} %get-tuple-element.54.delta_ref, ...), custom_call_target="tpu_custom_call" | custom-call | flops 2200000000 | tf_op jit(solution)/shard_map/pallas_call | solution.py:489
  42.2 5.8 %all-to-all-start.1 = ((bf16[8,16,1792]{2,1,0:T(8,128)(2,1)}), bf16[8,16,1792]{2,1,0:T(8,128)(2,1)S(1)}, u32[]{:S(2)}, u32[]{:S(2)}) async-start(bf16[8,16,1792]{2,1,0:T(8,128)(2,1)} %get-tuple-element.64), calls=%async_computation.1 | async-start | bytes 917504 | tf_op jit(solution)/shard_map/all_to_all | solution.py:498
  48.0 2.3 %collective-permute-start.12 = (bf16[128,256]{1,0:T(8,128)(2,1)S(1)}, bf16[128,256]{1,0:T(8,128)(2,1)S(1)}, u32[]{:S(2)}, u32[]{:S(2)}) collective-permute-start(bf16[128,256]{1,0:T(8,128)(2,1)S(1)} %get-tuple-element.68), channel_id=1, source_target_pairs={{0,32},{8,40},{16,48},{24,56},{32,64},{40,72},{48,80},{56,88},{64,... | collective-permute-start | bytes 196616 | tf_op jit(solution)/shard_map/ppermute | solution.py:415
  50.3 1.5 %collective-permute-start.13 = (bf16[128,256]{1,0:T(8,128)(2,1)S(1)}, bf16[128,256]{1,0:T(8,128)(2,1)S(1)}, u32[]{:S(2)}, u32[]{:S(2)}) collective-permute-start(bf16[128,256]{1,0:T(8,128)(2,1)S(1)} %get-tuple-element.69), channel_id=1, source_target_pairs={{0,64},{8,72},{16,80},{24,88},{32,96},{40,104},{48,112},{56,120},{... | collective-permute-start | bytes 196616 | tf_op jit(solution)/shard_map/ppermute | solution.py:415
  51.8 1.5 %collective-permute-start.14 = (bf16[128,256]{1,0:T(8,128)(2,1)S(1)}, bf16[128,256]{1,0:T(8,128)(2,1)S(1)}, u32[]{:S(2)}, u32[]{:S(2)}) collective-permute-start(bf16[128,256]{1,0:T(8,128)(2,1)S(1)} %get-tuple-element.70), channel_id=1, source_target_pairs={{0,96},{8,104},{16,112},{24,120},{32,0},{40,8},{48,16},{56,24},{64... | collective-permute-start | bytes 196616 | tf_op jit(solution)/shard_map/ppermute | solution.py:415
  53.2 0.9 %shard_map.184 = bf16[128,1536]{1,0:T(8,128)(2,1)} custom-call(bf16[128,1536]{1,0:T(8,128)(2,1)S(1)} %get-tuple-element.49.turned_ref), custom_call_target="tpu_custom_call" | custom-call | flops 2200000000 | tf_op jit(solution)/shard_map/pallas_call | solution.py:49
  54.2 1.9 %collective-permute-done.13.refs_1_ = bf16[128,256]{1,0:T(8,128)(2,1)S(1)} collective-permute-done((bf16[128,256]{1,0:T(8,128)(2,1)S(1)}, bf16[128,256]{1,0:T(8,128)(2,1)S(1)}, u32[]{:S(2)}, u32[]{:S(2)}) %collective-permute-start.13) | collective-permute-done | bytes 65568 | tf_op jit(solution)/shard_map/ppermute | solution.py:415
  56.1 2.5 %all-to-all-done.1.back_ref = bf16[8,16,1792]{2,1,0:T(8,128)(2,1)S(1)} async-done(((bf16[8,16,1792]{2,1,0:T(8,128)(2,1)}), bf16[8,16,1792]{2,1,0:T(8,128)(2,1)S(1)}, u32[]{:S(2)}, u32[]{:S(2)}) %all-to-all-start.1) | async-done | bytes 458784 | tf_op jit(solution)/shard_map/all_to_all | solution.py:498
  58.5 0.8 %shard_map.190 = (bf16[16,12288]{1,0:T(8,128)(2,1)}, bf16[16,1024]{1,0:T(8,128)(2,1)}, bf16[16,1024]{1,0:T(8,128)(2,1)}, bf16[128,128]{1,0:T(8,128)(2,1)}, bf16[128,128]{1,0:T(8,128)(2,1)}) custom-call(bf16[8,16,1792]{2,1,0:T(8,128)(2,1)S(1)} %all-to-all-done.1.back_ref, f32[128,256]{1,0:T(8,128)S(1)} %get-tuple-element.67.keep_ref, ...), custom_call_target="tpu_custom_call" | custom-call | flops 880000000 | tf_op jit(solution)/shard_map/pallas_call | solution.py:49
  (36 shorter events, 1.5 us)
Async XLA Ops:
  0.6 4.8 %collective-permute-start = (bf16[128,128]{1,0:T(8,128)(2,1)}, bf16[128,128]{1,0:T(8,128)(2,1)S(1)}, u32[]{:S(2)}, u32[]{:S(2)}) collective-permute-start(bf16[128,128]{1,0:T(8,128)(2,1)} %dk_ref.1), channel_id=1, source_target_pairs={{0,16},{8,24},{16,0},{24,8},{32,48},{40,56},{48,32},{56,40},{64,80... | collective-permute-start | bytes 98312 | tf_op jit(solution)/shard_map/ppermute | solution.py:412
  2.3 4.1 %collective-permute-start.1 = (bf16[128,128]{1,0:T(8,128)(2,1)}, bf16[128,128]{1,0:T(8,128)(2,1)S(1)}, u32[]{:S(2)}, u32[]{:S(2)}) collective-permute-start(bf16[128,128]{1,0:T(8,128)(2,1)} %dv_ref.1), channel_id=1, source_target_pairs={{0,16},{8,24},{16,0},{24,8},{32,48},{40,56},{48,32},{56,40},{64,80... | collective-permute-start | bytes 98312 | tf_op jit(solution)/shard_map/ppermute | solution.py:412
  6.4 12.2 %collective-permute-start.3 = (bf16[512,128]{1,0:T(8,128)(2,1)S(1)}, bf16[512,128]{1,0:T(8,128)(2,1)S(1)}, u32[]{:S(2)}, u32[]{:S(2)}) collective-permute-start(bf16[512,128]{1,0:T(8,128)(2,1)S(1)} %constant_dynamic-update-slice_fusion.refs_0_), channel_id=1, source_target_pairs={{0,96},{8,104},{16,112},{24,120},{32,0},{40,8},{48,16},{56,24},{64... | collective-permute-start | bytes 393224 | tf_op jit(solution)/shard_map/ppermute | solution.py:415
  10.5 8.7 %collective-permute-start.5 = (bf16[512,128]{1,0:T(8,128)(2,1)S(1)}, bf16[512,128]{1,0:T(8,128)(2,1)S(1)}, u32[]{:S(2)}, u32[]{:S(2)}) collective-permute-start(bf16[512,128]{1,0:T(8,128)(2,1)S(1)} %constant_dynamic-update-slice_fusion.refs_0_), channel_id=1, source_target_pairs={{0,64},{8,72},{16,80},{24,88},{32,96},{40,104},{48,112},{56,120},{... | collective-permute-start | bytes 393224 | tf_op jit(solution)/shard_map/ppermute | solution.py:415
  10.5 8.8 %collective-permute-start.7 = (bf16[512,128]{1,0:T(8,128)(2,1)S(1)}, bf16[512,128]{1,0:T(8,128)(2,1)S(1)}, u32[]{:S(2)}, u32[]{:S(2)}) collective-permute-start(bf16[512,128]{1,0:T(8,128)(2,1)S(1)} %constant_dynamic-update-slice_fusion.refs_0_), channel_id=1, source_target_pairs={{0,32},{8,40},{16,48},{24,56},{32,64},{40,72},{48,80},{56,88},{64,... | collective-permute-start | bytes 393224 | tf_op jit(solution)/shard_map/ppermute | solution.py:415
  11.7 7.9 %copy-start = (bf16[128,1536]{1,0:T(8,128)(2,1)S(1)}, bf16[128,1536]{1,0:T(8,128)(2,1)}, u32[]{:S(2)}) copy-start(bf16[128,1536]{1,0:T(8,128)(2,1)} %refs_4_.1) | copy-start | bytes 1179652
  11.7 7.9 %copy-start.1 = (bf16[128,1536]{1,0:T(8,128)(2,1)S(1)}, bf16[128,1536]{1,0:T(8,128)(2,1)}, u32[]{:S(2)}) copy-start(bf16[128,1536]{1,0:T(8,128)(2,1)} %refs_5_.1) | copy-start | bytes 1179652
  11.7 7.9 %copy-start.2 = (bf16[128,1536]{1,0:T(8,128)(2,1)S(1)}, bf16[128,1536]{1,0:T(8,128)(2,1)}, u32[]{:S(2)}) copy-start(bf16[128,1536]{1,0:T(8,128)(2,1)} %refs_6_.1) | copy-start | bytes 1179652
  11.7 7.9 %copy-start.3 = (f32[128,12]{0,1:T(8,128)S(1)}, f32[128,12]{0,1:T(8,128)}, u32[]{:S(2)}) copy-start(f32[128,12]{0,1:T(8,128)} %param.21) | copy-start | bytes 18436
  11.7 19.5 %all-to-all-start = ((bf16[8,16,3456]{2,1,0:T(8,128)(2,1)}), bf16[8,16,3456]{2,1,0:T(8,128)(2,1)S(1)}, u32[]{:S(2)}, u32[]{:S(2)}) async-start(bf16[8,16,3456]{2,1,0:T(8,128)(2,1)} %get-tuple-element.50), calls=%async_computation | async-start | bytes 1769472 | tf_op jit(solution)/shard_map/all_to_all | solution.py:448
  18.5 1.1 %copy-start.4 = (s32[32]{0:T(128)S(1)}, s32[32]{0:T(128)}, u32[]{:S(2)}) copy-start(s32[32]{0:T(128)} %order_ref.3) | copy-start | bytes 388
  18.5 6.0 %collective-permute-start.2 = (bf16[512,128]{1,0:T(8,128)(2,1)S(1)}, bf16[512,128]{1,0:T(8,128)(2,1)S(1)}, u32[]{:S(2)}, u32[]{:S(2)}) collective-permute-start(bf16[512,128]{1,0:T(8,128)(2,1)S(1)} %constant_dynamic-update-slice_fusion.refs_0_), channel_id=1, source_target_pairs={{0,8},{8,0},{16,24},{24,16},{32,40},{40,32},{48,56},{56,48},{64,72... | collective-permute-start | bytes 393224 | tf_op jit(solution)/shard_map/ppermute | solution.py:409
  18.6 5.9 %collective-permute-start.4 = (bf16[512,128]{1,0:T(8,128)(2,1)S(1)}, bf16[512,128]{1,0:T(8,128)(2,1)S(1)}, u32[]{:S(2)}, u32[]{:S(2)}) collective-permute-start(bf16[512,128]{1,0:T(8,128)(2,1)S(1)} %collective-permute-done.3.refs_1_), channel_id=1, source_target_pairs={{0,8},{8,0},{16,24},{24,16},{32,40},{40,32},{48,56},{56,48},{64,72... | collective-permute-start | bytes 393224 | tf_op jit(solution)/shard_map/ppermute | solution.py:409
  19.1 5.4 %collective-permute-start.6 = (bf16[512,128]{1,0:T(8,128)(2,1)S(1)}, bf16[512,128]{1,0:T(8,128)(2,1)S(1)}, u32[]{:S(2)}, u32[]{:S(2)}) collective-permute-start(bf16[512,128]{1,0:T(8,128)(2,1)S(1)} %collective-permute-done.5.refs_2_.refs_0_), channel_id=1, source_target_pairs={{0,8},{8,0},{16,24},{24,16},{32,40},{40,32},{48,56},{56,48},{64,72... | collective-permute-start | bytes 393224 | tf_op jit(solution)/shard_map/ppermute | solution.py:409
  19.2 5.3 %collective-permute-start.8 = (bf16[512,128]{1,0:T(8,128)(2,1)S(1)}, bf16[512,128]{1,0:T(8,128)(2,1)S(1)}, u32[]{:S(2)}, u32[]{:S(2)}) collective-permute-start(bf16[512,128]{1,0:T(8,128)(2,1)S(1)} %collective-permute-done.7.refs_3_.refs_1_), channel_id=1, source_target_pairs={{0,8},{8,0},{16,24},{24,16},{32,40},{40,32},{48,56},{56,48},{64,72... | collective-permute-start | bytes 393224 | tf_op jit(solution)/shard_map/ppermute | solution.py:409
  29.3 7.8 %collective-permute-start.10 = (bf16[4,256,256]{2,1,0:T(8,128)(2,1)S(1)}, bf16[4,256,256]{2,1,0:T(8,128)(2,1)S(1)}, u32[]{:S(2)}, u32[]{:S(2)}) collective-permute-start(bf16[4,256,256]{2,1,0:T(8,128)(2,1)S(1)} %get-tuple-element.58), channel_id=1, source_target_pairs={{0,8},{8,0},{16,24},{24,16},{32,40},{40,32},{48,56},{56,48},{64,72... | collective-permute-start | bytes 1572872 | tf_op jit(solution)/shard_map/ppermute | solution.py:409
  35.3 2.0 %collective-permute-start.9 = (bf16[4,256,256]{2,1,0:T(8,128)(2,1)S(1)}, bf16[4,256,256]{2,1,0:T(8,128)(2,1)S(1)}, u32[]{:S(2)}, u32[]{:S(2)}) collective-permute-start(bf16[4,256,256]{2,1,0:T(8,128)(2,1)S(1)} %get-tuple-element.57), channel_id=1, source_target_pairs={{0,8},{8,0},{16,24},{24,16},{32,40},{40,32},{48,56},{56,48},{64,72... | collective-permute-start | bytes 1572872 | tf_op jit(solution)/shard_map/ppermute | solution.py:409
  35.4 1.9 %copy-start.6 = (f32[4,128,256]{2,1,0:T(8,128)S(1)}, f32[4,128,256]{2,1,0:T(8,128)}, u32[]{:S(2)}) copy-start(f32[4,128,256]{2,1,0:T(8,128)} %get-tuple-element.59.refs_4_) | copy-start | bytes 1572868
  37.3 2.9 %copy-start.5 = (f32[4,128,256]{2,1,0:T(8,128)S(1)}, f32[4,128,256]{2,1,0:T(8,128)}, u32[]{:S(2)}) copy-start(f32[4,128,256]{2,1,0:T(8,128)} %get-tuple-element.63.doc_ref) | copy-start | bytes 1572868
  39.3 8.6 %collective-permute-start.11 = (bf16[4,128,256]{2,1,0:T(8,128)(2,1)S(1)}, bf16[4,128,256]{2,1,0:T(8,128)(2,1)S(1)}, u32[]{:S(2)}, u32[]{:S(2)}) collective-permute-start(bf16[4,128,256]{2,1,0:T(8,128)(2,1)S(1)} %get-tuple-element.66), channel_id=1, source_target_pairs={{0,16},{8,24},{16,0},{24,8},{32,48},{40,56},{48,32},{56,40},{64,80... | collective-permute-start | bytes 786440 | tf_op jit(solution)/shard_map/ppermute | solution.py:412
  42.2 16.4 %all-to-all-start.1 = ((bf16[8,16,1792]{2,1,0:T(8,128)(2,1)}), bf16[8,16,1792]{2,1,0:T(8,128)(2,1)S(1)}, u32[]{:S(2)}, u32[]{:S(2)}) async-start(bf16[8,16,1792]{2,1,0:T(8,128)(2,1)} %get-tuple-element.64), calls=%async_computation.1 | async-start | bytes 917504 | tf_op jit(solution)/shard_map/all_to_all | solution.py:498
  48.0 6.2 %collective-permute-start.12 = (bf16[128,256]{1,0:T(8,128)(2,1)S(1)}, bf16[128,256]{1,0:T(8,128)(2,1)S(1)}, u32[]{:S(2)}, u32[]{:S(2)}) collective-permute-start(bf16[128,256]{1,0:T(8,128)(2,1)S(1)} %get-tuple-element.68), channel_id=1, source_target_pairs={{0,32},{8,40},{16,48},{24,56},{32,64},{40,72},{48,80},{56,88},{64,... | collective-permute-start | bytes 196616 | tf_op jit(solution)/shard_map/ppermute | solution.py:415
  50.3 5.8 %collective-permute-start.13 = (bf16[128,256]{1,0:T(8,128)(2,1)S(1)}, bf16[128,256]{1,0:T(8,128)(2,1)S(1)}, u32[]{:S(2)}, u32[]{:S(2)}) collective-permute-start(bf16[128,256]{1,0:T(8,128)(2,1)S(1)} %get-tuple-element.69), channel_id=1, source_target_pairs={{0,64},{8,72},{16,80},{24,88},{32,96},{40,104},{48,112},{56,120},{... | collective-permute-start | bytes 196616 | tf_op jit(solution)/shard_map/ppermute | solution.py:415
  51.8 4.3 %collective-permute-start.14 = (bf16[128,256]{1,0:T(8,128)(2,1)S(1)}, bf16[128,256]{1,0:T(8,128)(2,1)S(1)}, u32[]{:S(2)}, u32[]{:S(2)}) collective-permute-start(bf16[128,256]{1,0:T(8,128)(2,1)S(1)} %get-tuple-element.70), channel_id=1, source_target_pairs={{0,96},{8,104},{16,112},{24,120},{32,0},{40,8},{48,16},{56,24},{64... | collective-permute-start | bytes 196616 | tf_op jit(solution)/shard_map/ppermute | solution.py:415

commit v7 on v6

--- a/solution.py
+++ b/solution.py
@@ -237,8 +237,8 @@
         for side, grad in enumerate((dk, dv)):
             cut = slice(side * D, (side + 1) * D)
             if core == 0:
-                own_ref[depth, :, cut] = grad[:D]
-                near_ref[depth, :, cut] = grad[D:]
+                own_ref[depth, :, cut] = grad[:D].astype(BF)
+                near_ref[depth, :, cut] = grad[D:].astype(BF)
             else:
                 far_ref[depth, :, cut] = grad.astype(BF)
         if len(blocks) == 2:
@@ -298,7 +298,7 @@
     send_ref, dq_ref = refs[5:]
 
     def store(n, cut, grad):
-        send_ref[n, :, cut] = (grad + doc_ref[n, :, cut] + core_ref[n, D:, cut].astype(F32) + core_doc_ref[n, D:, cut].astype(F32)).astype(BF)
+        send_ref[n, :, cut] = (grad + doc_ref[n, :, cut].astype(F32) + core_ref[n, D:, cut].astype(F32) + core_doc_ref[n, D:, cut].astype(F32)).astype(BF)
 
     dq_ref[...] = column(1, qs_ref, dos_ref, lse_ref[...], delta_ref[...], kv_refs, dq_in[...], store)
 
@@ -342,7 +342,7 @@
     send(wide, 2 * D)
 
     def other(n, cut):
-        return doc_ref[n, :, cut] + core_ref[n, :D, cut].astype(F32) + core_doc_ref[n, :D, cut].astype(F32)
+        return doc_ref[n, :, cut].astype(F32) + core_ref[n, :D, cut].astype(F32) + core_doc_ref[n, :D, cut].astype(F32)
 
     def store(n, cut, grad):
         out_ref[n + 2, :, cut] = grad + other(n + 2, cut)
@@ -449,6 +449,7 @@
 
     quarter = ((depth, rows, 2 * D), F32)
     double = ((depth, 2 * rows, 2 * D), BF)
+    single = ((depth, rows, 2 * D), BF)
     row_state = [((stacked, D), BF), ((stacked, D), BF), ((1, stacked), F32), ((1, stacked), F32)]
     query_sum = ((D, stacked), F32)
     flat = ((rows, wide), BF)
@@ -456,7 +457,7 @@
     *doc_state, dq, near_doc, own_doc = call(
         6,
         functools.partial(doc_kernel, 0, heads, ctx_size),
-        row_state + [query_sum, quarter, quarter],
+        row_state + [query_sum, single, single],
         1,
         block_order, *mine, document_query_matrix, document_output, document_outgrad, document_excess.T,
     )
@@ -464,7 +465,7 @@
     far_doc, doc_turned, near_doc, own_doc = pl.pallas_call(
         functools.partial(doc_kernel, 1, heads, ctx_size),
         out_shape=tuple(jax.ShapeDtypeStruct(*out) for out in (double, turned))
-        + tuple(pltpu.HBM(*out) for out in (quarter, quarter)),
+        + tuple(pltpu.HBM(*out) for out in (single, single)),
         in_specs=[smem()] + [vmem()] * 11,
         out_specs=(vmem(), vmem(), hbm(), hbm()),
         scratch_shapes=[pltpu.SemaphoreType.DMA((2,))],

time: 59.9 us -> 60.8 us (1.015)
  waiting for transfers between devices: 6.95 us -> 8.47 us
    all_to_all x1, waiting for transfers between devices: 2.47 us -> 3.32 us  [local(): back = lax.all_to_all(back, 'head', 0, 0, tiled=True)]
  transfers between devices with their start and end apart: 17 -> 17, of which waited for: 5 -> 8; matrix products, arithmetic and copies ran while one was open for 0% -> 0% of each run, Pallas kernels for 35% -> 34%
where the time goes in v7:
time: 60.8 us; the launch traced here: 60.5 us
  starting transfers between devices  27.6 us (45%)
  Pallas kernels  23.6 us (39%)
  waiting for transfers between devices  8.47 us (14%)
  between operations  0.81 us (1%)
    pallas_call x7, Pallas kernels, call(): pl.pallas_call(body, out_shape=tuple((jax.ShapeDtypeStruct(s, t) for s, t...  14.3 us
    ppermute x6, starting transfers between devices, along_z(): lax.ppermute(x, 'ctx', [(i, (i + 4 * d) % ctx_size) for i in range(ctx_si...  10.4 us
    all_to_all x1, starting transfers between devices, local(): lax.all_to_all(payload, 'head', 0, 0, tiled=True).reshape(groups * each, -1)  6.8 us
    all_to_all x1, starting transfers between devices, local(): back = lax.all_to_all(back, 'head', 0, 0, tiled=True)  5.67 us
    pallas_call x1, Pallas kernels, local(): pl.pallas_call(functools.partial(doc_kernel, 1, heads, ctx_size), out_sha...  4.61 us
    all_to_all x1, waiting for transfers between devices, local(): back = lax.all_to_all(back, 'head', 0, 0, tiled=True)  3.32 us
    ppermute x3, starting transfers between devices, other_chip(): return lax.ppermute(x, 'ctx', [(i, i ^ 2) for i in range(ctx_size)])  2.98 us
    pallas_call x1, Pallas kernels, local(): pl.pallas_call(functools.partial(pack_kernel, heads, groups, total_doc),...  2.71 us
  transfers between devices with their start and end apart: 17, of which 8 were waited for; matrix products, arithmetic and copies ran while one was open for 0% of the time, Pallas kernels for 34%

profile of v7, /device:TPU:0, one launch (start us, length us, event | category | flops | bytes accessed | tf_op | source)
XLA Modules:
  0.0 60.5 jit_solution(800741729070142250)
XLA Ops:
  0.6 1.7 %collective-permute-start = (bf16[128,128]{1,0:T(8,128)(2,1)}, bf16[128,128]{1,0:T(8,128)(2,1)S(1)}, u32[]{:S(2)}, u32[]{:S(2)}) collective-permute-start(bf16[128,128]{1,0:T(8,128)(2,1)} %dk_ref.1), channel_id=1, source_target_pairs={{0,16},{8,24},{16,0},{24,8},{32,48},{40,56},{48,32},{56,40},{64,80... | collective-permute-start | bytes 98312 | tf_op jit(solution)/shard_map/ppermute | solution.py:412
  2.7 2.7 %shard_map.181 = (bf16[8,16,3456]{2,1,0:T(8,128)(2,1)}, bf16[512,128]{1,0:T(8,128)(2,1)S(1)}) custom-call(s32[1,2]{1,0:T(1,128)} %len_hbm.1, bf16[16,12288]{1,0:T(8,128)(2,1)} %do_ref.1, bf16[16,12288]{1,0:T(8,128)(2,1)} %o_ref.1, bf16[16,12288]{1,0:T(8,128)(2,1)} %q_ref.1, bf16[16,1024]{1,0:T(8,128)(2,1)} %k_ref.1, bf16[16,1024]{1,0:T(8,128)(2,1)} %v_ref.1, ...), custom_call_target="tpu_custom_call" | custom-call | flops 5500000256 | tf_op jit(solution)/shard_map/pallas_call | solution.py:421
  5.5 0.9 %collective-permute-done.1 = bf16[128,128]{1,0:T(8,128)(2,1)S(1)} collective-permute-done((bf16[128,128]{1,0:T(8,128)(2,1)}, bf16[128,128]{1,0:T(8,128)(2,1)S(1)}, u32[]{:S(2)}, u32[]{:S(2)}) %collective-permute-start.1) | collective-permute-done | bytes 32800 | tf_op jit(solution)/shard_map/ppermute | solution.py:412
  6.4 1.9 %collective-permute-start.7 = (bf16[512,128]{1,0:T(8,128)(2,1)S(1)}, bf16[512,128]{1,0:T(8,128)(2,1)S(1)}, u32[]{:S(2)}, u32[]{:S(2)}) collective-permute-start(bf16[512,128]{1,0:T(8,128)(2,1)S(1)} %constant_dynamic-update-slice_fusion.refs_0_), channel_id=1, source_target_pairs={{0,32},{8,40},{16,48},{24,56},{32,64},{40,72},{48,80},{56,88},{64,... | collective-permute-start | bytes 393224 | tf_op jit(solution)/shard_map/ppermute | solution.py:415
  8.3 3.6 %collective-permute-start.5 = (bf16[512,128]{1,0:T(8,128)(2,1)S(1)}, bf16[512,128]{1,0:T(8,128)(2,1)S(1)}, u32[]{:S(2)}, u32[]{:S(2)}) collective-permute-start(bf16[512,128]{1,0:T(8,128)(2,1)S(1)} %constant_dynamic-update-slice_fusion.refs_0_), channel_id=1, source_target_pairs={{0,64},{8,72},{16,80},{24,88},{32,96},{40,104},{48,112},{56,120},{... | collective-permute-start | bytes 393224 | tf_op jit(solution)/shard_map/ppermute | solution.py:415
  11.9 1.0 %collective-permute-start.3 = (bf16[512,128]{1,0:T(8,128)(2,1)S(1)}, bf16[512,128]{1,0:T(8,128)(2,1)S(1)}, u32[]{:S(2)}, u32[]{:S(2)}) collective-permute-start(bf16[512,128]{1,0:T(8,128)(2,1)S(1)} %constant_dynamic-update-slice_fusion.refs_0_), channel_id=1, source_target_pairs={{0,96},{8,104},{16,112},{24,120},{32,0},{40,8},{48,16},{56,24},{64... | collective-permute-start | bytes 393224 | tf_op jit(solution)/shard_map/ppermute | solution.py:415
  12.9 6.8 %all-to-all-start = ((bf16[8,16,3456]{2,1,0:T(8,128)(2,1)}), bf16[8,16,3456]{2,1,0:T(8,128)(2,1)S(1)}, u32[]{:S(2)}, u32[]{:S(2)}) async-start(bf16[8,16,3456]{2,1,0:T(8,128)(2,1)} %get-tuple-element.50), calls=%async_computation | async-start | bytes 1769472 | tf_op jit(solution)/shard_map/all_to_all | solution.py:448
  20.9 4.8 %shard_map.182 = (bf16[1536,128]{1,0:T(8,128)(2,1)S(1)}, bf16[1536,128]{1,0:T(8,128)(2,1)S(1)}, f32[1,1536]{1,0:T(1,128)S(1)}, f32[1,1536]{1,0:T(1,128)S(1)}, f3...) custom-call(s32[32]{0:T(128)S(1)} %copy-done.4, ...), custom_call_target="tpu_custom_call" | custom-call | flops 6600000000 | tf_op jit(solution)/shard_map/pallas_call | solution.py:49
  25.7 4.6 %shard_map.183 = (bf16[4,256,256]{2,1,0:T(8,128)(2,1)S(1)}, bf16[128,1536]{1,0:T(8,128)(2,1)S(1)}, bf16[4,128,256]{2,1,0:T(8,128)(2,1)}, bf16[4,128,256]{2,1,0:T(8,128)(2,1)}) custom-call(s32[32]{0:T(128)S(1)} %copy-done.4, bf16[512,128]{1,0:T(8,128)(2,1)S(1)} %collective-permute-done.2.refs_0_, bf16[512,128]{1,0:T(8,128)(2,1)S(1)} %collective-permute-done.4.refs_1_, ...), custom_call_target="tpu_custom_call" | custom-call | flops 6600000000 | tf_op jit(solution)/shard_map/pallas_call | solution.py:465
  30.9 1.5 %all-to-all-done = bf16[8,16,3456]{2,1,0:T(8,128)(2,1)S(1)} async-done(((bf16[8,16,3456]{2,1,0:T(8,128)(2,1)}), bf16[8,16,3456]{2,1,0:T(8,128)(2,1)S(1)}, u32[]{:S(2)}, u32[]{:S(2)}) %all-to-all-start) | async-done | bytes 884768 | tf_op jit(solution)/shard_map/all_to_all | solution.py:448
  32.5 4.0 %shard_map.185 = (bf16[4,256,256]{2,1,0:T(8,128)(2,1)S(1)}, f32[128,1536]{1,0:T(8,128)S(1)}, bf16[1536,128]{1,0:T(8,128)(2,1)S(1)}, bf16[1536,128]{1,0:T(8,128)(...) custom-call(bf16[128,3456]{1,0:T(8,128)(2,1)S(1)} %bitcast.2, ...), custom_call_target="tpu_custom_call" | custom-call | flops 5280000000 | tf_op jit(solution)/shard_map/pallas_call | solution.py:49
  36.6 1.7 %shard_map.186 = (f32[2,128,256]{2,1,0:T(8,128)S(1)}, bf16[128,256]{1,0:T(8,128)(2,1)S(1)}, f32[128,1536]{1,0:T(8,128)S(1)}) custom-call(bf16[1536,128]{1,0:T(8,128)(2,1)S(1)} %get-tuple-element.51.qs_ref, bf16[1536,128]{1,0:T(8,128)(2,1)S(1)} %get-tuple-element.52.dos_ref, f32[1,1536]{1,0:T(1,128)S(1)} %get-tuple-element.53.lse_ref, ...), custom_call_target="tpu_custom_call" | custom-call | flops 2200000000 | tf_op jit(solution)/shard_map/pallas_call | solution.py:49
  38.5 2.1 %shard_map.187 = (bf16[4,128,256]{2,1,0:T(8,128)(2,1)S(1)}, f32[128,1536]{1,0:T(8,128)S(1)}) custom-call(bf16[1536,128]{1,0:T(8,128)(2,1)S(1)} %get-tuple-element.51.qs_ref, bf16[1536,128]{1,0:T(8,128)(2,1)S(1)} %get-tuple-element.52.dos_ref, f32[1,1536]{1,0:T(1,128)S(1)} %get-tuple-element.53.lse_ref, f32[1,1536]{1,0:T(1,128)S(1)} %get-tuple-element.54.delta_ref, ...), custom_call_target="tpu_custom_call" | custom-call | flops 2420000000 | tf_op jit(solution)/shard_map/pallas_call | solution.py:49
  40.6 0.9 %collective-permute-start.11 = (bf16[4,128,256]{2,1,0:T(8,128)(2,1)S(1)}, bf16[4,128,256]{2,1,0:T(8,128)(2,1)S(1)}, u32[]{:S(2)}, u32[]{:S(2)}) collective-permute-start(bf16[4,128,256]{2,1,0:T(8,128)(2,1)S(1)} %get-tuple-element.66), channel_id=1, source_target_pairs={{0,16},{8,24},{16,0},{24,8},{32,48},{40,56},{48,32},{56,40},{64,80... | collective-permute-start | bytes 786440 | tf_op jit(solution)/shard_map/ppermute | solution.py:412
  41.5 1.9 %shard_map.188 = (f32[4,128,256]{2,1,0:T(8,128)S(1)}, bf16[8,16,1792]{2,1,0:T(8,128)(2,1)}) custom-call(bf16[1536,128]{1,0:T(8,128)(2,1)S(1)} %get-tuple-element.51.qs_ref, bf16[1536,128]{1,0:T(8,128)(2,1)S(1)} %get-tuple-element.52.dos_ref, f32[1,1536]{1,0:T(1,128)S(1)} %get-tuple-element.53.lse_ref, f32[1,1536]{1,0:T(1,128)S(1)} %get-tuple-element.54.delta_ref, ...), custom_call_target="tpu_custom_call" | custom-call | flops 2200000000 | tf_op jit(solution)/shard_map/pallas_call | solution.py:490
  43.4 5.7 %all-to-all-start.1 = ((bf16[8,16,1792]{2,1,0:T(8,128)(2,1)}), bf16[8,16,1792]{2,1,0:T(8,128)(2,1)S(1)}, u32[]{:S(2)}, u32[]{:S(2)}) async-start(bf16[8,16,1792]{2,1,0:T(8,128)(2,1)} %get-tuple-element.64), calls=%async_computation.1 | async-start | bytes 917504 | tf_op jit(solution)/shard_map/all_to_all | solution.py:499
  49.2 1.1 %collective-permute-start.12 = (bf16[128,256]{1,0:T(8,128)(2,1)S(1)}, bf16[128,256]{1,0:T(8,128)(2,1)S(1)}, u32[]{:S(2)}, u32[]{:S(2)}) collective-permute-start(bf16[128,256]{1,0:T(8,128)(2,1)S(1)} %get-tuple-element.68), channel_id=1, source_target_pairs={{0,32},{8,40},{16,48},{24,56},{32,64},{40,72},{48,80},{56,88},{64,... | collective-permute-start | bytes 196616 | tf_op jit(solution)/shard_map/ppermute | solution.py:415
  50.3 0.7 %collective-permute-start.13 = (bf16[128,256]{1,0:T(8,128)(2,1)S(1)}, bf16[128,256]{1,0:T(8,128)(2,1)S(1)}, u32[]{:S(2)}, u32[]{:S(2)}) collective-permute-start(bf16[128,256]{1,0:T(8,128)(2,1)S(1)} %get-tuple-element.69), channel_id=1, source_target_pairs={{0,64},{8,72},{16,80},{24,88},{32,96},{40,104},{48,112},{56,120},{... | collective-permute-start | bytes 196616 | tf_op jit(solution)/shard_map/ppermute | solution.py:415
  51.0 2.0 %collective-permute-start.14 = (bf16[128,256]{1,0:T(8,128)(2,1)S(1)}, bf16[128,256]{1,0:T(8,128)(2,1)S(1)}, u32[]{:S(2)}, u32[]{:S(2)}) collective-permute-start(bf16[128,256]{1,0:T(8,128)(2,1)S(1)} %get-tuple-element.70), channel_id=1, source_target_pairs={{0,96},{8,104},{16,112},{24,120},{32,0},{40,8},{48,16},{56,24},{64... | collective-permute-start | bytes 196616 | tf_op jit(solution)/shard_map/ppermute | solution.py:415
  53.1 0.9 %shard_map.184 = bf16[128,1536]{1,0:T(8,128)(2,1)} custom-call(bf16[128,1536]{1,0:T(8,128)(2,1)S(1)} %get-tuple-element.49.turned_ref), custom_call_target="tpu_custom_call" | custom-call | flops 2200000000 | tf_op jit(solution)/shard_map/pallas_call | solution.py:49
  54.0 1.1 %collective-permute-done.12.refs_0_ = bf16[128,256]{1,0:T(8,128)(2,1)S(1)} collective-permute-done((bf16[128,256]{1,0:T(8,128)(2,1)S(1)}, bf16[128,256]{1,0:T(8,128)(2,1)S(1)}, u32[]{:S(2)}, u32[]{:S(2)}) %collective-permute-start.12) | collective-permute-done | bytes 65568 | tf_op jit(solution)/shard_map/ppermute | solution.py:415
  55.1 1.0 %collective-permute-done.13.refs_1_ = bf16[128,256]{1,0:T(8,128)(2,1)S(1)} collective-permute-done((bf16[128,256]{1,0:T(8,128)(2,1)S(1)}, bf16[128,256]{1,0:T(8,128)(2,1)S(1)}, u32[]{:S(2)}, u32[]{:S(2)}) %collective-permute-start.13) | collective-permute-done | bytes 65568 | tf_op jit(solution)/shard_map/ppermute | solution.py:415
  56.3 3.3 %all-to-all-done.1.back_ref = bf16[8,16,1792]{2,1,0:T(8,128)(2,1)S(1)} async-done(((bf16[8,16,1792]{2,1,0:T(8,128)(2,1)}), bf16[8,16,1792]{2,1,0:T(8,128)(2,1)S(1)}, u32[]{:S(2)}, u32[]{:S(2)}) %all-to-all-start.1) | async-done | bytes 458784 | tf_op jit(solution)/shard_map/all_to_all | solution.py:499
  59.7 0.8 %shard_map.190 = (bf16[16,12288]{1,0:T(8,128)(2,1)}, bf16[16,1024]{1,0:T(8,128)(2,1)}, bf16[16,1024]{1,0:T(8,128)(2,1)}, bf16[128,128]{1,0:T(8,128)(2,1)}, bf16[128,128]{1,0:T(8,128)(2,1)}) custom-call(bf16[8,16,1792]{2,1,0:T(8,128)(2,1)S(1)} %all-to-all-done.1.back_ref, f32[128,256]{1,0:T(8,128)S(1)} %get-tuple-element.67.keep_ref, ...), custom_call_target="tpu_custom_call" | custom-call | flops 880000000 | tf_op jit(solution)/shard_map/pallas_call | solution.py:49
  (36 shorter events, 2.9 us)
Async XLA Ops:
  0.6 4.8 %collective-permute-start = (bf16[128,128]{1,0:T(8,128)(2,1)}, bf16[128,128]{1,0:T(8,128)(2,1)S(1)}, u32[]{:S(2)}, u32[]{:S(2)}) collective-permute-start(bf16[128,128]{1,0:T(8,128)(2,1)} %dk_ref.1), channel_id=1, source_target_pairs={{0,16},{8,24},{16,0},{24,8},{32,48},{40,56},{48,32},{56,40},{64,80... | collective-permute-start | bytes 98312 | tf_op jit(solution)/shard_map/ppermute | solution.py:412
  2.3 4.1 %collective-permute-start.1 = (bf16[128,128]{1,0:T(8,128)(2,1)}, bf16[128,128]{1,0:T(8,128)(2,1)S(1)}, u32[]{:S(2)}, u32[]{:S(2)}) collective-permute-start(bf16[128,128]{1,0:T(8,128)(2,1)} %dv_ref.1), channel_id=1, source_target_pairs={{0,16},{8,24},{16,0},{24,8},{32,48},{40,56},{48,32},{56,40},{64,80... | collective-permute-start | bytes 98312 | tf_op jit(solution)/shard_map/ppermute | solution.py:412
  6.4 13.4 %collective-permute-start.7 = (bf16[512,128]{1,0:T(8,128)(2,1)S(1)}, bf16[512,128]{1,0:T(8,128)(2,1)S(1)}, u32[]{:S(2)}, u32[]{:S(2)}) collective-permute-start(bf16[512,128]{1,0:T(8,128)(2,1)S(1)} %constant_dynamic-update-slice_fusion.refs_0_), channel_id=1, source_target_pairs={{0,32},{8,40},{16,48},{24,56},{32,64},{40,72},{48,80},{56,88},{64,... | collective-permute-start | bytes 393224 | tf_op jit(solution)/shard_map/ppermute | solution.py:415
  8.3 12.0 %collective-permute-start.5 = (bf16[512,128]{1,0:T(8,128)(2,1)S(1)}, bf16[512,128]{1,0:T(8,128)(2,1)S(1)}, u32[]{:S(2)}, u32[]{:S(2)}) collective-permute-start(bf16[512,128]{1,0:T(8,128)(2,1)S(1)} %constant_dynamic-update-slice_fusion.refs_0_), channel_id=1, source_target_pairs={{0,64},{8,72},{16,80},{24,88},{32,96},{40,104},{48,112},{56,120},{... | collective-permute-start | bytes 393224 | tf_op jit(solution)/shard_map/ppermute | solution.py:415
  11.9 8.5 %collective-permute-start.3 = (bf16[512,128]{1,0:T(8,128)(2,1)S(1)}, bf16[512,128]{1,0:T(8,128)(2,1)S(1)}, u32[]{:S(2)}, u32[]{:S(2)}) collective-permute-start(bf16[512,128]{1,0:T(8,128)(2,1)S(1)} %constant_dynamic-update-slice_fusion.refs_0_), channel_id=1, source_target_pairs={{0,96},{8,104},{16,112},{24,120},{32,0},{40,8},{48,16},{56,24},{64... | collective-permute-start | bytes 393224 | tf_op jit(solution)/shard_map/ppermute | solution.py:415
  12.9 7.9 %copy-start = (bf16[128,1536]{1,0:T(8,128)(2,1)S(1)}, bf16[128,1536]{1,0:T(8,128)(2,1)}, u32[]{:S(2)}) copy-start(bf16[128,1536]{1,0:T(8,128)(2,1)} %refs_4_.1) | copy-start | bytes 1179652
  12.9 7.9 %copy-start.1 = (bf16[128,1536]{1,0:T(8,128)(2,1)S(1)}, bf16[128,1536]{1,0:T(8,128)(2,1)}, u32[]{:S(2)}) copy-start(bf16[128,1536]{1,0:T(8,128)(2,1)} %refs_5_.1) | copy-start | bytes 1179652
  12.9 7.9 %copy-start.2 = (bf16[128,1536]{1,0:T(8,128)(2,1)S(1)}, bf16[128,1536]{1,0:T(8,128)(2,1)}, u32[]{:S(2)}) copy-start(bf16[128,1536]{1,0:T(8,128)(2,1)} %refs_6_.1) | copy-start | bytes 1179652
  12.9 7.9 %copy-start.3 = (f32[128,12]{0,1:T(8,128)S(1)}, f32[128,12]{0,1:T(8,128)}, u32[]{:S(2)}) copy-start(f32[128,12]{0,1:T(8,128)} %param.21) | copy-start | bytes 18436
  12.9 19.5 %all-to-all-start = ((bf16[8,16,3456]{2,1,0:T(8,128)(2,1)}), bf16[8,16,3456]{2,1,0:T(8,128)(2,1)S(1)}, u32[]{:S(2)}, u32[]{:S(2)}) async-start(bf16[8,16,3456]{2,1,0:T(8,128)(2,1)} %get-tuple-element.50), calls=%async_computation | async-start | bytes 1769472 | tf_op jit(solution)/shard_map/all_to_all | solution.py:448
  19.7 1.1 %copy-start.4 = (s32[32]{0:T(128)S(1)}, s32[32]{0:T(128)}, u32[]{:S(2)}) copy-start(s32[32]{0:T(128)} %order_ref.3) | copy-start | bytes 388
  19.8 6.0 %collective-permute-start.2 = (bf16[512,128]{1,0:T(8,128)(2,1)S(1)}, bf16[512,128]{1,0:T(8,128)(2,1)S(1)}, u32[]{:S(2)}, u32[]{:S(2)}) collective-permute-start(bf16[512,128]{1,0:T(8,128)(2,1)S(1)} %constant_dynamic-update-slice_fusion.refs_0_), channel_id=1, source_target_pairs={{0,8},{8,0},{16,24},{24,16},{32,40},{40,32},{48,56},{56,48},{64,72... | collective-permute-start | bytes 393224 | tf_op jit(solution)/shard_map/ppermute | solution.py:409
  19.9 5.9 %collective-permute-start.8 = (bf16[512,128]{1,0:T(8,128)(2,1)S(1)}, bf16[512,128]{1,0:T(8,128)(2,1)S(1)}, u32[]{:S(2)}, u32[]{:S(2)}) collective-permute-start(bf16[512,128]{1,0:T(8,128)(2,1)S(1)} %collective-permute-done.7.refs_3_.refs_1_), channel_id=1, source_target_pairs={{0,8},{8,0},{16,24},{24,16},{32,40},{40,32},{48,56},{56,48},{64,72... | collective-permute-start | bytes 393224 | tf_op jit(solution)/shard_map/ppermute | solution.py:409
  20.4 5.4 %collective-permute-start.6 = (bf16[512,128]{1,0:T(8,128)(2,1)S(1)}, bf16[512,128]{1,0:T(8,128)(2,1)S(1)}, u32[]{:S(2)}, u32[]{:S(2)}) collective-permute-start(bf16[512,128]{1,0:T(8,128)(2,1)S(1)} %collective-permute-done.5.refs_2_.refs_0_), channel_id=1, source_target_pairs={{0,8},{8,0},{16,24},{24,16},{32,40},{40,32},{48,56},{56,48},{64,72... | collective-permute-start | bytes 393224 | tf_op jit(solution)/shard_map/ppermute | solution.py:409
  20.5 5.3 %collective-permute-start.4 = (bf16[512,128]{1,0:T(8,128)(2,1)S(1)}, bf16[512,128]{1,0:T(8,128)(2,1)S(1)}, u32[]{:S(2)}, u32[]{:S(2)}) collective-permute-start(bf16[512,128]{1,0:T(8,128)(2,1)S(1)} %collective-permute-done.3.refs_1_), channel_id=1, source_target_pairs={{0,8},{8,0},{16,24},{24,16},{32,40},{40,32},{48,56},{56,48},{64,72... | collective-permute-start | bytes 393224 | tf_op jit(solution)/shard_map/ppermute | solution.py:409
  30.4 7.9 %collective-permute-start.10 = (bf16[4,256,256]{2,1,0:T(8,128)(2,1)S(1)}, bf16[4,256,256]{2,1,0:T(8,128)(2,1)S(1)}, u32[]{:S(2)}, u32[]{:S(2)}) collective-permute-start(bf16[4,256,256]{2,1,0:T(8,128)(2,1)S(1)} %get-tuple-element.58), channel_id=1, source_target_pairs={{0,8},{8,0},{16,24},{24,16},{32,40},{40,32},{48,56},{56,48},{64,72... | collective-permute-start | bytes 1572872 | tf_op jit(solution)/shard_map/ppermute | solution.py:409
  36.5 2.0 %collective-permute-start.9 = (bf16[4,256,256]{2,1,0:T(8,128)(2,1)S(1)}, bf16[4,256,256]{2,1,0:T(8,128)(2,1)S(1)}, u32[]{:S(2)}, u32[]{:S(2)}) collective-permute-start(bf16[4,256,256]{2,1,0:T(8,128)(2,1)S(1)} %get-tuple-element.57), channel_id=1, source_target_pairs={{0,8},{8,0},{16,24},{24,16},{32,40},{40,32},{48,56},{56,48},{64,72... | collective-permute-start | bytes 1572872 | tf_op jit(solution)/shard_map/ppermute | solution.py:409
  36.6 1.9 %copy-start.6 = (bf16[4,128,256]{2,1,0:T(8,128)(2,1)S(1)}, bf16[4,128,256]{2,1,0:T(8,128)(2,1)}, u32[]{:S(2)}) copy-start(bf16[4,128,256]{2,1,0:T(8,128)(2,1)} %get-tuple-element.59.refs_4_) | copy-start | bytes 786436
  38.5 2.9 %copy-start.5 = (bf16[4,128,256]{2,1,0:T(8,128)(2,1)S(1)}, bf16[4,128,256]{2,1,0:T(8,128)(2,1)}, u32[]{:S(2)}) copy-start(bf16[4,128,256]{2,1,0:T(8,128)(2,1)} %get-tuple-element.63.doc_ref) | copy-start | bytes 786436
  40.6 8.6 %collective-permute-start.11 = (bf16[4,128,256]{2,1,0:T(8,128)(2,1)S(1)}, bf16[4,128,256]{2,1,0:T(8,128)(2,1)S(1)}, u32[]{:S(2)}, u32[]{:S(2)}) collective-permute-start(bf16[4,128,256]{2,1,0:T(8,128)(2,1)S(1)} %get-tuple-element.66), channel_id=1, source_target_pairs={{0,16},{8,24},{16,0},{24,8},{32,48},{40,56},{48,32},{56,40},{64,80... | collective-permute-start | bytes 786440 | tf_op jit(solution)/shard_map/ppermute | solution.py:412
  43.4 16.3 %all-to-all-start.1 = ((bf16[8,16,1792]{2,1,0:T(8,128)(2,1)}), bf16[8,16,1792]{2,1,0:T(8,128)(2,1)S(1)}, u32[]{:S(2)}, u32[]{:S(2)}) async-start(bf16[8,16,1792]{2,1,0:T(8,128)(2,1)} %get-tuple-element.64), calls=%async_computation.1 | async-start | bytes 917504 | tf_op jit(solution)/shard_map/all_to_all | solution.py:499
  49.2 5.9 %collective-permute-start.12 = (bf16[128,256]{1,0:T(8,128)(2,1)S(1)}, bf16[128,256]{1,0:T(8,128)(2,1)S(1)}, u32[]{:S(2)}, u32[]{:S(2)}) collective-permute-start(bf16[128,256]{1,0:T(8,128)(2,1)S(1)} %get-tuple-element.68), channel_id=1, source_target_pairs={{0,32},{8,40},{16,48},{24,56},{32,64},{40,72},{48,80},{56,88},{64,... | collective-permute-start | bytes 196616 | tf_op jit(solution)/shard_map/ppermute | solution.py:415
  50.3 5.8 %collective-permute-start.13 = (bf16[128,256]{1,0:T(8,128)(2,1)S(1)}, bf16[128,256]{1,0:T(8,128)(2,1)S(1)}, u32[]{:S(2)}, u32[]{:S(2)}) collective-permute-start(bf16[128,256]{1,0:T(8,128)(2,1)S(1)} %get-tuple-element.69), channel_id=1, source_target_pairs={{0,64},{8,72},{16,80},{24,88},{32,96},{40,104},{48,112},{56,120},{... | collective-permute-start | bytes 196616 | tf_op jit(solution)/shard_map/ppermute | solution.py:415
  51.0 5.3 %collective-permute-start.14 = (bf16[128,256]{1,0:T(8,128)(2,1)S(1)}, bf16[128,256]{1,0:T(8,128)(2,1)S(1)}, u32[]{:S(2)}, u32[]{:S(2)}) collective-permute-start(bf16[128,256]{1,0:T(8,128)(2,1)S(1)} %get-tuple-element.70), channel_id=1, source_target_pairs={{0,96},{8,104},{16,112},{24,120},{32,0},{40,8},{48,16},{56,24},{64... | collective-permute-start | bytes 196616 | tf_op jit(solution)/shard_map/ppermute | solution.py:415
